TPU v7x, 32 devices: a whole 2x2x4 slice. The times are simulated.
32 devices in a mesh: parts: 2 (over y), expert: 8 (over z, x), tensor: 2 (over core).
Axes of the slice: x: 2, y: 2, z: 4, core: 2. Of those that a mesh axis runs over, the one named last changes fastest.
Arguments:
- latent_rows: bfloat16 [4096, 1024], P(('parts', 'expert', 'tensor')), parts along dimension 0, may hold values from -6 to 6
- expert_ids: int32 [4096, 4], P(('parts', 'expert', 'tensor')), parts along dimension 0, may hold values from 0 to 7, all different within a row; in each aligned block of 128 rows (0 to 127, 128 to 255, ...) at most 96 rows name the same one
- route_weights: float32 [4096, 4], P(('parts', 'expert', 'tensor')), parts along dimension 0, may hold values from 0.05 to 0.6
- up_weight: bfloat16 [8, 1024, 2048], P('expert', None, 'tensor'), may hold values from -0.1875 to 0.1875
- down_weight: bfloat16 [8, 2048, 1024], P('expert', 'tensor'), may hold values from -0.125 to 0.125
Outputs:
- combined: bfloat16 [4096, 1024], P(('parts', 'expert', 'tensor')), parts along dimension 0
There are 2 independent parts, one for each index of `parts`. A program takes and returns all parts, laid end to end along the dimension named above; an argument that names none is the same for every part. Nothing has to cross between parts.
Inputs may be any that keep to these rules, and one draw needn't show every extreme that they name: `expert_ids`: in each aligned block of 128 rows no expert is named more than 96 times, a bound that some block reaches; the ids of a row differ.
All inputs are finite; a program needn't handle non-finite values.
Results may differ from a plain program's by a relative error of at most 0.0065.
Values may be sent and summed in bfloat16 or wider, within the bound.
No kernel may reach another device: no remote copies, remote signals or barrier semaphores. Data moves between devices by JAX's collectives and lax.ppermute only.
A program may use at most 64 MiB of HBM per device.

v0:
```python
import jax
import jax.numpy as jnp
from jax import lax
from jax.sharding import PartitionSpec as P


def body(latent_rows, expert_ids, route_weights, up_weight, down_weight):
    rows_dev = latent_rows.shape[0]
    width = latent_rows.shape[1]
    choose = expert_ids.shape[1]
    groups = lax.axis_size("expert")
    capacity = 3 * choose * rows_dev // (2 * groups)
    flat_ids = expert_ids.reshape(-1)
    onehot = (flat_ids[:, None] == jnp.arange(groups, dtype=jnp.int32)[None, :]).astype(jnp.int32)
    ranks = jnp.cumsum(onehot, axis=0) - onehot
    slots = jnp.sum(ranks * onehot, axis=1)
    target = flat_ids * capacity + slots
    repeated = jnp.repeat(latent_rows, choose, axis=0)
    outgoing = jnp.zeros((groups * capacity, width), jnp.bfloat16).at[target].set(repeated)
    outgoing = outgoing.reshape(groups, capacity, width)
    arrived = lax.all_to_all(outgoing, "expert", split_axis=0, concat_axis=0, tiled=True)
    arrived_rows = arrived.reshape(-1, width)
    both_rows = lax.all_gather(arrived_rows, "tensor", axis=0, tiled=True)
    pre = jnp.dot(both_rows, up_weight[0], preferred_element_type=jnp.float32)
    hidden = (jnp.maximum(pre, 0.0) ** 2).astype(jnp.bfloat16)
    partial_out = jnp.dot(hidden, down_weight[0], preferred_element_type=jnp.float32)
    summed = lax.psum_scatter(
        partial_out.astype(jnp.bfloat16), "tensor", scatter_dimension=0, tiled=True
    )
    returned = lax.all_to_all(
        summed.reshape(groups, capacity, width), "expert", split_axis=0, concat_axis=0, tiled=True
    )
    returned_rows = returned.reshape(-1, width)
    picked = returned_rows[target].astype(jnp.float32)
    weighted = picked * route_weights.reshape(-1)[:, None]
    combined = jnp.sum(weighted.reshape(rows_dev, choose, width), axis=1)
    return combined.astype(jnp.bfloat16)


def solution(mesh):
    return jax.shard_map(
        body,
        mesh=mesh,
        in_specs=(
            P(("parts", "expert", "tensor"), None),
            P(("parts", "expert", "tensor"), None),
            P(("parts", "expert", "tensor"), None),
            P("expert", None, "tensor"),
            P("expert", "tensor", None),
        ),
        out_specs=P(("parts", "expert", "tensor"), None),
        check_vma=False,
    )
```

profile of v0, /device:TPU:0, one launch (start us, length us, event | category | flops | bytes accessed | tf_op | source)
XLA Modules:
  0.0 155.0 jit_solution(8445129067661504165)
XLA Ops:
  6.5 0.0 copy-start
  6.5 0.0 all-gather.2.cloned.1.call-start
  6.5 0.9 copy.8
  7.5 0.1 eq.29
  7.6 0.1 eq.25
  7.7 0.7 broadcast_multiply_fusion
  8.4 1.1 reduce-window.6
  9.5 0.2 slice_reduce_fusion
  9.8 0.1 copy.7
  9.9 0.1 mul.30
  10.0 1.3 broadcast_in_dim.10
  11.3 1.1 reshape.90
  12.4 0.1 fusion.7
  12.5 4.5 %scatter_custom_fusion = bf16[768,1024]{1,0:T(8,128)(2,1)} fusion(s32[512]{0:T(512)S(1)} %bitcast.26, bf16[512,1024]{1,0:T(8,128)(2,1)} %reshape.90, bf16[]{:T(256)} %constant.5.clone.1), kind=kCustom, calls=%fused_computation.7 | custom fusion | bytes 1573376 | tf_op jit(solution)/shard_map/scatter | solution.py:19
  17.0 44.4 %all_to_all.10 = bf16[8,96,1024]{2,1,0:T(8,128)(2,1)} all-to-all(bf16[8,96,1024]{2,1,0:T(8,128)(2,1)} %bitcast.24), channel_id=1, replica_groups=mesh['parts'=2,'expert'=8,'tensor'=2] {'expert'}, dimensions={0} | all-to-all | bytes 3145728 | tf_op jit(solution)/shard_map/all_to_all | solution.py:21
  61.3 0.0 all-gather.2.cloned.1.call-update
  61.4 0.0 reduce-scatter.2.cloned.1.call-start
  61.4 11.3 %all-gather.2.cloned.1.call-done = bf16[1536,1024]{1,0:T(8,128)(2,1)} async-done(((bf16[768,1024]{1,0:T(8,128)(2,1)}), bf16[1536,1024]{1,0:T(8,128)(2,1)}) %all-gather.2.cloned.1.call-update) | async-done | bytes 3145744 | tf_op jit(solution)/shard_map/all_gather | solution.py:23
  72.7 0.0 copy-done
  72.7 10.1 %convolution_convert_fusion = bf16[1536,1024]{1,0:T(8,128)(2,1)} fusion(bf16[1,1024,1024]{2,1,0:T(8,128)(2,1)S(1)} %copy-done, bf16[1536,1024]{1,0:T(8,128)(2,1)} %all-gather.2.cloned.1.call-done, bf16[1,1024,1024]{2,1,0:T(8,128)(2,1)} %param.8), kind=kOutput, calls=%fused_computation.3 | convolution fusion | flops 6448742400 | bytes 10485760 | tf_op jit(solution)/shard_map/dot_general | solution.py:26
  82.8 0.0 reduce-scatter.2.cloned.1.call-update
  82.8 0.0 copy-start.1
  82.8 12.2 %reduce-scatter.2.cloned.1.call-done = bf16[768,1024]{1,0:T(8,128)(2,1)} async-done(((bf16[1536,1024]{1,0:T(8,128)(2,1)}), bf16[768,1024]{1,0:T(8,128)(2,1)}) %reduce-scatter.2.cloned.1.call-update) | async-done | bytes 1572880 | tf_op jit(solution)/shard_map/reduce_scatter | solution.py:27
  95.0 5.7 %all-to-all-start.1 = ((bf16[8,96,1024]{2,1,0:T(8,128)(2,1)}), bf16[8,96,1024]{2,1,0:T(8,128)(2,1)}, u32[]{:S(2)}, u32[]{:S(2)}) async-start(bf16[8,96,1024]{2,1,0:T(8,128)(2,1)} %bitcast.25), calls=%async_computation.2 | async-start | bytes 3145728 | tf_op jit(solution)/shard_map/all_to_all | solution.py:30
  100.8 0.0 copy-done.1
  100.8 0.1 copy.10
  100.9 37.5 %all-to-all-done.1 = bf16[8,96,1024]{2,1,0:T(8,128)(2,1)} async-done(((bf16[8,96,1024]{2,1,0:T(8,128)(2,1)}), bf16[8,96,1024]{2,1,0:T(8,128)(2,1)}, u32[]{:S(2)}, u32[]{:S(2)}) %all-to-all-start.1) | async-done | bytes 1572896 | tf_op jit(solution)/shard_map/all_to_all | solution.py:30
  138.4 4.3 %gather_fusion = bf16[512,1024]{1,0:T(8,128)(2,1)S(1)} fusion(bf16[768,1024]{1,0:T(8,128)(2,1)} %bitcast.9, s32[1024]{0:T(1024)S(1)} %pad_clamp_fusion), kind=kCustom, calls=%fused_computation | custom fusion | bytes 2099200 | tf_op jit(solution)/shard_map/gather | solution.py:34
  142.7 1.7 %reshape.77 = f32[128,4,1024]{2,1,0:T(4,128)} reshape(bf16[512,1024]{1,0:T(8,128)(2,1)S(1)} %gather_fusion) | data formatting | bytes 3145728 | tf_op jit(solution)/shard_map/convert_element_type | solution.py:34
  144.4 3.7 %multiply_reduce_fusion = bf16[128,1024]{1,0:T(8,128)(2,1)} fusion(f32[128,4,1024]{2,1,0:T(4,128)} %reshape.77, f32[128,4]{1,0:T(8,128)S(1)} %copy.10), kind=kLoop, calls=%fused_computation.6 | loop fusion | flops 917504 | bytes 2361344 | tf_op jit(solution)/shard_map/reduce_sum | solution.py:36
  (5 shorter events, 0.1 us)
Async XLA Ops:
  6.5 66.2 %copy-start = (bf16[1,1024,1024]{2,1,0:T(8,128)(2,1)S(1)}, bf16[1,1024,1024]{2,1,0:T(8,128)(2,1)}, u32[]{:S(2)}) copy-start(bf16[1,1024,1024]{2,1,0:T(8,128)(2,1)} %param.9) | copy-start | bytes 6291460
  6.5 66.1 %all-gather.2.cloned.1.call-start = ((), (), s32[]{:S(2)}) async-start(), calls=%async_computation.3 | async-start | bytes 4718592 | tf_op jit(solution)/shard_map/all_gather | solution.py:23
  61.4 33.7 %reduce-scatter.2.cloned.1.call-start = ((), (), s32[]{:S(2)}) async-start(), calls=%async_computation.4 | async-start | bytes 4718592 | tf_op jit(solution)/shard_map/reduce_scatter | solution.py:27
  82.8 18.0 %copy-start.1 = (f32[128,4]{0,1:T(4,128)S(1)}, f32[128,4]{0,1:T(4,128)}, u32[]{:S(2)}) copy-start(f32[128,4]{0,1:T(4,128)} %param.7) | copy-start | bytes 6148
  95.0 43.3 %all-to-all-start.1 = ((bf16[8,96,1024]{2,1,0:T(8,128)(2,1)}), bf16[8,96,1024]{2,1,0:T(8,128)(2,1)}, u32[]{:S(2)}, u32[]{:S(2)}) async-start(bf16[8,96,1024]{2,1,0:T(8,128)(2,1)} %bitcast.25), calls=%async_computation.2 | async-start | bytes 3145728 | tf_op jit(solution)/shard_map/all_to_all | solution.py:30
Sparse Core Ops, SparseCore 0:
  61.5 11.1 all-gather.1
  82.9 12.0 reduce-scatter.1
where the time goes:
time: 155 us
  waiting for transfers between devices  61 us (39%)
  blocking collectives  44.4 us (29%)
  local copies, waits for them, and re-layouts  14.7 us (9%)
  between operations  13.4 us (9%)
  matrix products  10.1 us (7%)
  starting transfers between devices  5.79 us (4%)
  other arithmetic  5.66 us (4%)
    all_to_all x1, blocking collectives, body(): lax.all_to_all(outgoing, 'expert', split_axis=0, concat_axis=0, tiled=True)  44.4 us
    all_to_all x1, waiting for transfers between devices, body(): lax.all_to_all(summed.reshape(groups, capacity, width), 'expert', split_a...  37.5 us
    reduce_scatter x1, waiting for transfers between devices, body(): lax.psum_scatter(partial_out.astype(jnp.bfloat16), 'tensor', scatter_dime...  12.2 us
    all_gather x1, waiting for transfers between devices, body(): both_rows = lax.all_gather(arrived_rows, 'tensor', axis=0, tiled=True)  11.3 us
    dot_general x1, matrix products, body(): jnp.dot(hidden, down_weight[0], preferred_element_type=jnp.float32)  10.1 us
    all_to_all x1, starting transfers between devices, body(): lax.all_to_all(summed.reshape(groups, capacity, width), 'expert', split_a...  5.74 us
    scatter x1, local copies, waits for them, and re-layouts, body(): jnp.zeros((groups * capacity, width), jnp.bfloat16).at[target].set(repeated)  4.51 us
    gather x1, local copies, waits for them, and re-layouts, body(): picked = returned_rows[target].astype(jnp.float32)  4.34 us
  transfers between devices with their start and end apart: 3, of which 3 were waited for; matrix products, arithmetic and copies ran while one was open for 0% of the time, Pallas kernels for 0%

commit v1 on v0

--- a/solution.py
+++ b/solution.py
@@ -4,7 +4,7 @@
 from jax.sharding import PartitionSpec as P
 
 
-def body(latent_rows, expert_ids, route_weights, up_weight, down_weight):
+def exchange_body(latent_rows, expert_ids, route_weights, up_weight, down_weight):
     rows_dev = latent_rows.shape[0]
     width = latent_rows.shape[1]
     choose = expert_ids.shape[1]
@@ -37,6 +37,62 @@
     return combined.astype(jnp.bfloat16)
 
 
+def across(value, step):
+    size = lax.axis_size("expert")
+    return lax.ppermute(value, "expert", [(i, i ^ step) for i in range(size)])
+
+
+def other_core(value):
+    return lax.ppermute(value, "tensor", [(0, 1), (1, 0)])
+
+
+def gather_body(latent_rows, expert_ids, route_weights, up_weight, down_weight):
+    groups = lax.axis_size("expert")
+    me = lax.axis_index("expert")
+    core = lax.axis_index("tensor")
+    f32 = jnp.float32
+    chosen = expert_ids[None, :, :] == jnp.arange(groups, dtype=jnp.int32)[:, None, None]
+    table = jnp.sum(jnp.where(chosen, route_weights[None], 0.0), axis=2)
+    tables = lax.all_gather(table, ("expert", "tensor"), axis=0, tiled=False)
+    mine = lax.dynamic_index_in_dim(tables, me, axis=1, keepdims=False)
+    near = [latent_rows] + [across(latent_rows, 2 * k) for k in range(1, groups // 2)]
+    far = [across(rows, 1) for rows in near]
+
+    def weights_of(step, swap):
+        place = (me ^ step) * 2 + (core ^ swap)
+        return lax.dynamic_index_in_dim(mine, place, axis=0, keepdims=False)
+
+    def core_sum(rows, step):
+        both = jnp.concatenate([rows, other_core(rows)], axis=0)
+        weight = jnp.concatenate([weights_of(step, 0), weights_of(step, 1)])
+        pre = jnp.dot(both, up_weight[0], preferred_element_type=f32)
+        hidden = jnp.square(jnp.maximum(pre, 0.0)).astype(jnp.bfloat16)
+        out = jnp.dot(hidden, down_weight[0], preferred_element_type=f32)
+        out = (out * weight[:, None]).astype(jnp.bfloat16)
+        n = rows.shape[0]
+        return out[:n].astype(f32), other_core(out[n:]).astype(f32)
+
+    total = None
+    for k in [*range(1, groups // 2), 0]:
+        a, b = core_sum(far[k], 2 * k + 1)
+        over = across((a + b).astype(jnp.bfloat16), 1).astype(f32)
+        a, b = core_sum(near[k], 2 * k)
+        part = a + b + over
+        if k:
+            part = across(part.astype(jnp.bfloat16), 2 * k).astype(f32)
+        total = part if total is None else total + part
+    return total.astype(jnp.bfloat16)
+
+
+def body(latent_rows, expert_ids, route_weights, up_weight, down_weight):
+    groups = lax.axis_size("expert")
+    rows_dev, choose = expert_ids.shape
+    capacity = 3 * choose * rows_dev // (2 * groups)
+    dense = rows_dev <= 2 * capacity and groups & (groups - 1) == 0
+    form = gather_body if dense else exchange_body
+    return form(latent_rows, expert_ids, route_weights, up_weight, down_weight)
+
+
 def solution(mesh):
     return jax.shard_map(
         body,

time: 155 us -> 121 us (0.78)
  the two profiles are of different devices: /device:TPU:0 before, /device:TPU:16 now
where the time goes in v1:
time: 121 us
  blocking collectives  29.3 us (24%)
  waiting for transfers between devices  28.8 us (24%)
  matrix products  27.3 us (23%)
  starting transfers between devices  20.2 us (17%)
  local copies, waits for them, and re-layouts  8.51 us (7%)
  other arithmetic  6.24 us (5%)
    all_gather x1, blocking collectives, gather_body(): tables = lax.all_gather(table, ('expert', 'tensor'), axis=0, tiled=False)  29.3 us
    ppermute x14, waiting for transfers between devices, across(): return lax.ppermute(value, 'expert', [(i, i ^ step) for i in range(size)])  28.8 us
    dot_general x8, matrix products, core_sum(): out = jnp.dot(hidden, down_weight[0], preferred_element_type=f32)  27.3 us
    ppermute x14, starting transfers between devices, across(): return lax.ppermute(value, 'expert', [(i, i ^ step) for i in range(size)])  16.6 us
    slice x8, local copies, waits for them, and re-layouts, core_sum(): return (out[:n].astype(f32), other_core(out[n:]).astype(f32))  8.45 us
    ppermute x16, starting transfers between devices, other_core(): return lax.ppermute(value, 'tensor', [(0, 1), (1, 0)])  3.57 us
  transfers between devices with their start and end apart: 30, of which 7 were waited for; matrix products, arithmetic and copies ran while one was open for 34% of the time, Pallas kernels for 0%

profile of v1, /device:TPU:16, one launch (start us, length us, event | category | flops | bytes accessed | tf_op | source)
XLA Modules:
  0.0 120.7 jit_solution(14873908258747924078)
XLA Ops:
  0.0 1.9 %collective-permute-start = (bf16[128,1024]{1,0:T(8,128)(2,1)}, bf16[128,1024]{1,0:T(8,128)(2,1)}, u32[]{:S(2)}, u32[]{:S(2)}) collective-permute-start(bf16[128,1024]{1,0:T(8,128)(2,1)} %param.5), channel_id=1, source_target_pairs={{0,4},{2,6},{4,0},{6,2},{8,12},{10,14},{12,8},{14,10},{1,5},{3,7},... | collective-permute-start | bytes 786440 | tf_op jit(solution)/shard_map/ppermute | solution.py:42
  1.9 1.6 %collective-permute-start.16 = (bf16[128,1024]{1,0:T(8,128)(2,1)}, bf16[128,1024]{1,0:T(8,128)(2,1)}, u32[]{:S(2)}, u32[]{:S(2)}) collective-permute-start(bf16[128,1024]{1,0:T(8,128)(2,1)} %param.5), channel_id=1, source_target_pairs={{0,12},{2,14},{4,8},{6,10},{8,4},{10,6},{12,0},{14,2},{1,13},{3,15... | collective-permute-start | bytes 786440 | tf_op jit(solution)/shard_map/ppermute | solution.py:42
  3.5 1.5 %collective-permute-start.26 = (bf16[128,1024]{1,0:T(8,128)(2,1)}, bf16[128,1024]{1,0:T(8,128)(2,1)}, u32[]{:S(2)}, u32[]{:S(2)}) collective-permute-start(bf16[128,1024]{1,0:T(8,128)(2,1)} %param.5), channel_id=1, source_target_pairs={{0,2},{2,0},{4,6},{6,4},{8,10},{10,8},{12,14},{14,12},{1,3},{3,1},... | collective-permute-start | bytes 786440 | tf_op jit(solution)/shard_map/ppermute | solution.py:42
  5.0 0.7 select_reduce_fusion
  5.7 29.3 %all-gather = f32[128,128]{1,0:T(8,128)S(1)} all-gather(f32[8,128]{1,0:T(8,128)S(1)} %select_reduce_fusion), channel_id=2, replica_groups=mesh['parts'=2,'expert'=8,'tensor'=2] {'expert','tensor'}, dimensions={0}, use_global_device_ids=true | all-gather | bytes 69632 | tf_op jit(solution)/shard_map/all_gather | solution.py:56
  35.2 0.3 collective-permute-start.9
  35.5 0.0 collective-permute-done.24
  35.5 3.0 %fusion.107 = bf16[256,1024]{1,0:T(8,128)(2,1)S(1)} fusion(bf16[1,1024,1024]{2,1,0:T(8,128)(2,1)S(1)} %copy-done, bf16[1,1024,1024]{2,1,0:T(8,128)(2,1)} %param.8, bf16[128,1024]{1,0:T(8,128)(2,1)S(1)} %collective-permute-done.24, bf16[128,1024]{1,0:T(8,128)(2,1)} %param.5, f32[256]{0:T(256)S(1)} %pad_maximum_fusion.6), kind=kOutput, calls=%fused_computation.57 | convolution fusion | flops 1076101120 | bytes 5243904 | tf_op jit(solution)/shard_map/dot_general | solution.py:70
  38.5 0.7 slice.77
  39.2 0.3 collective-permute-start.25
  39.4 0.0 collective-permute-done
  39.4 2.6 %collective-permute-start.11 = (bf16[128,1024]{1,0:T(8,128)(2,1)}, bf16[128,1024]{1,0:T(8,128)(2,1)}, u32[]{:S(2)}, u32[]{:S(2)}) collective-permute-start(bf16[128,1024]{1,0:T(8,128)(2,1)} %collective-permute-done.8), channel_id=1, source_target_pairs={{0,2},{2,0},{4,6},{6,4},{8,10},{10,8},{12,14},{14,12},{1,3},{3,1},... | collective-permute-start | bytes 786440 | tf_op jit(solution)/shard_map/ppermute | solution.py:42
  42.0 0.1 collective-permute-start.1
  42.1 3.0 %fusion.119 = bf16[256,1024]{1,0:T(8,128)(2,1)S(1)} fusion(bf16[1,1024,1024]{2,1,0:T(8,128)(2,1)S(1)} %copy-done, bf16[1,1024,1024]{2,1,0:T(8,128)(2,1)} %param.8, bf16[128,1024]{1,0:T(8,128)(2,1)} %collective-permute-done.9, bf16[128,1024]{1,0:T(8,128)(2,1)} %collective-permute-done.8, f32[256]{0:T(256)S(1)} %pad_maximum_fusion.2), kind=kOutput, calls=%fused_computation.61 | convolution fusion | flops 1076101120 | bytes 5243904 | tf_op jit(solution)/shard_map/dot_general | solution.py:70
  45.2 0.8 slice.69
  45.9 0.0 collective-permute-done.16
  45.9 0.4 collective-permute-start.3
  46.3 0.0 collective-permute-done.1
  46.3 0.2 collective-permute-start.17
  46.5 3.0 %fusion.125 = bf16[256,1024]{1,0:T(8,128)(2,1)S(1)} fusion(bf16[1,1024,1024]{2,1,0:T(8,128)(2,1)S(1)} %copy-done, bf16[1,1024,1024]{2,1,0:T(8,128)(2,1)} %param.8, bf16[128,1024]{1,0:T(8,128)(2,1)} %collective-permute-done.1, bf16[128,1024]{1,0:T(8,128)(2,1)} %collective-permute-done, f32[256]{0:T(256)S(1)} %pad_maximum_fusion), kind=kOutput, calls=%fused_computation.63 | convolution fusion | flops 1076101120 | bytes 5243904 | tf_op jit(solution)/shard_map/dot_general | solution.py:70
  49.5 0.8 slice.65
  50.3 1.7 %collective-permute-start.19 = (bf16[128,1024]{1,0:T(8,128)(2,1)}, bf16[128,1024]{1,0:T(8,128)(2,1)}, u32[]{:S(2)}, u32[]{:S(2)}) collective-permute-start(bf16[128,1024]{1,0:T(8,128)(2,1)} %collective-permute-done.16), channel_id=1, source_target_pairs={{0,2},{2,0},{4,6},{6,4},{8,10},{10,8},{12,14},{14,12},{1,3},{3,1},... | collective-permute-start | bytes 786440 | tf_op jit(solution)/shard_map/ppermute | solution.py:42
  51.9 0.1 collective-permute-start.27
  52.0 3.8 %fusion.113 = bf16[256,1024]{1,0:T(8,128)(2,1)} fusion(bf16[1,1024,1024]{2,1,0:T(8,128)(2,1)S(1)} %copy-done, bf16[1,1024,1024]{2,1,0:T(8,128)(2,1)} %param.8, bf16[128,1024]{1,0:T(8,128)(2,1)} %collective-permute-done.17, bf16[128,1024]{1,0:T(8,128)(2,1)} %collective-permute-done.16, f32[256]{0:T(256)S(1)} %pad_maximum_fusion.4), kind=kOutput, calls=%fused_computation.59 | convolution fusion | flops 1076101120 | bytes 5243904 | tf_op jit(solution)/shard_map/dot_general | solution.py:70
  55.8 1.7 %slice.73 = bf16[128,1024]{1,0:T(8,128)(2,1)} slice(bf16[256,1024]{1,0:T(8,128)(2,1)} %fusion.113), slice={[128:256], [0:1024]} | slice | bytes 524288 | tf_op jit(solution)/shard_map/slice | solution.py:73
  57.5 0.4 collective-permute-start.10
  58.0 0.1 collective-permute-start.12
  58.0 3.0 %fusion.104 = bf16[256,1024]{1,0:T(8,128)(2,1)S(1)} fusion(bf16[1,1024,1024]{2,1,0:T(8,128)(2,1)S(1)} %copy-done, bf16[1,1024,1024]{2,1,0:T(8,128)(2,1)} %param.8, bf16[128,1024]{1,0:T(8,128)(2,1)} %collective-permute-done.27, bf16[128,1024]{1,0:T(8,128)(2,1)} %collective-permute-done.26, f32[256]{0:T(256)S(1)} %pad_maximum_fusion.7), kind=kOutput, calls=%fused_computation.56 | convolution fusion | flops 1076101120 | bytes 5243904 | tf_op jit(solution)/shard_map/dot_general | solution.py:70
  61.1 0.7 slice.79
  61.8 0.4 collective-permute-start.2
  62.2 0.1 collective-permute-start.4
  62.3 3.8 %fusion.116 = bf16[256,1024]{1,0:T(8,128)(2,1)} fusion(bf16[1,1024,1024]{2,1,0:T(8,128)(2,1)S(1)} %copy-done, bf16[1,1024,1024]{2,1,0:T(8,128)(2,1)} %param.8, bf16[128,1024]{1,0:T(8,128)(2,1)} %collective-permute-done.12, bf16[128,1024]{1,0:T(8,128)(2,1)} %collective-permute-done.11, f32[256]{0:T(256)S(1)} %pad_maximum_fusion.3), kind=kOutput, calls=%fused_computation.60 | convolution fusion | flops 1076101120 | bytes 5243904 | tf_op jit(solution)/shard_map/dot_general | solution.py:70
  66.1 1.7 %slice.71 = bf16[128,1024]{1,0:T(8,128)(2,1)} slice(bf16[256,1024]{1,0:T(8,128)(2,1)} %fusion.116), slice={[128:256], [0:1024]} | slice | bytes 524288 | tf_op jit(solution)/shard_map/slice | solution.py:73
  67.8 0.4 collective-permute-start.28
  68.2 0.1 collective-permute-start.20
  68.3 3.8 %fusion.122 = bf16[256,1024]{1,0:T(8,128)(2,1)} fusion(bf16[1,1024,1024]{2,1,0:T(8,128)(2,1)S(1)} %copy-done, bf16[1,1024,1024]{2,1,0:T(8,128)(2,1)} %param.8, bf16[128,1024]{1,0:T(8,128)(2,1)} %collective-permute-done.4, bf16[128,1024]{1,0:T(8,128)(2,1)} %collective-permute-done.3, f32[256]{0:T(256)S(1)} %pad_maximum_fusion.1), kind=kOutput, calls=%fused_computation.62 | convolution fusion | flops 1076101120 | bytes 5243904 | tf_op jit(solution)/shard_map/dot_general | solution.py:70
  72.2 0.4 collective-permute-start.13
  72.6 3.8 %fusion.110 = bf16[256,1024]{1,0:T(8,128)(2,1)} fusion(bf16[1,1024,1024]{2,1,0:T(8,128)(2,1)S(1)} %copy-done, bf16[1,1024,1024]{2,1,0:T(8,128)(2,1)} %param.8, bf16[128,1024]{1,0:T(8,128)(2,1)} %collective-permute-done.20, bf16[128,1024]{1,0:T(8,128)(2,1)} %collective-permute-done.19, f32[256]{0:T(256)S(1)} %pad_maximum_fusion.5), kind=kOutput, calls=%fused_computation.58 | convolution fusion | flops 1076101120 | bytes 5243904 | tf_op jit(solution)/shard_map/dot_general | solution.py:70
  76.4 1.1 slice.67
  77.5 0.1 collective-permute-start.5
  77.7 1.0 add_convert_fusion.1
  78.7 1.0 slice.75
  79.8 0.5 collective-permute-start.21
  80.3 1.1 add_convert_fusion.5
  81.4 0.4 collective-permute-start.14
  81.8 0.1 add_convert_fusion.7
  81.9 1.7 %collective-permute-start.6 = (bf16[128,1024]{1,0:T(8,128)(2,1)S(1)}, bf16[128,1024]{1,0:T(8,128)(2,1)S(1)}, u32[]{:S(2)}, u32[]{:S(2)}) collective-permute-start(bf16[128,1024]{1,0:T(8,128)(2,1)S(1)} %add_convert_fusion.7), channel_id=1, source_target_pairs={{0,2},{2,0},{4,6},{6,4},{8,10},{10,8},{12,14},{14,12},{1,3},{3,1},... | collective-permute-start | bytes 786440 | tf_op jit(solution)/shard_map/ppermute | solution.py:42
  83.6 0.1 add_convert_fusion.3
  83.7 0.1 collective-permute-start.18
  83.8 6.8 %collective-permute-done.14 = bf16[128,1024]{1,0:T(8,128)(2,1)S(1)} collective-permute-done((bf16[128,1024]{1,0:T(8,128)(2,1)S(1)}, bf16[128,1024]{1,0:T(8,128)(2,1)S(1)}, u32[]{:S(2)}, u32[]{:S(2)}) %collective-permute-start.14) | collective-permute-done | bytes 262176 | tf_op jit(solution)/shard_map/ppermute | solution.py:42
  90.6 0.3 collective-permute-start.22
  91.0 1.1 add_convert_fusion.4
  92.1 1.7 %collective-permute-start.29 = (bf16[128,1024]{1,0:T(8,128)(2,1)S(1)}, bf16[128,1024]{1,0:T(8,128)(2,1)S(1)}, u32[]{:S(2)}, u32[]{:S(2)}) collective-permute-start(bf16[128,1024]{1,0:T(8,128)(2,1)S(1)} %add_convert_fusion.1), channel_id=1, source_target_pairs={{0,2},{2,0},{4,6},{6,4},{8,10},{10,8},{12,14},{14,12},{1,3},{3,1},... | collective-permute-start | bytes 786440 | tf_op jit(solution)/shard_map/ppermute | solution.py:42
  93.8 2.4 %collective-permute-done.6 = bf16[128,1024]{1,0:T(8,128)(2,1)S(1)} collective-permute-done((bf16[128,1024]{1,0:T(8,128)(2,1)S(1)}, bf16[128,1024]{1,0:T(8,128)(2,1)S(1)}, u32[]{:S(2)}, u32[]{:S(2)}) %collective-permute-start.6) | collective-permute-done | bytes 262176 | tf_op jit(solution)/shard_map/ppermute | solution.py:42
  96.2 1.1 add_convert_fusion.6
  97.3 2.1 %collective-permute-start.7 = (bf16[128,1024]{1,0:T(8,128)(2,1)S(1)}, bf16[128,1024]{1,0:T(8,128)(2,1)S(1)}, u32[]{:S(2)}, u32[]{:S(2)}) collective-permute-start(bf16[128,1024]{1,0:T(8,128)(2,1)S(1)} %add_convert_fusion.6), channel_id=1, source_target_pairs={{0,4},{2,6},{4,0},{6,2},{8,12},{10,14},{12,8},{14,10},{1,5},{3,7},... | collective-permute-start | bytes 786440 | tf_op jit(solution)/shard_map/ppermute | solution.py:42
  99.4 2.4 %collective-permute-done.22 = bf16[128,1024]{1,0:T(8,128)(2,1)S(1)} collective-permute-done((bf16[128,1024]{1,0:T(8,128)(2,1)S(1)}, bf16[128,1024]{1,0:T(8,128)(2,1)S(1)}, u32[]{:S(2)}, u32[]{:S(2)}) %collective-permute-start.22) | collective-permute-done | bytes 262176 | tf_op jit(solution)/shard_map/ppermute | solution.py:42
  101.9 0.1 add_convert_fusion.2
  102.0 0.6 collective-permute-start.23
  102.6 4.0 %collective-permute-done.29 = bf16[128,1024]{1,0:T(8,128)(2,1)S(1)} collective-permute-done((bf16[128,1024]{1,0:T(8,128)(2,1)S(1)}, bf16[128,1024]{1,0:T(8,128)(2,1)S(1)}, u32[]{:S(2)}, u32[]{:S(2)}) %collective-permute-start.29) | collective-permute-done | bytes 262176 | tf_op jit(solution)/shard_map/ppermute | solution.py:42
  106.6 3.2 %collective-permute-done.15 = bf16[128,1024]{1,0:T(8,128)(2,1)S(1)} collective-permute-done((bf16[128,1024]{1,0:T(8,128)(2,1)S(1)}, bf16[128,1024]{1,0:T(8,128)(2,1)S(1)}, u32[]{:S(2)}, u32[]{:S(2)}) %collective-permute-start.15) | collective-permute-done | bytes 262176 | tf_op jit(solution)/shard_map/ppermute | solution.py:42
  109.8 1.3 %collective-permute-done.7 = bf16[128,1024]{1,0:T(8,128)(2,1)S(1)} collective-permute-done((bf16[128,1024]{1,0:T(8,128)(2,1)S(1)}, bf16[128,1024]{1,0:T(8,128)(2,1)S(1)}, u32[]{:S(2)}, u32[]{:S(2)}) %collective-permute-start.7) | collective-permute-done | bytes 262176 | tf_op jit(solution)/shard_map/ppermute | solution.py:42
  111.1 8.6 %collective-permute-done.23 = bf16[128,1024]{1,0:T(8,128)(2,1)S(1)} collective-permute-done((bf16[128,1024]{1,0:T(8,128)(2,1)S(1)}, bf16[128,1024]{1,0:T(8,128)(2,1)S(1)}, u32[]{:S(2)}, u32[]{:S(2)}) %collective-permute-start.23) | collective-permute-done | bytes 262176 | tf_op jit(solution)/shard_map/ppermute | solution.py:42
  119.7 1.0 add_convert_fusion
  (49 shorter events, 0.2 us)
Async XLA Ops:
  0.0 35.5 %copy-start = (bf16[1,1024,1024]{2,1,0:T(8,128)(2,1)S(1)}, bf16[1,1024,1024]{2,1,0:T(8,128)(2,1)}, u32[]{:S(2)}) copy-start(bf16[1,1024,1024]{2,1,0:T(8,128)(2,1)} %param.9) | copy-start | bytes 6291460
  0.0 35.2 %collective-permute-start.8 = (bf16[128,1024]{1,0:T(8,128)(2,1)}, bf16[128,1024]{1,0:T(8,128)(2,1)}, u32[]{:S(2)}, u32[]{:S(2)}) collective-permute-start(bf16[128,1024]{1,0:T(8,128)(2,1)} %param.5), channel_id=1, source_target_pairs={{0,8},{2,10},{4,12},{6,14},{8,0},{10,2},{12,4},{14,6},{1,9},{3,11}... | collective-permute-start | bytes 786440 | tf_op jit(solution)/shard_map/ppermute | solution.py:42
  0.0 39.4 %collective-permute-start = (bf16[128,1024]{1,0:T(8,128)(2,1)}, bf16[128,1024]{1,0:T(8,128)(2,1)}, u32[]{:S(2)}, u32[]{:S(2)}) collective-permute-start(bf16[128,1024]{1,0:T(8,128)(2,1)} %param.5), channel_id=1, source_target_pairs={{0,4},{2,6},{4,0},{6,2},{8,12},{10,14},{12,8},{14,10},{1,5},{3,7},... | collective-permute-start | bytes 786440 | tf_op jit(solution)/shard_map/ppermute | solution.py:42
  1.9 44.0 %collective-permute-start.16 = (bf16[128,1024]{1,0:T(8,128)(2,1)}, bf16[128,1024]{1,0:T(8,128)(2,1)}, u32[]{:S(2)}, u32[]{:S(2)}) collective-permute-start(bf16[128,1024]{1,0:T(8,128)(2,1)} %param.5), channel_id=1, source_target_pairs={{0,12},{2,14},{4,8},{6,10},{8,4},{10,6},{12,0},{14,2},{1,13},{3,15... | collective-permute-start | bytes 786440 | tf_op jit(solution)/shard_map/ppermute | solution.py:42
  3.5 46.8 %collective-permute-start.26 = (bf16[128,1024]{1,0:T(8,128)(2,1)}, bf16[128,1024]{1,0:T(8,128)(2,1)}, u32[]{:S(2)}, u32[]{:S(2)}) collective-permute-start(bf16[128,1024]{1,0:T(8,128)(2,1)} %param.5), channel_id=1, source_target_pairs={{0,2},{2,0},{4,6},{6,4},{8,10},{10,8},{12,14},{14,12},{1,3},{3,1},... | collective-permute-start | bytes 786440 | tf_op jit(solution)/shard_map/ppermute | solution.py:42
  5.0 30.5 %collective-permute-start.24 = (bf16[128,1024]{1,0:T(8,128)(2,1)}, bf16[128,1024]{1,0:T(8,128)(2,1)S(1)}, u32[]{:S(2)}, u32[]{:S(2)}) collective-permute-start(bf16[128,1024]{1,0:T(8,128)(2,1)} %param.5), channel_id=1, source_target_pairs={{0,1},{1,0},{2,3},{3,2},{4,5},{5,4},{6,7},{7,6},{8,9},{9,8},{10,11... | collective-permute-start | bytes 786440 | tf_op jit(solution)/shard_map/ppermute | solution.py:46
  35.2 6.9 %collective-permute-start.9 = (bf16[128,1024]{1,0:T(8,128)(2,1)}, bf16[128,1024]{1,0:T(8,128)(2,1)}, u32[]{:S(2)}, u32[]{:S(2)}) collective-permute-start(bf16[128,1024]{1,0:T(8,128)(2,1)} %collective-permute-done.8), channel_id=1, source_target_pairs={{0,1},{1,0},{2,3},{3,2},{4,5},{5,4},{6,7},{7,6},{8,9},{9,8},{10,11... | collective-permute-start | bytes 786440 | tf_op jit(solution)/shard_map/ppermute | solution.py:46
  39.2 63.4 %collective-permute-start.25 = (bf16[128,1024]{1,0:T(8,128)(2,1)}, bf16[128,1024]{1,0:T(8,128)(2,1)S(1)}, u32[]{:S(2)}, u32[]{:S(2)}) collective-permute-start(bf16[128,1024]{1,0:T(8,128)(2,1)} %slice.77), channel_id=1, source_target_pairs={{0,1},{1,0},{2,3},{3,2},{4,5},{5,4},{6,7},{7,6},{8,9},{9,8},{10,11... | collective-permute-start | bytes 786440 | tf_op jit(solution)/shard_map/ppermute | solution.py:46
  39.4 18.1 %collective-permute-start.11 = (bf16[128,1024]{1,0:T(8,128)(2,1)}, bf16[128,1024]{1,0:T(8,128)(2,1)}, u32[]{:S(2)}, u32[]{:S(2)}) collective-permute-start(bf16[128,1024]{1,0:T(8,128)(2,1)} %collective-permute-done.8), channel_id=1, source_target_pairs={{0,2},{2,0},{4,6},{6,4},{8,10},{10,8},{12,14},{14,12},{1,3},{3,1},... | collective-permute-start | bytes 786440 | tf_op jit(solution)/shard_map/ppermute | solution.py:42
  42.0 4.2 %collective-permute-start.1 = (bf16[128,1024]{1,0:T(8,128)(2,1)}, bf16[128,1024]{1,0:T(8,128)(2,1)}, u32[]{:S(2)}, u32[]{:S(2)}) collective-permute-start(bf16[128,1024]{1,0:T(8,128)(2,1)} %collective-permute-done), channel_id=1, source_target_pairs={{0,1},{1,0},{2,3},{3,2},{4,5},{5,4},{6,7},{7,6},{8,9},{9,8},{10,11... | collective-permute-start | bytes 786440 | tf_op jit(solution)/shard_map/ppermute | solution.py:46
  45.1 1.1 copy-start.5
  45.9 15.9 %collective-permute-start.3 = (bf16[128,1024]{1,0:T(8,128)(2,1)}, bf16[128,1024]{1,0:T(8,128)(2,1)}, u32[]{:S(2)}, u32[]{:S(2)}) collective-permute-start(bf16[128,1024]{1,0:T(8,128)(2,1)} %collective-permute-done), channel_id=1, source_target_pairs={{0,2},{2,0},{4,6},{6,4},{8,10},{10,8},{12,14},{14,12},{1,3},{3,1},... | collective-permute-start | bytes 786440 | tf_op jit(solution)/shard_map/ppermute | solution.py:42
  46.3 5.7 %collective-permute-start.17 = (bf16[128,1024]{1,0:T(8,128)(2,1)}, bf16[128,1024]{1,0:T(8,128)(2,1)}, u32[]{:S(2)}, u32[]{:S(2)}) collective-permute-start(bf16[128,1024]{1,0:T(8,128)(2,1)} %collective-permute-done.16), channel_id=1, source_target_pairs={{0,1},{1,0},{2,3},{3,2},{4,5},{5,4},{6,7},{7,6},{8,9},{9,8},{10,11... | collective-permute-start | bytes 786440 | tf_op jit(solution)/shard_map/ppermute | solution.py:46
  49.5 6.3 %copy-start.3 = (bf16[256,1024]{1,0:T(8,128)(2,1)}, bf16[256,1024]{1,0:T(8,128)(2,1)S(1)}, u32[]{:S(2)}) copy-start(bf16[256,1024]{1,0:T(8,128)(2,1)S(1)} %fusion.125) | copy-start | bytes 1572868
  50.3 17.5 %collective-permute-start.19 = (bf16[128,1024]{1,0:T(8,128)(2,1)}, bf16[128,1024]{1,0:T(8,128)(2,1)}, u32[]{:S(2)}, u32[]{:S(2)}) collective-permute-start(bf16[128,1024]{1,0:T(8,128)(2,1)} %collective-permute-done.16), channel_id=1, source_target_pairs={{0,2},{2,0},{4,6},{6,4},{8,10},{10,8},{12,14},{14,12},{1,3},{3,1},... | collective-permute-start | bytes 786440 | tf_op jit(solution)/shard_map/ppermute | solution.py:42
  51.9 6.0 %collective-permute-start.27 = (bf16[128,1024]{1,0:T(8,128)(2,1)}, bf16[128,1024]{1,0:T(8,128)(2,1)}, u32[]{:S(2)}, u32[]{:S(2)}) collective-permute-start(bf16[128,1024]{1,0:T(8,128)(2,1)} %collective-permute-done.26), channel_id=1, source_target_pairs={{0,1},{1,0},{2,3},{3,2},{4,5},{5,4},{6,7},{7,6},{8,9},{9,8},{10,11... | collective-permute-start | bytes 786440 | tf_op jit(solution)/shard_map/ppermute | solution.py:46
  57.5 26.2 %collective-permute-start.10 = (bf16[128,1024]{1,0:T(8,128)(2,1)}, bf16[128,1024]{1,0:T(8,128)(2,1)}, u32[]{:S(2)}, u32[]{:S(2)}) collective-permute-start(bf16[128,1024]{1,0:T(8,128)(2,1)} %slice.69), channel_id=1, source_target_pairs={{0,1},{1,0},{2,3},{3,2},{4,5},{5,4},{6,7},{7,6},{8,9},{9,8},{10,11... | collective-permute-start | bytes 786440 | tf_op jit(solution)/shard_map/ppermute | solution.py:46
  58.0 4.3 %collective-permute-start.12 = (bf16[128,1024]{1,0:T(8,128)(2,1)}, bf16[128,1024]{1,0:T(8,128)(2,1)}, u32[]{:S(2)}, u32[]{:S(2)}) collective-permute-start(bf16[128,1024]{1,0:T(8,128)(2,1)} %collective-permute-done.11), channel_id=1, source_target_pairs={{0,1},{1,0},{2,3},{3,2},{4,5},{5,4},{6,7},{7,6},{8,9},{9,8},{10,11... | collective-permute-start | bytes 786440 | tf_op jit(solution)/shard_map/ppermute | solution.py:46
  61.8 30.3 %collective-permute-start.2 = (bf16[128,1024]{1,0:T(8,128)(2,1)}, bf16[128,1024]{1,0:T(8,128)(2,1)}, u32[]{:S(2)}, u32[]{:S(2)}) collective-permute-start(bf16[128,1024]{1,0:T(8,128)(2,1)} %slice.65), channel_id=1, source_target_pairs={{0,1},{1,0},{2,3},{3,2},{4,5},{5,4},{6,7},{7,6},{8,9},{9,8},{10,11... | collective-permute-start | bytes 786440 | tf_op jit(solution)/shard_map/ppermute | solution.py:46
  62.2 6.0 %collective-permute-start.4 = (bf16[128,1024]{1,0:T(8,128)(2,1)}, bf16[128,1024]{1,0:T(8,128)(2,1)}, u32[]{:S(2)}, u32[]{:S(2)}) collective-permute-start(bf16[128,1024]{1,0:T(8,128)(2,1)} %collective-permute-done.3), channel_id=1, source_target_pairs={{0,1},{1,0},{2,3},{3,2},{4,5},{5,4},{6,7},{7,6},{8,9},{9,8},{10,11... | collective-permute-start | bytes 786440 | tf_op jit(solution)/shard_map/ppermute | solution.py:46
  67.8 9.7 %collective-permute-start.28 = (bf16[128,1024]{1,0:T(8,128)(2,1)}, bf16[128,1024]{1,0:T(8,128)(2,1)}, u32[]{:S(2)}, u32[]{:S(2)}) collective-permute-start(bf16[128,1024]{1,0:T(8,128)(2,1)} %slice.79), channel_id=1, source_target_pairs={{0,1},{1,0},{2,3},{3,2},{4,5},{5,4},{6,7},{7,6},{8,9},{9,8},{10,11... | collective-permute-start | bytes 786440 | tf_op jit(solution)/shard_map/ppermute | solution.py:46
  68.2 3.9 %collective-permute-start.20 = (bf16[128,1024]{1,0:T(8,128)(2,1)}, bf16[128,1024]{1,0:T(8,128)(2,1)}, u32[]{:S(2)}, u32[]{:S(2)}) collective-permute-start(bf16[128,1024]{1,0:T(8,128)(2,1)} %collective-permute-done.19), channel_id=1, source_target_pairs={{0,1},{1,0},{2,3},{3,2},{4,5},{5,4},{6,7},{7,6},{8,9},{9,8},{10,11... | collective-permute-start | bytes 786440 | tf_op jit(solution)/shard_map/ppermute | solution.py:46
  72.2 7.6 %collective-permute-start.13 = (bf16[128,1024]{1,0:T(8,128)(2,1)}, bf16[128,1024]{1,0:T(8,128)(2,1)}, u32[]{:S(2)}, u32[]{:S(2)}) collective-permute-start(bf16[128,1024]{1,0:T(8,128)(2,1)} %slice.71), channel_id=1, source_target_pairs={{0,1},{1,0},{2,3},{3,2},{4,5},{5,4},{6,7},{7,6},{8,9},{9,8},{10,11... | collective-permute-start | bytes 786440 | tf_op jit(solution)/shard_map/ppermute | solution.py:46
  76.4 5.4 %copy-start.1 = (bf16[256,1024]{1,0:T(8,128)(2,1)S(1)}, bf16[256,1024]{1,0:T(8,128)(2,1)}, u32[]{:S(2)}) copy-start(bf16[256,1024]{1,0:T(8,128)(2,1)} %fusion.122) | copy-start | bytes 1572868
  76.4 7.2 %copy-start.2 = (bf16[256,1024]{1,0:T(8,128)(2,1)S(1)}, bf16[256,1024]{1,0:T(8,128)(2,1)}, u32[]{:S(2)}) copy-start(bf16[256,1024]{1,0:T(8,128)(2,1)} %fusion.110) | copy-start | bytes 1572868
  76.4 7.3 %copy-start.8 = (bf16[128,1024]{1,0:T(8,128)(2,1)S(1)}, bf16[128,1024]{1,0:T(8,128)(2,1)}, u32[]{:S(2)}) copy-start(bf16[128,1024]{1,0:T(8,128)(2,1)} %slice.73) | copy-start | bytes 786436
  76.4 14.5 %copy-start.6 = (bf16[256,1024]{1,0:T(8,128)(2,1)S(1)}, bf16[256,1024]{1,0:T(8,128)(2,1)}, u32[]{:S(2)}) copy-start(bf16[256,1024]{1,0:T(8,128)(2,1)} %copy-done.5) | copy-start | bytes 1572868
  77.5 3.8 %collective-permute-start.5 = (bf16[128,1024]{1,0:T(8,128)(2,1)S(1)}, bf16[128,1024]{1,0:T(8,128)(2,1)S(1)}, u32[]{:S(2)}, u32[]{:S(2)}) collective-permute-start(bf16[128,1024]{1,0:T(8,128)(2,1)S(1)} %slice.67), channel_id=1, source_target_pairs={{0,1},{1,0},{2,3},{3,2},{4,5},{5,4},{6,7},{7,6},{8,9},{9,8},{10,11... | collective-permute-start | bytes 786440 | tf_op jit(solution)/shard_map/ppermute | solution.py:46
  78.7 17.5 %copy-start.4 = (bf16[256,1024]{1,0:T(8,128)(2,1)S(1)}, bf16[256,1024]{1,0:T(8,128)(2,1)}, u32[]{:S(2)}) copy-start(bf16[256,1024]{1,0:T(8,128)(2,1)} %copy-done.3) | copy-start | bytes 1572868
  79.7 22.1 %copy-start.7 = (bf16[256,1024]{1,0:T(8,128)(2,1)S(1)}, bf16[256,1024]{1,0:T(8,128)(2,1)}, u32[]{:S(2)}) copy-start(bf16[256,1024]{1,0:T(8,128)(2,1)} %fusion.113) | copy-start | bytes 1572868
  79.8 2.1 %collective-permute-start.21 = (bf16[128,1024]{1,0:T(8,128)(2,1)S(1)}, bf16[128,1024]{1,0:T(8,128)(2,1)S(1)}, u32[]{:S(2)}, u32[]{:S(2)}) collective-permute-start(bf16[128,1024]{1,0:T(8,128)(2,1)S(1)} %slice.75), channel_id=1, source_target_pairs={{0,1},{1,0},{2,3},{3,2},{4,5},{5,4},{6,7},{7,6},{8,9},{9,8},{10,11... | collective-permute-start | bytes 786440 | tf_op jit(solution)/shard_map/ppermute | solution.py:46
  81.4 9.2 %collective-permute-start.14 = (bf16[128,1024]{1,0:T(8,128)(2,1)S(1)}, bf16[128,1024]{1,0:T(8,128)(2,1)S(1)}, u32[]{:S(2)}, u32[]{:S(2)}) collective-permute-start(bf16[128,1024]{1,0:T(8,128)(2,1)S(1)} %add_convert_fusion.5), channel_id=1, source_target_pairs={{0,2},{2,0},{4,6},{6,4},{8,10},{10,8},{12,14},{14,12},{1,3},{3,1},... | collective-permute-start | bytes 786440 | tf_op jit(solution)/shard_map/ppermute | solution.py:42
  81.9 14.3 %collective-permute-start.6 = (bf16[128,1024]{1,0:T(8,128)(2,1)S(1)}, bf16[128,1024]{1,0:T(8,128)(2,1)S(1)}, u32[]{:S(2)}, u32[]{:S(2)}) collective-permute-start(bf16[128,1024]{1,0:T(8,128)(2,1)S(1)} %add_convert_fusion.7), channel_id=1, source_target_pairs={{0,2},{2,0},{4,6},{6,4},{8,10},{10,8},{12,14},{14,12},{1,3},{3,1},... | collective-permute-start | bytes 786440 | tf_op jit(solution)/shard_map/ppermute | solution.py:42
  83.7 13.6 %collective-permute-start.18 = (bf16[128,1024]{1,0:T(8,128)(2,1)S(1)}, bf16[128,1024]{1,0:T(8,128)(2,1)S(1)}, u32[]{:S(2)}, u32[]{:S(2)}) collective-permute-start(bf16[128,1024]{1,0:T(8,128)(2,1)S(1)} %copy-done.8), channel_id=1, source_target_pairs={{0,1},{1,0},{2,3},{3,2},{4,5},{5,4},{6,7},{7,6},{8,9},{9,8},{10,11... | collective-permute-start | bytes 786440 | tf_op jit(solution)/shard_map/ppermute | solution.py:46
  90.6 11.2 %collective-permute-start.22 = (bf16[128,1024]{1,0:T(8,128)(2,1)S(1)}, bf16[128,1024]{1,0:T(8,128)(2,1)S(1)}, u32[]{:S(2)}, u32[]{:S(2)}) collective-permute-start(bf16[128,1024]{1,0:T(8,128)(2,1)S(1)} %add_convert_fusion.3), channel_id=1, source_target_pairs={{0,2},{2,0},{4,6},{6,4},{8,10},{10,8},{12,14},{14,12},{1,3},{3,1},... | collective-permute-start | bytes 786440 | tf_op jit(solution)/shard_map/ppermute | solution.py:42
  92.1 14.5 %collective-permute-start.29 = (bf16[128,1024]{1,0:T(8,128)(2,1)S(1)}, bf16[128,1024]{1,0:T(8,128)(2,1)S(1)}, u32[]{:S(2)}, u32[]{:S(2)}) collective-permute-start(bf16[128,1024]{1,0:T(8,128)(2,1)S(1)} %add_convert_fusion.1), channel_id=1, source_target_pairs={{0,2},{2,0},{4,6},{6,4},{8,10},{10,8},{12,14},{14,12},{1,3},{3,1},... | collective-permute-start | bytes 786440 | tf_op jit(solution)/shard_map/ppermute | solution.py:42
  96.2 13.6 %collective-permute-start.15 = (bf16[128,1024]{1,0:T(8,128)(2,1)S(1)}, bf16[128,1024]{1,0:T(8,128)(2,1)S(1)}, u32[]{:S(2)}, u32[]{:S(2)}) collective-permute-start(bf16[128,1024]{1,0:T(8,128)(2,1)S(1)} %add_convert_fusion.4), channel_id=1, source_target_pairs={{0,8},{2,10},{4,12},{6,14},{8,0},{10,2},{12,4},{14,6},{1,9},{3,11}... | collective-permute-start | bytes 786440 | tf_op jit(solution)/shard_map/ppermute | solution.py:42
  97.3 13.8 %collective-permute-start.7 = (bf16[128,1024]{1,0:T(8,128)(2,1)S(1)}, bf16[128,1024]{1,0:T(8,128)(2,1)S(1)}, u32[]{:S(2)}, u32[]{:S(2)}) collective-permute-start(bf16[128,1024]{1,0:T(8,128)(2,1)S(1)} %add_convert_fusion.6), channel_id=1, source_target_pairs={{0,4},{2,6},{4,0},{6,2},{8,12},{10,14},{12,8},{14,10},{1,5},{3,7},... | collective-permute-start | bytes 786440 | tf_op jit(solution)/shard_map/ppermute | solution.py:42
  102.0 17.7 %collective-permute-start.23 = (bf16[128,1024]{1,0:T(8,128)(2,1)S(1)}, bf16[128,1024]{1,0:T(8,128)(2,1)S(1)}, u32[]{:S(2)}, u32[]{:S(2)}) collective-permute-start(bf16[128,1024]{1,0:T(8,128)(2,1)S(1)} %add_convert_fusion.2), channel_id=1, source_target_pairs={{0,12},{2,14},{4,8},{6,10},{8,4},{10,6},{12,0},{14,2},{1,13},{3,15... | collective-permute-start | bytes 786440 | tf_op jit(solution)/shard_map/ppermute | solution.py:42

commit v2 on v0

--- a/solution.py
+++ b/solution.py
@@ -1,10 +1,12 @@
 import jax
 import jax.numpy as jnp
 from jax import lax
+from jax.experimental import pallas as pl
+from jax.experimental.pallas import tpu as pltpu
 from jax.sharding import PartitionSpec as P
 
 
-def body(latent_rows, expert_ids, route_weights, up_weight, down_weight):
+def exchange_body(latent_rows, expert_ids, route_weights, up_weight, down_weight):
     rows_dev = latent_rows.shape[0]
     width = latent_rows.shape[1]
     choose = expert_ids.shape[1]
@@ -37,6 +39,94 @@
     return combined.astype(jnp.bfloat16)
 
 
+def across(value, step):
+    size = lax.axis_size("expert")
+    return lax.ppermute(value, "expert", [(i, i ^ step) for i in range(size)])
+
+
+def other_core(value):
+    return lax.ppermute(value, "tensor", [(0, 1), (1, 0)])
+
+
+def expert_kernel(near, far, choice, up_a, down_a, up_b, down_b, near_out, far_out):
+    f32 = jnp.float32
+    n = near_out.shape[0]
+    blocks = [near[...], far[...]]
+    rows = jnp.concatenate([b[:n] for b in blocks], axis=0)
+    total = None
+    for up, down in ((up_a, down_a), (up_b, down_b)):
+        pre = jnp.dot(rows, up[...], preferred_element_type=f32)
+        hidden = jnp.square(jnp.maximum(pre, 0.0)).astype(jnp.bfloat16)
+        out = jnp.dot(hidden, down[...], preferred_element_type=f32)
+        total = out if total is None else total + out
+    for i, ref in enumerate((near_out, far_out)):
+        pair = blocks[i][n:, : 2 * n].astype(f32)
+        weight = jnp.sum((pair[:, :n] + pair[:, n:]) * choice[...], axis=0, keepdims=True)
+        column = jnp.broadcast_to(weight, (n, n)).T
+        for c in range(0, ref.shape[1], n):
+            ref[:, c : c + n] = (total[i * n : (i + 1) * n, c : c + n] * column).astype(ref.dtype)
+
+
+def expert(near, far, choice, weights, n):
+    width = near.shape[1]
+    units = weights[0].shape[1]
+    return pl.pallas_call(
+        expert_kernel,
+        out_shape=[
+            jax.ShapeDtypeStruct((n, width), jnp.float32),
+            jax.ShapeDtypeStruct((n, width), jnp.bfloat16),
+        ],
+        in_specs=[pl.BlockSpec(memory_space=pltpu.VMEM)] * 7,
+        out_specs=[pl.BlockSpec(memory_space=pltpu.VMEM)] * 2,
+        compiler_params=pltpu.CompilerParams(vmem_limit_bytes=40 << 20),
+        cost_estimate=pl.CostEstimate(
+            flops=16 * n * width * units, bytes_accessed=8 * width * units, transcendentals=0
+        ),
+    )(near, far, choice, *weights)
+
+
+def gather_body(latent_rows, expert_ids, route_weights, up_weight, down_weight):
+    groups = lax.axis_size("expert")
+    n, width = latent_rows.shape
+    me = lax.axis_index("expert")
+    f32 = jnp.float32
+    names = jnp.arange(groups, dtype=jnp.int32)
+    chosen = expert_ids[None, :, :] == names[:, None, None]
+    table = jnp.sum(jnp.where(chosen, route_weights[None], 0.0), axis=2)
+    high = lax.reduce_precision(table, 8, 7)
+    strip = jnp.concatenate([high, table - high], axis=1).astype(jnp.bfloat16)
+    strip = jnp.pad(strip, ((0, 0), (0, width - 2 * n)))
+    choice = jnp.broadcast_to((names == me).astype(f32)[:, None], (groups, n))
+
+    near = {0: jnp.concatenate([latent_rows, strip], axis=0)}
+    far = {0: across(near[0], 1)}
+    for k in range(1, groups // 2):
+        low = k & -k
+        near[k] = across(near[k ^ low], 2 * low)
+        far[k] = across(near[k], 1)
+    weights = (up_weight[0], down_weight[0], other_core(up_weight[0]), other_core(down_weight[0]))
+
+    own, away = {}, {}
+    for k in range(groups // 2):
+        own[k], away[k] = expert(near[k], far[k], choice, weights, n)
+    sums = {}
+    for k in reversed(range(groups // 2)):
+        sums[k] = own[k] + across(away[k], 1).astype(f32)
+    for k in reversed(range(1, groups // 2)):
+        low = k & -k
+        sums[k ^ low] = sums[k ^ low] + across(sums[k].astype(jnp.bfloat16), 2 * low).astype(f32)
+    return sums[0].astype(jnp.bfloat16)
+
+
+def body(latent_rows, expert_ids, route_weights, up_weight, down_weight):
+    groups = lax.axis_size("expert")
+    rows_dev, choose = expert_ids.shape
+    capacity = 3 * choose * rows_dev // (2 * groups)
+    dense = rows_dev <= 2 * capacity and groups & (groups - 1) == 0
+    form = gather_body if dense else exchange_body
+    return form(latent_rows, expert_ids, route_weights, up_weight, down_weight)
+
+
 def solution(mesh):
     return jax.shard_map(
         body,

time: 155 us -> 85.7 us (0.55)
  blocking collectives: 44.4 us -> 0 us
  waiting for transfers between devices: 61 us -> 40.6 us
  starting transfers between devices: 5.79 us -> 22.8 us
  Pallas kernels: 0 us -> 15.9 us
  between operations: 13.4 us -> 0.09 us
  local copies, waits for them, and re-layouts: 14.7 us -> 3.26 us
  matrix products: 10.1 us -> 0 us
  other arithmetic: 5.66 us -> 2.77 us
    all_to_all x1 -> x0, blocking collectives: 44.4 us -> none  [body(): lax.all_to_all(outgoing, 'expert', split_axis=0, concat_axis=0, tiled=True)]
    ppermute x0 -> x16, waiting for transfers between devices: none -> 40.6 us  [the longest x14 40.6 us: across(): return lax.ppermute(value, 'expert', [(i, i ^ step) for i in range(size)])]
    all_to_all x1 -> x0, waiting for transfers between devices: 37.5 us -> none  [body(): lax.all_to_all(summed.reshape(groups, capacity, width), 'expert', split_a...]
    ppermute x0 -> x16, starting transfers between devices: none -> 22.8 us  [the longest x14 22.3 us: across(): return lax.ppermute(value, 'expert', [(i, i ^ step) for i in range(size)])]
    pallas_call x0 -> x4, Pallas kernels: none -> 15.9 us  [expert(): pl.pallas_call(expert_kernel, out_shape=[jax.ShapeDtypeStruct((n, width),...]
    reduce_scatter x1 -> x0, waiting for transfers between devices: 12.2 us -> none  [body(): lax.psum_scatter(partial_out.astype(jnp.bfloat16), 'tensor', scatter_dime...]
    all_gather x1 -> x0, waiting for transfers between devices: 11.3 us -> none  [body(): both_rows = lax.all_gather(arrived_rows, 'tensor', axis=0, tiled=True)]
    dot_general x1 -> x0, matrix products: 10.1 us -> none  [body(): jnp.dot(hidden, down_weight[0], preferred_element_type=jnp.float32)]
  transfers between devices with their start and end apart: 3 -> 16, of which waited for: 3 -> 8; matrix products, arithmetic and copies ran while one was open for 0% -> 2% of each run, Pallas kernels for 0% -> 19%
where the time goes in v2:
time: 85.7 us; the launch traced here: 85.4 us
  waiting for transfers between devices  40.6 us (47%)
  starting transfers between devices  22.8 us (27%)
  Pallas kernels  15.9 us (19%)
  local copies, waits for them, and re-layouts  3.26 us (4%)
  other arithmetic  2.77 us (3%)
    ppermute x14, waiting for transfers between devices, across(): return lax.ppermute(value, 'expert', [(i, i ^ step) for i in range(size)])  40.6 us
    ppermute x14, starting transfers between devices, across(): return lax.ppermute(value, 'expert', [(i, i ^ step) for i in range(size)])  22.3 us
    pallas_call x4, Pallas kernels, expert(): pl.pallas_call(expert_kernel, out_shape=[jax.ShapeDtypeStruct((n, width),...  15.9 us
    unnamed x6, local copies, waits for them, and re-layouts  3.19 us
  transfers between devices with their start and end apart: 16, of which 8 were waited for; matrix products, arithmetic and copies ran while one was open for 2% of the time, Pallas kernels for 19%

profile of v2, /device:TPU:0, one launch (start us, length us, event | category | flops | bytes accessed | tf_op | source)
XLA Modules:
  0.0 85.4 jit_solution(12224687560586707327)
XLA Ops:
  0.0 0.5 collective-permute-start.1
  0.5 0.1 collective-permute-start.2
  0.5 0.7 select_reduce_fusion
  1.2 1.0 %pad_maximum_fusion.near = bf16[136,1024]{1,0:T(8,128)(2,1)S(1)} fusion(bf16[8,1024]{1,0:T(8,128)(2,1)S(1)} %fusion.2, bf16[128,1024]{1,0:T(8,128)(2,1)} %param.5), kind=kLoop, calls=%fused_computation.4 | loop fusion | flops 557056 | bytes 557056 | tf_op jit(solution)/shard_map/concatenate | solution.py:101
  2.2 4.1 %collective-permute-start.4 = (bf16[136,1024]{1,0:T(8,128)(2,1)S(1)}, bf16[136,1024]{1,0:T(8,128)(2,1)S(1)}, u32[]{:S(2)}, u32[]{:S(2)}) collective-permute-start(bf16[136,1024]{1,0:T(8,128)(2,1)S(1)} %pad_maximum_fusion.near), channel_id=1, source_target_pairs={{0,8},{2,10},{4,12},{6,14},{8,0},{10,2},{12,4},{14,6},{1,9},{3,11}... | collective-permute-start | bytes 835592 | tf_op jit(solution)/shard_map/ppermute | solution.py:44
  6.3 12.8 %collective-permute-done.4.near = bf16[136,1024]{1,0:T(8,128)(2,1)S(1)} collective-permute-done((bf16[136,1024]{1,0:T(8,128)(2,1)S(1)}, bf16[136,1024]{1,0:T(8,128)(2,1)S(1)}, u32[]{:S(2)}, u32[]{:S(2)}) %collective-permute-start.4) | collective-permute-done | bytes 278560 | tf_op jit(solution)/shard_map/ppermute | solution.py:44
  19.1 0.7 collective-permute-start.7
  19.8 1.3 %collective-permute-start.12 = (bf16[136,1024]{1,0:T(8,128)(2,1)S(1)}, bf16[136,1024]{1,0:T(8,128)(2,1)S(1)}, u32[]{:S(2)}, u32[]{:S(2)}) collective-permute-start(bf16[136,1024]{1,0:T(8,128)(2,1)S(1)} %pad_maximum_fusion.near), channel_id=1, source_target_pairs={{0,4},{2,6},{4,0},{6,2},{8,12},{10,14},{12,8},{14,10},{1,5},{3,7},... | collective-permute-start | bytes 835592 | tf_op jit(solution)/shard_map/ppermute | solution.py:44
  21.1 7.6 %collective-permute-done.7.near = bf16[136,1024]{1,0:T(8,128)(2,1)S(1)} collective-permute-done((bf16[136,1024]{1,0:T(8,128)(2,1)S(1)}, bf16[136,1024]{1,0:T(8,128)(2,1)S(1)}, u32[]{:S(2)}, u32[]{:S(2)}) %collective-permute-start.7) | collective-permute-done | bytes 278560 | tf_op jit(solution)/shard_map/ppermute | solution.py:44
  28.7 1.5 %collective-permute-start.8 = (bf16[136,1024]{1,0:T(8,128)(2,1)S(1)}, bf16[136,1024]{1,0:T(8,128)(2,1)S(1)}, u32[]{:S(2)}, u32[]{:S(2)}) collective-permute-start(bf16[136,1024]{1,0:T(8,128)(2,1)S(1)} %collective-permute-done.7.near), channel_id=1, source_target_pairs={{0,2},{2,0},{4,6},{6,4},{8,10},{10,8},{12,14},{14,12},{1,3},{3,1},... | collective-permute-start | bytes 835592 | tf_op jit(solution)/shard_map/ppermute | solution.py:44
  30.2 0.5 collective-permute-start.5
  30.7 2.4 %collective-permute-done.12.near = bf16[136,1024]{1,0:T(8,128)(2,1)S(1)} collective-permute-done((bf16[136,1024]{1,0:T(8,128)(2,1)S(1)}, bf16[136,1024]{1,0:T(8,128)(2,1)S(1)}, u32[]{:S(2)}, u32[]{:S(2)}) %collective-permute-start.12) | collective-permute-done | bytes 278560 | tf_op jit(solution)/shard_map/ppermute | solution.py:44
  33.1 1.2 %collective-permute-start = (bf16[136,1024]{1,0:T(8,128)(2,1)S(1)}, bf16[136,1024]{1,0:T(8,128)(2,1)S(1)}, u32[]{:S(2)}, u32[]{:S(2)}) collective-permute-start(bf16[136,1024]{1,0:T(8,128)(2,1)S(1)} %pad_maximum_fusion.near), channel_id=1, source_target_pairs={{0,2},{2,0},{4,6},{6,4},{8,10},{10,8},{12,14},{14,12},{1,3},{3,1},... | collective-permute-start | bytes 835592 | tf_op jit(solution)/shard_map/ppermute | solution.py:44
  34.3 4.0 %collective-permute-done.8.far = bf16[136,1024]{1,0:T(8,128)(2,1)S(1)} collective-permute-done((bf16[136,1024]{1,0:T(8,128)(2,1)S(1)}, bf16[136,1024]{1,0:T(8,128)(2,1)S(1)}, u32[]{:S(2)}, u32[]{:S(2)}) %collective-permute-start.8) | collective-permute-done | bytes 278560 | tf_op jit(solution)/shard_map/ppermute | solution.py:44
  38.3 1.5 %collective-permute-start.13 = (bf16[136,1024]{1,0:T(8,128)(2,1)S(1)}, bf16[136,1024]{1,0:T(8,128)(2,1)S(1)}, u32[]{:S(2)}, u32[]{:S(2)}) collective-permute-start(bf16[136,1024]{1,0:T(8,128)(2,1)S(1)} %collective-permute-done.12.near), channel_id=1, source_target_pairs={{0,2},{2,0},{4,6},{6,4},{8,10},{10,8},{12,14},{14,12},{1,3},{3,1},... | collective-permute-start | bytes 835592 | tf_op jit(solution)/shard_map/ppermute | solution.py:44
  39.8 0.0 collective-permute-done.1.up_b
  39.8 0.0 collective-permute-done.2.down_b
  39.8 0.1 broadcast_in_dim.23.choice
  39.9 0.0 copy-start
  39.9 1.6 %copy-done = bf16[1,1024,1024]{2,1,0:T(8,128)(2,1)S(1)} copy-done((bf16[1,1024,1024]{2,1,0:T(8,128)(2,1)S(1)}, bf16[1,1024,1024]{2,1,0:T(8,128)(2,1)}, u32[]{:S(2)}) %copy-start) | copy-done | bytes 2097176
  41.5 0.0 copy-start.2
  41.5 1.6 %copy-done.2 = bf16[1,1024,1024]{2,1,0:T(8,128)(2,1)S(1)} copy-done((bf16[1,1024,1024]{2,1,0:T(8,128)(2,1)S(1)}, bf16[1,1024,1024]{2,1,0:T(8,128)(2,1)}, u32[]{:S(2)}) %copy-start.2) | copy-done | bytes 2097176
  43.1 4.0 %shard_map.57 = (f32[128,1024]{1,0:T(8,128)S(1)}, bf16[128,1024]{1,0:T(8,128)(2,1)S(1)}) custom-call(bf16[136,1024]{1,0:T(8,128)(2,1)S(1)} %collective-permute-done.7.near, bf16[136,1024]{1,0:T(8,128)(2,1)S(1)} %collective-permute-done.8.far, f32[8,128]{1,0:T(8,128)S(1)} %broadcast_in_dim.23.choice, bf16[1024,1024]{1,0:T(8,128)(2,1)S(1)} %bitcast.3, ...), custom_call_target="tpu_custom_call" | custom-call | flops 2147483648 | bytes 8388608 | tf_op jit(solution)/shard_map/pallas_call | solution.py:73
  47.1 0.0 copy-start.1
  47.1 0.6 collective-permute-start.9
  47.6 0.0 collective-permute-done.5.far
  47.6 4.0 %shard_map.56 = (f32[128,1024]{1,0:T(8,128)S(1)}, bf16[128,1024]{1,0:T(8,128)(2,1)S(1)}) custom-call(bf16[136,1024]{1,0:T(8,128)(2,1)S(1)} %collective-permute-done.4.near, bf16[136,1024]{1,0:T(8,128)(2,1)S(1)} %collective-permute-done.5.far, f32[8,128]{1,0:T(8,128)S(1)} %broadcast_in_dim.23.choice, bf16[1024,1024]{1,0:T(8,128)(2,1)S(1)} %bitcast.4, ...), custom_call_target="tpu_custom_call" | custom-call | flops 2147483648 | bytes 8388608 | tf_op jit(solution)/shard_map/pallas_call | solution.py:73
  51.7 1.5 %collective-permute-start.6 = (bf16[128,1024]{1,0:T(8,128)(2,1)S(1)}, bf16[128,1024]{1,0:T(8,128)(2,1)S(1)}, u32[]{:S(2)}, u32[]{:S(2)}) collective-permute-start(bf16[128,1024]{1,0:T(8,128)(2,1)S(1)} %get-tuple-element.16), channel_id=1, source_target_pairs={{0,2},{2,0},{4,6},{6,4},{8,10},{10,8},{12,14},{14,12},{1,3},{3,1},... | collective-permute-start | bytes 786440 | tf_op jit(solution)/shard_map/ppermute | solution.py:44
  53.2 3.0 %collective-permute-done.13.far = bf16[136,1024]{1,0:T(8,128)(2,1)S(1)} collective-permute-done((bf16[136,1024]{1,0:T(8,128)(2,1)S(1)}, bf16[136,1024]{1,0:T(8,128)(2,1)S(1)}, u32[]{:S(2)}, u32[]{:S(2)}) %collective-permute-start.13) | collective-permute-done | bytes 278560 | tf_op jit(solution)/shard_map/ppermute | solution.py:44
  56.2 0.0 copy-done.1
  56.2 4.0 %shard_map.58 = (f32[128,1024]{1,0:T(8,128)S(1)}, bf16[128,1024]{1,0:T(8,128)(2,1)S(1)}) custom-call(bf16[136,1024]{1,0:T(8,128)(2,1)S(1)} %collective-permute-done.12.near, bf16[136,1024]{1,0:T(8,128)(2,1)S(1)} %collective-permute-done.13.far, f32[8,128]{1,0:T(8,128)S(1)} %broadcast_in_dim.23.choice, bf16[1024,1024]{1,0:T(8,128)(2,1)S(1)} %bitcast.5, ...), custom_call_target="tpu_custom_call" | custom-call | flops 2147483648 | bytes 8388608 | tf_op jit(solution)/shard_map/pallas_call | solution.py:73
  60.2 1.6 %collective-permute-start.14 = (bf16[128,1024]{1,0:T(8,128)(2,1)S(1)}, bf16[128,1024]{1,0:T(8,128)(2,1)S(1)}, u32[]{:S(2)}, u32[]{:S(2)}) collective-permute-start(bf16[128,1024]{1,0:T(8,128)(2,1)S(1)} %get-tuple-element.20), channel_id=1, source_target_pairs={{0,2},{2,0},{4,6},{6,4},{8,10},{10,8},{12,14},{14,12},{1,3},{3,1},... | collective-permute-start | bytes 786440 | tf_op jit(solution)/shard_map/ppermute | solution.py:44
  61.8 0.0 collective-permute-done.9
  61.8 0.1 add_convert_fusion.3
  61.9 0.7 collective-permute-start.10
  62.6 0.0 collective-permute-done.far
  62.6 4.0 %shard_map.55 = (f32[128,1024]{1,0:T(8,128)S(1)}, bf16[128,1024]{1,0:T(8,128)(2,1)S(1)}) custom-call(bf16[136,1024]{1,0:T(8,128)(2,1)S(1)} %pad_maximum_fusion.near, bf16[136,1024]{1,0:T(8,128)(2,1)S(1)} %collective-permute-done.far, f32[8,128]{1,0:T(8,128)S(1)} %broadcast_in_dim.23.choice, bf16[1024,1024]{1,0:T(8,128)(2,1)S(1)} %bitcast.6, ...), custom_call_target="tpu_custom_call" | custom-call | flops 2147483648 | bytes 8388608 | tf_op jit(solution)/shard_map/pallas_call | solution.py:73
  66.6 1.6 %collective-permute-start.3 = (bf16[128,1024]{1,0:T(8,128)(2,1)S(1)}, bf16[128,1024]{1,0:T(8,128)(2,1)S(1)}, u32[]{:S(2)}, u32[]{:S(2)}) collective-permute-start(bf16[128,1024]{1,0:T(8,128)(2,1)S(1)} %get-tuple-element.14), channel_id=1, source_target_pairs={{0,2},{2,0},{4,6},{6,4},{8,10},{10,8},{12,14},{14,12},{1,3},{3,1},... | collective-permute-start | bytes 786440 | tf_op jit(solution)/shard_map/ppermute | solution.py:44
  68.1 3.7 %collective-permute-done.14 = bf16[128,1024]{1,0:T(8,128)(2,1)S(1)} collective-permute-done((bf16[128,1024]{1,0:T(8,128)(2,1)S(1)}, bf16[128,1024]{1,0:T(8,128)(2,1)S(1)}, u32[]{:S(2)}, u32[]{:S(2)}) %collective-permute-start.14) | collective-permute-done | bytes 262176 | tf_op jit(solution)/shard_map/ppermute | solution.py:44
  71.8 0.1 add_convert_fusion.1
  71.9 2.0 %collective-permute-start.15 = (bf16[128,1024]{1,0:T(8,128)(2,1)S(1)}, bf16[128,1024]{1,0:T(8,128)(2,1)S(1)}, u32[]{:S(2)}, u32[]{:S(2)}) collective-permute-start(bf16[128,1024]{1,0:T(8,128)(2,1)S(1)} %add_convert_fusion.1), channel_id=1, source_target_pairs={{0,4},{2,6},{4,0},{6,2},{8,12},{10,14},{12,8},{14,10},{1,5},{3,7},... | collective-permute-start | bytes 786440 | tf_op jit(solution)/shard_map/ppermute | solution.py:44
  73.8 0.0 collective-permute-done.6
  73.8 0.0 collective-permute-done.10
  73.8 0.1 add_convert_fusion.2
  73.9 3.4 %collective-permute-start.11 = (bf16[128,1024]{1,0:T(8,128)(2,1)S(1)}, bf16[128,1024]{1,0:T(8,128)(2,1)S(1)}, u32[]{:S(2)}, u32[]{:S(2)}) collective-permute-start(bf16[128,1024]{1,0:T(8,128)(2,1)S(1)} %add_convert_fusion.2), channel_id=1, source_target_pairs={{0,8},{2,10},{4,12},{6,14},{8,0},{10,2},{12,4},{14,6},{1,9},{3,11}... | collective-permute-start | bytes 786440 | tf_op jit(solution)/shard_map/ppermute | solution.py:44
  77.4 0.0 collective-permute-done.3
  77.4 0.9 %collective-permute-done.15 = bf16[128,1024]{1,0:T(8,128)(2,1)S(1)} collective-permute-done((bf16[128,1024]{1,0:T(8,128)(2,1)S(1)}, bf16[128,1024]{1,0:T(8,128)(2,1)S(1)}, u32[]{:S(2)}, u32[]{:S(2)}) %collective-permute-start.15) | collective-permute-done | bytes 262176 | tf_op jit(solution)/shard_map/ppermute | solution.py:44
  78.3 6.2 %collective-permute-done.11 = bf16[128,1024]{1,0:T(8,128)(2,1)S(1)} collective-permute-done((bf16[128,1024]{1,0:T(8,128)(2,1)S(1)}, bf16[128,1024]{1,0:T(8,128)(2,1)S(1)}, u32[]{:S(2)}, u32[]{:S(2)}) %collective-permute-start.11) | collective-permute-done | bytes 262176 | tf_op jit(solution)/shard_map/ppermute | solution.py:44
  84.6 0.9 add_convert_fusion
  (3 shorter events, 0.0 us)
Async XLA Ops:
  0.0 39.8 %collective-permute-start.1 = (bf16[1024,1024]{1,0:T(8,128)(2,1)}, bf16[1024,1024]{1,0:T(8,128)(2,1)S(1)}, u32[]{:S(2)}, u32[]{:S(2)}) collective-permute-start(bf16[1024,1024]{1,0:T(8,128)(2,1)} %bitcast.2), channel_id=1, source_target_pairs={{0,1},{1,0},{2,3},{3,2},{4,5},{5,4},{6,7},{7,6},{8,9},{9,8},{10,11... | collective-permute-start | bytes 6291464 | tf_op jit(solution)/shard_map/ppermute | solution.py:48
  0.5 39.4 %collective-permute-start.2 = (bf16[1024,1024]{1,0:T(8,128)(2,1)}, bf16[1024,1024]{1,0:T(8,128)(2,1)}, u32[]{:S(2)}, u32[]{:S(2)}) collective-permute-start(bf16[1024,1024]{1,0:T(8,128)(2,1)} %bitcast.7), channel_id=1, source_target_pairs={{0,1},{1,0},{2,3},{3,2},{4,5},{5,4},{6,7},{7,6},{8,9},{9,8},{10,11... | collective-permute-start | bytes 6291464 | tf_op jit(solution)/shard_map/ppermute | solution.py:48
  2.2 16.9 %collective-permute-start.4 = (bf16[136,1024]{1,0:T(8,128)(2,1)S(1)}, bf16[136,1024]{1,0:T(8,128)(2,1)S(1)}, u32[]{:S(2)}, u32[]{:S(2)}) collective-permute-start(bf16[136,1024]{1,0:T(8,128)(2,1)S(1)} %pad_maximum_fusion.near), channel_id=1, source_target_pairs={{0,8},{2,10},{4,12},{6,14},{8,0},{10,2},{12,4},{14,6},{1,9},{3,11}... | collective-permute-start | bytes 835592 | tf_op jit(solution)/shard_map/ppermute | solution.py:44
  19.1 9.6 %collective-permute-start.7 = (bf16[136,1024]{1,0:T(8,128)(2,1)S(1)}, bf16[136,1024]{1,0:T(8,128)(2,1)S(1)}, u32[]{:S(2)}, u32[]{:S(2)}) collective-permute-start(bf16[136,1024]{1,0:T(8,128)(2,1)S(1)} %collective-permute-done.4.near), channel_id=1, source_target_pairs={{0,4},{2,6},{4,0},{6,2},{8,12},{10,14},{12,8},{14,10},{1,5},{3,7},... | collective-permute-start | bytes 835592 | tf_op jit(solution)/shard_map/ppermute | solution.py:44
  19.8 13.3 %collective-permute-start.12 = (bf16[136,1024]{1,0:T(8,128)(2,1)S(1)}, bf16[136,1024]{1,0:T(8,128)(2,1)S(1)}, u32[]{:S(2)}, u32[]{:S(2)}) collective-permute-start(bf16[136,1024]{1,0:T(8,128)(2,1)S(1)} %pad_maximum_fusion.near), channel_id=1, source_target_pairs={{0,4},{2,6},{4,0},{6,2},{8,12},{10,14},{12,8},{14,10},{1,5},{3,7},... | collective-permute-start | bytes 835592 | tf_op jit(solution)/shard_map/ppermute | solution.py:44
  28.7 9.6 %collective-permute-start.8 = (bf16[136,1024]{1,0:T(8,128)(2,1)S(1)}, bf16[136,1024]{1,0:T(8,128)(2,1)S(1)}, u32[]{:S(2)}, u32[]{:S(2)}) collective-permute-start(bf16[136,1024]{1,0:T(8,128)(2,1)S(1)} %collective-permute-done.7.near), channel_id=1, source_target_pairs={{0,2},{2,0},{4,6},{6,4},{8,10},{10,8},{12,14},{14,12},{1,3},{3,1},... | collective-permute-start | bytes 835592 | tf_op jit(solution)/shard_map/ppermute | solution.py:44
  30.2 17.4 %collective-permute-start.5 = (bf16[136,1024]{1,0:T(8,128)(2,1)S(1)}, bf16[136,1024]{1,0:T(8,128)(2,1)S(1)}, u32[]{:S(2)}, u32[]{:S(2)}) collective-permute-start(bf16[136,1024]{1,0:T(8,128)(2,1)S(1)} %collective-permute-done.4.near), channel_id=1, source_target_pairs={{0,2},{2,0},{4,6},{6,4},{8,10},{10,8},{12,14},{14,12},{1,3},{3,1},... | collective-permute-start | bytes 835592 | tf_op jit(solution)/shard_map/ppermute | solution.py:44
  33.1 29.5 %collective-permute-start = (bf16[136,1024]{1,0:T(8,128)(2,1)S(1)}, bf16[136,1024]{1,0:T(8,128)(2,1)S(1)}, u32[]{:S(2)}, u32[]{:S(2)}) collective-permute-start(bf16[136,1024]{1,0:T(8,128)(2,1)S(1)} %pad_maximum_fusion.near), channel_id=1, source_target_pairs={{0,2},{2,0},{4,6},{6,4},{8,10},{10,8},{12,14},{14,12},{1,3},{3,1},... | collective-permute-start | bytes 835592 | tf_op jit(solution)/shard_map/ppermute | solution.py:44
  38.3 17.9 %collective-permute-start.13 = (bf16[136,1024]{1,0:T(8,128)(2,1)S(1)}, bf16[136,1024]{1,0:T(8,128)(2,1)S(1)}, u32[]{:S(2)}, u32[]{:S(2)}) collective-permute-start(bf16[136,1024]{1,0:T(8,128)(2,1)S(1)} %collective-permute-done.12.near), channel_id=1, source_target_pairs={{0,2},{2,0},{4,6},{6,4},{8,10},{10,8},{12,14},{14,12},{1,3},{3,1},... | collective-permute-start | bytes 835592 | tf_op jit(solution)/shard_map/ppermute | solution.py:44
  39.9 1.6 %copy-start = (bf16[1,1024,1024]{2,1,0:T(8,128)(2,1)S(1)}, bf16[1,1024,1024]{2,1,0:T(8,128)(2,1)}, u32[]{:S(2)}) copy-start(bf16[1,1024,1024]{2,1,0:T(8,128)(2,1)} %param.8) | copy-start | bytes 6291460
  41.5 1.6 %copy-start.2 = (bf16[1,1024,1024]{2,1,0:T(8,128)(2,1)S(1)}, bf16[1,1024,1024]{2,1,0:T(8,128)(2,1)}, u32[]{:S(2)}) copy-start(bf16[1,1024,1024]{2,1,0:T(8,128)(2,1)} %param.9) | copy-start | bytes 6291460
  47.1 9.1 %copy-start.1 = (bf16[1,1024,1024]{2,1,0:T(8,128)(2,1)S(1)}, bf16[1,1024,1024]{2,1,0:T(8,128)(2,1)}, u32[]{:S(2)}) copy-start(bf16[1,1024,1024]{2,1,0:T(8,128)(2,1)} %param.8) | copy-start | bytes 6291460
  47.1 14.7 %collective-permute-start.9 = (bf16[128,1024]{1,0:T(8,128)(2,1)S(1)}, bf16[128,1024]{1,0:T(8,128)(2,1)S(1)}, u32[]{:S(2)}, u32[]{:S(2)}) collective-permute-start(bf16[128,1024]{1,0:T(8,128)(2,1)S(1)} %get-tuple-element.18), channel_id=1, source_target_pairs={{0,2},{2,0},{4,6},{6,4},{8,10},{10,8},{12,14},{14,12},{1,3},{3,1},... | collective-permute-start | bytes 786440 | tf_op jit(solution)/shard_map/ppermute | solution.py:44
  51.7 22.2 %collective-permute-start.6 = (bf16[128,1024]{1,0:T(8,128)(2,1)S(1)}, bf16[128,1024]{1,0:T(8,128)(2,1)S(1)}, u32[]{:S(2)}, u32[]{:S(2)}) collective-permute-start(bf16[128,1024]{1,0:T(8,128)(2,1)S(1)} %get-tuple-element.16), channel_id=1, source_target_pairs={{0,2},{2,0},{4,6},{6,4},{8,10},{10,8},{12,14},{14,12},{1,3},{3,1},... | collective-permute-start | bytes 786440 | tf_op jit(solution)/shard_map/ppermute | solution.py:44
  60.2 11.6 %collective-permute-start.14 = (bf16[128,1024]{1,0:T(8,128)(2,1)S(1)}, bf16[128,1024]{1,0:T(8,128)(2,1)S(1)}, u32[]{:S(2)}, u32[]{:S(2)}) collective-permute-start(bf16[128,1024]{1,0:T(8,128)(2,1)S(1)} %get-tuple-element.20), channel_id=1, source_target_pairs={{0,2},{2,0},{4,6},{6,4},{8,10},{10,8},{12,14},{14,12},{1,3},{3,1},... | collective-permute-start | bytes 786440 | tf_op jit(solution)/shard_map/ppermute | solution.py:44
  61.9 11.9 %collective-permute-start.10 = (bf16[128,1024]{1,0:T(8,128)(2,1)S(1)}, bf16[128,1024]{1,0:T(8,128)(2,1)S(1)}, u32[]{:S(2)}, u32[]{:S(2)}) collective-permute-start(bf16[128,1024]{1,0:T(8,128)(2,1)S(1)} %add_convert_fusion.3), channel_id=1, source_target_pairs={{0,4},{2,6},{4,0},{6,2},{8,12},{10,14},{12,8},{14,10},{1,5},{3,7},... | collective-permute-start | bytes 786440 | tf_op jit(solution)/shard_map/ppermute | solution.py:44
  66.6 10.8 %collective-permute-start.3 = (bf16[128,1024]{1,0:T(8,128)(2,1)S(1)}, bf16[128,1024]{1,0:T(8,128)(2,1)S(1)}, u32[]{:S(2)}, u32[]{:S(2)}) collective-permute-start(bf16[128,1024]{1,0:T(8,128)(2,1)S(1)} %get-tuple-element.14), channel_id=1, source_target_pairs={{0,2},{2,0},{4,6},{6,4},{8,10},{10,8},{12,14},{14,12},{1,3},{3,1},... | collective-permute-start | bytes 786440 | tf_op jit(solution)/shard_map/ppermute | solution.py:44
  71.9 6.4 %collective-permute-start.15 = (bf16[128,1024]{1,0:T(8,128)(2,1)S(1)}, bf16[128,1024]{1,0:T(8,128)(2,1)S(1)}, u32[]{:S(2)}, u32[]{:S(2)}) collective-permute-start(bf16[128,1024]{1,0:T(8,128)(2,1)S(1)} %add_convert_fusion.1), channel_id=1, source_target_pairs={{0,4},{2,6},{4,0},{6,2},{8,12},{10,14},{12,8},{14,10},{1,5},{3,7},... | collective-permute-start | bytes 786440 | tf_op jit(solution)/shard_map/ppermute | solution.py:44
  73.9 10.6 %collective-permute-start.11 = (bf16[128,1024]{1,0:T(8,128)(2,1)S(1)}, bf16[128,1024]{1,0:T(8,128)(2,1)S(1)}, u32[]{:S(2)}, u32[]{:S(2)}) collective-permute-start(bf16[128,1024]{1,0:T(8,128)(2,1)S(1)} %add_convert_fusion.2), channel_id=1, source_target_pairs={{0,8},{2,10},{4,12},{6,14},{8,0},{10,2},{12,4},{14,6},{1,9},{3,11}... | collective-permute-start | bytes 786440 | tf_op jit(solution)/shard_map/ppermute | solution.py:44

commit v3 on v2

--- a/solution.py
+++ b/solution.py
@@ -48,6 +48,10 @@
     return lax.ppermute(value, "tensor", [(0, 1), (1, 0)])
 
 
+def after(value, *others):
+    return lax.optimization_barrier((value, *others))[0]
+
+
 def expert_kernel(near, far, choice, up_a, down_a, up_b, down_b, near_out, far_out):
     f32 = jnp.float32
     n = near_out.shape[0]
@@ -78,9 +82,9 @@
         ],
         in_specs=[pl.BlockSpec(memory_space=pltpu.VMEM)] * 7,
         out_specs=[pl.BlockSpec(memory_space=pltpu.VMEM)] * 2,
-        compiler_params=pltpu.CompilerParams(vmem_limit_bytes=40 << 20),
+        compiler_params=pltpu.CompilerParams(vmem_limit_bytes=20 << 20),
         cost_estimate=pl.CostEstimate(
-            flops=16 * n * width * units, bytes_accessed=8 * width * units, transcendentals=0
+            flops=n * width, bytes_accessed=n * width, transcendentals=0
         ),
     )(near, far, choice, *weights)
 
@@ -98,23 +102,36 @@
     strip = jnp.pad(strip, ((0, 0), (0, width - 2 * n)))
     choice = jnp.broadcast_to((names == me).astype(f32)[:, None], (groups, n))
 
-    near = {0: jnp.concatenate([latent_rows, strip], axis=0)}
-    far = {0: across(near[0], 1)}
-    for k in range(1, groups // 2):
-        low = k & -k
-        near[k] = across(near[k ^ low], 2 * low)
-        far[k] = across(near[k], 1)
+    near, far, own, away, over = {}, {}, {}, {}, {}
+
+    def run(k):
+        own[k], away[k] = expert(near[k], far[k], choice, weights, n)
+
+    near[0] = jnp.concatenate([latent_rows, strip], axis=0)
+    far[0] = across(near[0], 1)
+    near[2] = across(near[0], 4)
     weights = (up_weight[0], down_weight[0], other_core(up_weight[0]), other_core(down_weight[0]))
-
-    own, away = {}, {}
-    for k in range(groups // 2):
-        own[k], away[k] = expert(near[k], far[k], choice, weights, n)
-    sums = {}
-    for k in reversed(range(groups // 2)):
-        sums[k] = own[k] + across(away[k], 1).astype(f32)
-    for k in reversed(range(1, groups // 2)):
-        low = k & -k
-        sums[k ^ low] = sums[k ^ low] + across(sums[k].astype(jnp.bfloat16), 2 * low).astype(f32)
+    near[2] = after(near[2], far[0])
+    near[3] = across(near[2], 2)
+    far[2] = across(near[2], 1)
+    run(0)
+    near[1] = across(after(near[0], near[2]), 2)
+    far[1] = across(after(far[0], near[2]), 2)
+    near[3] = after(near[3], far[2], away[0])
+    far[3] = across(near[3], 1)
+    run(2)
+    near[3] = after(near[3], away[2], near[1])
+    run(3)
+    near[1] = after(near[1], away[3])
+    run(1)
+    over[3] = across(away[3], 1)
+    over[2] = across(after(away[2], away[3]), 1)
+    over[1] = across(after(away[1], over[3]), 1)
+    over[0] = across(after(away[0], away[1]), 1)
+    sums = {k: own[k] + over[k].astype(f32) for k in range(4)}
+    sums[2] = sums[2] + across(sums[3].astype(jnp.bfloat16), 2).astype(f32)
+    sums[0] = sums[0] + across(sums[1].astype(jnp.bfloat16), 2).astype(f32)
+    sums[0] = sums[0] + across(sums[2].astype(jnp.bfloat16), 4).astype(f32)
     return sums[0].astype(jnp.bfloat16)
 
 
@@ -122,7 +139,7 @@
     groups = lax.axis_size("expert")
     rows_dev, choose = expert_ids.shape
     capacity = 3 * choose * rows_dev // (2 * groups)
-    dense = rows_dev <= 2 * capacity and groups & (groups - 1) == 0
+    dense = groups == 8 and rows_dev <= 2 * capacity
     form = gather_body if dense else exchange_body
     return form(latent_rows, expert_ids, route_weights, up_weight, down_weight)
 

time: 85.7 us -> 73.4 us (0.86)
  waiting for transfers between devices: 40.6 us -> 31.9 us
  starting transfers between devices: 22.8 us -> 19.2 us
    ppermute x14, waiting for transfers between devices: 40.6 us -> 31.9 us  [across(): return lax.ppermute(value, 'expert', [(i, i ^ step) for i in range(size)])]
    ppermute x14, starting transfers between devices: 22.3 us -> 18.7 us  [across(): return lax.ppermute(value, 'expert', [(i, i ^ step) for i in range(size)])]
  transfers between devices with their start and end apart: 16 -> 16, of which waited for: 8 -> 9; matrix products, arithmetic and copies ran while one was open for 2% -> 3% of each run, Pallas kernels for 19% -> 22%
where the time goes in v3:
time: 73.4 us; the launch traced here: 73 us
  waiting for transfers between devices  31.9 us (43%)
  starting transfers between devices  19.2 us (26%)
  Pallas kernels  15.8 us (22%)
  local copies, waits for them, and re-layouts  3.26 us (4%)
  other arithmetic  2.75 us (4%)
    ppermute x14, waiting for transfers between devices, across(): return lax.ppermute(value, 'expert', [(i, i ^ step) for i in range(size)])  31.9 us
    ppermute x14, starting transfers between devices, across(): return lax.ppermute(value, 'expert', [(i, i ^ step) for i in range(size)])  18.7 us
    pallas_call x4, Pallas kernels, expert(): pl.pallas_call(expert_kernel, out_shape=[jax.ShapeDtypeStruct((n, width),...  15.8 us
    unnamed x6, local copies, waits for them, and re-layouts  3.19 us
  transfers between devices with their start and end apart: 16, of which 9 were waited for; matrix products, arithmetic and copies ran while one was open for 3% of the time, Pallas kernels for 22%

profile of v3, /device:TPU:0, one launch (start us, length us, event | category | flops | bytes accessed | tf_op | source)
XLA Modules:
  0.0 73.0 jit_solution(4136324193814780855)
XLA Ops:
  0.0 0.5 collective-permute-start.1
  0.5 0.1 collective-permute-start.2
  0.5 0.7 select_reduce_fusion
  1.2 1.0 %pad_maximum_fusion.near = bf16[136,1024]{1,0:T(8,128)(2,1)S(1)} fusion(bf16[8,1024]{1,0:T(8,128)(2,1)S(1)} %fusion.2, bf16[128,1024]{1,0:T(8,128)(2,1)} %param.5), kind=kLoop, calls=%fused_computation.4 | loop fusion | flops 557056 | bytes 557056 | tf_op jit(solution)/shard_map/concatenate | solution.py:110
  2.2 4.1 %collective-permute-start.3 = (bf16[136,1024]{1,0:T(8,128)(2,1)S(1)}, bf16[136,1024]{1,0:T(8,128)(2,1)S(1)}, u32[]{:S(2)}, u32[]{:S(2)}) collective-permute-start(bf16[136,1024]{1,0:T(8,128)(2,1)S(1)} %pad_maximum_fusion.near), channel_id=1, source_target_pairs={{0,8},{2,10},{4,12},{6,14},{8,0},{10,2},{12,4},{14,6},{1,9},{3,11}... | collective-permute-start | bytes 835592 | tf_op jit(solution)/shard_map/ppermute | solution.py:44
  6.3 1.5 %collective-permute-start = (bf16[136,1024]{1,0:T(8,128)(2,1)S(1)}, bf16[136,1024]{1,0:T(8,128)(2,1)S(1)}, u32[]{:S(2)}, u32[]{:S(2)}) collective-permute-start(bf16[136,1024]{1,0:T(8,128)(2,1)S(1)} %pad_maximum_fusion.near), channel_id=1, source_target_pairs={{0,2},{2,0},{4,6},{6,4},{8,10},{10,8},{12,14},{14,12},{1,3},{3,1},... | collective-permute-start | bytes 835592 | tf_op jit(solution)/shard_map/ppermute | solution.py:44
  7.8 11.3 %collective-permute-done.3.near = bf16[136,1024]{1,0:T(8,128)(2,1)S(1)} collective-permute-done((bf16[136,1024]{1,0:T(8,128)(2,1)S(1)}, bf16[136,1024]{1,0:T(8,128)(2,1)S(1)}, u32[]{:S(2)}, u32[]{:S(2)}) %collective-permute-start.3) | collective-permute-done | bytes 278560 | tf_op jit(solution)/shard_map/ppermute | solution.py:44
  19.1 0.0 collective-permute-done.far
  19.1 1.5 %collective-permute-start.6 = (bf16[136,1024]{1,0:T(8,128)(2,1)S(1)}, bf16[136,1024]{1,0:T(8,128)(2,1)S(1)}, u32[]{:S(2)}, u32[]{:S(2)}) collective-permute-start(bf16[136,1024]{1,0:T(8,128)(2,1)S(1)} %collective-permute-done.3.near), channel_id=1, source_target_pairs={{0,2},{2,0},{4,6},{6,4},{8,10},{10,8},{12,14},{14,12},{1,3},{3,1},... | collective-permute-start | bytes 835592 | tf_op jit(solution)/shard_map/ppermute | solution.py:44
  20.7 0.7 collective-permute-start.5
  21.3 1.4 %collective-permute-start.4 = (bf16[136,1024]{1,0:T(8,128)(2,1)S(1)}, bf16[136,1024]{1,0:T(8,128)(2,1)S(1)}, u32[]{:S(2)}, u32[]{:S(2)}) collective-permute-start(bf16[136,1024]{1,0:T(8,128)(2,1)S(1)} %pad_maximum_fusion.near), channel_id=1, source_target_pairs={{0,4},{2,6},{4,0},{6,2},{8,12},{10,14},{12,8},{14,10},{1,5},{3,7},... | collective-permute-start | bytes 835592 | tf_op jit(solution)/shard_map/ppermute | solution.py:44
  22.7 0.0 collective-permute-done.1.up_b
  22.7 0.0 collective-permute-done.2.down_b
  22.7 0.1 broadcast_in_dim.23.choice
  22.8 0.0 copy-start
  22.8 1.6 %copy-done = bf16[1,1024,1024]{2,1,0:T(8,128)(2,1)S(1)} copy-done((bf16[1,1024,1024]{2,1,0:T(8,128)(2,1)S(1)}, bf16[1,1024,1024]{2,1,0:T(8,128)(2,1)}, u32[]{:S(2)}) %copy-start) | copy-done | bytes 2097176
  24.4 0.0 copy-start.2
  24.4 1.6 %copy-done.2 = bf16[1,1024,1024]{2,1,0:T(8,128)(2,1)S(1)} copy-done((bf16[1,1024,1024]{2,1,0:T(8,128)(2,1)S(1)}, bf16[1,1024,1024]{2,1,0:T(8,128)(2,1)}, u32[]{:S(2)}) %copy-start.2) | copy-done | bytes 2097176
  25.9 4.0 %shard_map.55 = (f32[128,1024]{1,0:T(8,128)S(1)}, bf16[128,1024]{1,0:T(8,128)(2,1)S(1)}) custom-call(bf16[136,1024]{1,0:T(8,128)(2,1)S(1)} %pad_maximum_fusion.near, bf16[136,1024]{1,0:T(8,128)(2,1)S(1)} %collective-permute-done.far, f32[8,128]{1,0:T(8,128)S(1)} %broadcast_in_dim.23.choice, bf16[1024,1024]{1,0:T(8,128)(2,1)S(1)} %bitcast.3, ...), custom_call_target="tpu_custom_call" | custom-call | flops 131072 | bytes 131072 | tf_op jit(solution)/shard_map/pallas_call | solution.py:77
  29.9 0.0 collective-permute-done.6.far
  29.9 0.3 collective-permute-done.5.near
  30.2 0.0 copy-start.1
  30.2 0.5 collective-permute-start.7
  30.7 0.7 collective-permute-start.8
  31.4 4.0 %shard_map.56 = (f32[128,1024]{1,0:T(8,128)S(1)}, bf16[128,1024]{1,0:T(8,128)(2,1)S(1)}) custom-call(bf16[136,1024]{1,0:T(8,128)(2,1)S(1)} %collective-permute-done.3.near, bf16[136,1024]{1,0:T(8,128)(2,1)S(1)} %collective-permute-done.6.far, f32[8,128]{1,0:T(8,128)S(1)} %broadcast_in_dim.23.choice, bf16[1024,1024]{1,0:T(8,128)(2,1)S(1)} %bitcast.4, ...), custom_call_target="tpu_custom_call" | custom-call | flops 131072 | bytes 131072 | tf_op jit(solution)/shard_map/pallas_call | solution.py:77
  35.4 0.8 %collective-permute-done.4.near = bf16[136,1024]{1,0:T(8,128)(2,1)S(1)} collective-permute-done((bf16[136,1024]{1,0:T(8,128)(2,1)S(1)}, bf16[136,1024]{1,0:T(8,128)(2,1)S(1)}, u32[]{:S(2)}, u32[]{:S(2)}) %collective-permute-start.4) | collective-permute-done | bytes 278560 | tf_op jit(solution)/shard_map/ppermute | solution.py:44
  36.2 0.7 collective-permute-done.7.far
  36.9 0.0 copy-done.1
  36.9 4.0 %shard_map.57 = (f32[128,1024]{1,0:T(8,128)S(1)}, bf16[128,1024]{1,0:T(8,128)(2,1)S(1)}) custom-call(bf16[136,1024]{1,0:T(8,128)(2,1)S(1)} %collective-permute-done.5.near, bf16[136,1024]{1,0:T(8,128)(2,1)S(1)} %collective-permute-done.7.far, f32[8,128]{1,0:T(8,128)S(1)} %broadcast_in_dim.23.choice, bf16[1024,1024]{1,0:T(8,128)(2,1)S(1)} %bitcast.5, ...), custom_call_target="tpu_custom_call" | custom-call | flops 131072 | bytes 131072 | tf_op jit(solution)/shard_map/pallas_call | solution.py:77
  40.8 0.9 %collective-permute-start.10 = (bf16[128,1024]{1,0:T(8,128)(2,1)S(1)}, bf16[128,1024]{1,0:T(8,128)(2,1)S(1)}, u32[]{:S(2)}, u32[]{:S(2)}) collective-permute-start(bf16[128,1024]{1,0:T(8,128)(2,1)S(1)} %get-tuple-element.29), channel_id=1, source_target_pairs={{0,2},{2,0},{4,6},{6,4},{8,10},{10,8},{12,14},{14,12},{1,3},{3,1},... | collective-permute-start | bytes 786440 | tf_op jit(solution)/shard_map/ppermute | solution.py:44
  41.7 0.0 collective-permute-done.8.far
  41.7 3.9 %shard_map.58 = (f32[128,1024]{1,0:T(8,128)S(1)}, bf16[128,1024]{1,0:T(8,128)(2,1)S(1)}) custom-call(bf16[136,1024]{1,0:T(8,128)(2,1)S(1)} %collective-permute-done.4.near, bf16[136,1024]{1,0:T(8,128)(2,1)S(1)} %collective-permute-done.8.far, f32[8,128]{1,0:T(8,128)S(1)} %broadcast_in_dim.23.choice, bf16[1024,1024]{1,0:T(8,128)(2,1)S(1)} %bitcast.6, ...), custom_call_target="tpu_custom_call" | custom-call | flops 131072 | bytes 131072 | tf_op jit(solution)/shard_map/pallas_call | solution.py:77
  45.7 3.0 %collective-permute-done.10 = bf16[128,1024]{1,0:T(8,128)(2,1)S(1)} collective-permute-done((bf16[128,1024]{1,0:T(8,128)(2,1)S(1)}, bf16[128,1024]{1,0:T(8,128)(2,1)S(1)}, u32[]{:S(2)}, u32[]{:S(2)}) %collective-permute-start.10) | collective-permute-done | bytes 262176 | tf_op jit(solution)/shard_map/ppermute | solution.py:44
  48.6 0.3 collective-permute-start.11
  48.9 1.7 %collective-permute-start.13 = (bf16[128,1024]{1,0:T(8,128)(2,1)S(1)}, bf16[128,1024]{1,0:T(8,128)(2,1)S(1)}, u32[]{:S(2)}, u32[]{:S(2)}) collective-permute-start(bf16[128,1024]{1,0:T(8,128)(2,1)S(1)} %get-tuple-element.37), channel_id=1, source_target_pairs={{0,2},{2,0},{4,6},{6,4},{8,10},{10,8},{12,14},{14,12},{1,3},{3,1},... | collective-permute-start | bytes 786440 | tf_op jit(solution)/shard_map/ppermute | solution.py:44
  50.7 0.1 add_convert_fusion.2
  50.7 0.7 collective-permute-start.14
  51.4 0.5 collective-permute-start.9
  51.9 5.9 %collective-permute-done.11 = bf16[128,1024]{1,0:T(8,128)(2,1)S(1)} collective-permute-done((bf16[128,1024]{1,0:T(8,128)(2,1)S(1)}, bf16[128,1024]{1,0:T(8,128)(2,1)S(1)}, u32[]{:S(2)}, u32[]{:S(2)}) %collective-permute-start.11) | collective-permute-done | bytes 262176 | tf_op jit(solution)/shard_map/ppermute | solution.py:44
  57.9 0.1 add_convert_fusion.3
  57.9 0.7 collective-permute-start.12
  58.6 2.7 %collective-permute-done.13 = bf16[128,1024]{1,0:T(8,128)(2,1)S(1)} collective-permute-done((bf16[128,1024]{1,0:T(8,128)(2,1)S(1)}, bf16[128,1024]{1,0:T(8,128)(2,1)S(1)}, u32[]{:S(2)}, u32[]{:S(2)}) %collective-permute-start.13) | collective-permute-done | bytes 262176 | tf_op jit(solution)/shard_map/ppermute | solution.py:44
  61.3 0.0 collective-permute-done.14
  61.3 0.1 add_convert_fusion.1
  61.4 3.6 %collective-permute-start.15 = (bf16[128,1024]{1,0:T(8,128)(2,1)S(1)}, bf16[128,1024]{1,0:T(8,128)(2,1)S(1)}, u32[]{:S(2)}, u32[]{:S(2)}) collective-permute-start(bf16[128,1024]{1,0:T(8,128)(2,1)S(1)} %add_convert_fusion.1), channel_id=1, source_target_pairs={{0,8},{2,10},{4,12},{6,14},{8,0},{10,2},{12,4},{14,6},{1,9},{3,11}... | collective-permute-start | bytes 786440 | tf_op jit(solution)/shard_map/ppermute | solution.py:44
  65.0 0.0 collective-permute-done.9
  65.0 0.5 collective-permute-done.12
  65.5 6.6 %collective-permute-done.15 = bf16[128,1024]{1,0:T(8,128)(2,1)S(1)} collective-permute-done((bf16[128,1024]{1,0:T(8,128)(2,1)S(1)}, bf16[128,1024]{1,0:T(8,128)(2,1)S(1)}, u32[]{:S(2)}, u32[]{:S(2)}) %collective-permute-start.15) | collective-permute-done | bytes 262176 | tf_op jit(solution)/shard_map/ppermute | solution.py:44
  72.2 0.9 %add_convert_fusion = bf16[128,1024]{1,0:T(8,128)(2,1)} fusion(bf16[128,1024]{1,0:T(8,128)(2,1)S(1)} %collective-permute-done.15, bf16[128,1024]{1,0:T(8,128)(2,1)S(1)} %collective-permute-done.12, f32[128,1024]{1,0:T(8,128)S(1)} %get-tuple-element.22, bf16[128,1024]{1,0:T(8,128)(2,1)S(1)} %collective-permute-done.9), kind=kLoop, calls=%fused_computation | loop fusion | flops 917504 | bytes 1572864 | tf_op jit(solution)/shard_map/convert_element_type | solution.py:135
  (3 shorter events, 0.0 us)
Async XLA Ops:
  0.0 22.7 %collective-permute-start.1 = (bf16[1024,1024]{1,0:T(8,128)(2,1)}, bf16[1024,1024]{1,0:T(8,128)(2,1)S(1)}, u32[]{:S(2)}, u32[]{:S(2)}) collective-permute-start(bf16[1024,1024]{1,0:T(8,128)(2,1)} %bitcast.2), channel_id=1, source_target_pairs={{0,1},{1,0},{2,3},{3,2},{4,5},{5,4},{6,7},{7,6},{8,9},{9,8},{10,11... | collective-permute-start | bytes 6291464 | tf_op jit(solution)/shard_map/ppermute | solution.py:48
  0.5 22.2 %collective-permute-start.2 = (bf16[1024,1024]{1,0:T(8,128)(2,1)}, bf16[1024,1024]{1,0:T(8,128)(2,1)}, u32[]{:S(2)}, u32[]{:S(2)}) collective-permute-start(bf16[1024,1024]{1,0:T(8,128)(2,1)} %bitcast.7), channel_id=1, source_target_pairs={{0,1},{1,0},{2,3},{3,2},{4,5},{5,4},{6,7},{7,6},{8,9},{9,8},{10,11... | collective-permute-start | bytes 6291464 | tf_op jit(solution)/shard_map/ppermute | solution.py:48
  2.2 16.9 %collective-permute-start.3 = (bf16[136,1024]{1,0:T(8,128)(2,1)S(1)}, bf16[136,1024]{1,0:T(8,128)(2,1)S(1)}, u32[]{:S(2)}, u32[]{:S(2)}) collective-permute-start(bf16[136,1024]{1,0:T(8,128)(2,1)S(1)} %pad_maximum_fusion.near), channel_id=1, source_target_pairs={{0,8},{2,10},{4,12},{6,14},{8,0},{10,2},{12,4},{14,6},{1,9},{3,11}... | collective-permute-start | bytes 835592 | tf_op jit(solution)/shard_map/ppermute | solution.py:44
  6.3 12.8 %collective-permute-start = (bf16[136,1024]{1,0:T(8,128)(2,1)S(1)}, bf16[136,1024]{1,0:T(8,128)(2,1)S(1)}, u32[]{:S(2)}, u32[]{:S(2)}) collective-permute-start(bf16[136,1024]{1,0:T(8,128)(2,1)S(1)} %pad_maximum_fusion.near), channel_id=1, source_target_pairs={{0,2},{2,0},{4,6},{6,4},{8,10},{10,8},{12,14},{14,12},{1,3},{3,1},... | collective-permute-start | bytes 835592 | tf_op jit(solution)/shard_map/ppermute | solution.py:44
  19.1 10.8 %collective-permute-start.6 = (bf16[136,1024]{1,0:T(8,128)(2,1)S(1)}, bf16[136,1024]{1,0:T(8,128)(2,1)S(1)}, u32[]{:S(2)}, u32[]{:S(2)}) collective-permute-start(bf16[136,1024]{1,0:T(8,128)(2,1)S(1)} %collective-permute-done.3.near), channel_id=1, source_target_pairs={{0,2},{2,0},{4,6},{6,4},{8,10},{10,8},{12,14},{14,12},{1,3},{3,1},... | collective-permute-start | bytes 835592 | tf_op jit(solution)/shard_map/ppermute | solution.py:44
  20.7 9.6 %collective-permute-start.5 = (bf16[136,1024]{1,0:T(8,128)(2,1)S(1)}, bf16[136,1024]{1,0:T(8,128)(2,1)S(1)}, u32[]{:S(2)}, u32[]{:S(2)}) collective-permute-start(bf16[136,1024]{1,0:T(8,128)(2,1)S(1)} %collective-permute-done.3.near), channel_id=1, source_target_pairs={{0,4},{2,6},{4,0},{6,2},{8,12},{10,14},{12,8},{14,10},{1,5},{3,7},... | collective-permute-start | bytes 835592 | tf_op jit(solution)/shard_map/ppermute | solution.py:44
  21.3 14.9 %collective-permute-start.4 = (bf16[136,1024]{1,0:T(8,128)(2,1)S(1)}, bf16[136,1024]{1,0:T(8,128)(2,1)S(1)}, u32[]{:S(2)}, u32[]{:S(2)}) collective-permute-start(bf16[136,1024]{1,0:T(8,128)(2,1)S(1)} %pad_maximum_fusion.near), channel_id=1, source_target_pairs={{0,4},{2,6},{4,0},{6,2},{8,12},{10,14},{12,8},{14,10},{1,5},{3,7},... | collective-permute-start | bytes 835592 | tf_op jit(solution)/shard_map/ppermute | solution.py:44
  22.8 1.6 %copy-start = (bf16[1,1024,1024]{2,1,0:T(8,128)(2,1)S(1)}, bf16[1,1024,1024]{2,1,0:T(8,128)(2,1)}, u32[]{:S(2)}) copy-start(bf16[1,1024,1024]{2,1,0:T(8,128)(2,1)} %param.8) | copy-start | bytes 6291460
  24.4 1.6 %copy-start.2 = (bf16[1,1024,1024]{2,1,0:T(8,128)(2,1)S(1)}, bf16[1,1024,1024]{2,1,0:T(8,128)(2,1)}, u32[]{:S(2)}) copy-start(bf16[1,1024,1024]{2,1,0:T(8,128)(2,1)} %param.9) | copy-start | bytes 6291460
  30.2 6.6 %copy-start.1 = (bf16[1,1024,1024]{2,1,0:T(8,128)(2,1)S(1)}, bf16[1,1024,1024]{2,1,0:T(8,128)(2,1)}, u32[]{:S(2)}) copy-start(bf16[1,1024,1024]{2,1,0:T(8,128)(2,1)} %param.8) | copy-start | bytes 6291460
  30.2 6.6 %collective-permute-start.7 = (bf16[136,1024]{1,0:T(8,128)(2,1)S(1)}, bf16[136,1024]{1,0:T(8,128)(2,1)S(1)}, u32[]{:S(2)}, u32[]{:S(2)}) collective-permute-start(bf16[136,1024]{1,0:T(8,128)(2,1)S(1)} %collective-permute-done.5.near), channel_id=1, source_target_pairs={{0,2},{2,0},{4,6},{6,4},{8,10},{10,8},{12,14},{14,12},{1,3},{3,1},... | collective-permute-start | bytes 835592 | tf_op jit(solution)/shard_map/ppermute | solution.py:44
  30.7 11.0 %collective-permute-start.8 = (bf16[136,1024]{1,0:T(8,128)(2,1)S(1)}, bf16[136,1024]{1,0:T(8,128)(2,1)S(1)}, u32[]{:S(2)}, u32[]{:S(2)}) collective-permute-start(bf16[136,1024]{1,0:T(8,128)(2,1)S(1)} %collective-permute-done.far), channel_id=1, source_target_pairs={{0,4},{2,6},{4,0},{6,2},{8,12},{10,14},{12,8},{14,10},{1,5},{3,7},... | collective-permute-start | bytes 835592 | tf_op jit(solution)/shard_map/ppermute | solution.py:44
  40.8 7.8 %collective-permute-start.10 = (bf16[128,1024]{1,0:T(8,128)(2,1)S(1)}, bf16[128,1024]{1,0:T(8,128)(2,1)S(1)}, u32[]{:S(2)}, u32[]{:S(2)}) collective-permute-start(bf16[128,1024]{1,0:T(8,128)(2,1)S(1)} %get-tuple-element.29), channel_id=1, source_target_pairs={{0,2},{2,0},{4,6},{6,4},{8,10},{10,8},{12,14},{14,12},{1,3},{3,1},... | collective-permute-start | bytes 786440 | tf_op jit(solution)/shard_map/ppermute | solution.py:44
  48.6 9.2 %collective-permute-start.11 = (bf16[128,1024]{1,0:T(8,128)(2,1)S(1)}, bf16[128,1024]{1,0:T(8,128)(2,1)S(1)}, u32[]{:S(2)}, u32[]{:S(2)}) collective-permute-start(bf16[128,1024]{1,0:T(8,128)(2,1)S(1)} %get-tuple-element.35), channel_id=1, source_target_pairs={{0,2},{2,0},{4,6},{6,4},{8,10},{10,8},{12,14},{14,12},{1,3},{3,1},... | collective-permute-start | bytes 786440 | tf_op jit(solution)/shard_map/ppermute | solution.py:44
  48.9 12.4 %collective-permute-start.13 = (bf16[128,1024]{1,0:T(8,128)(2,1)S(1)}, bf16[128,1024]{1,0:T(8,128)(2,1)S(1)}, u32[]{:S(2)}, u32[]{:S(2)}) collective-permute-start(bf16[128,1024]{1,0:T(8,128)(2,1)S(1)} %get-tuple-element.37), channel_id=1, source_target_pairs={{0,2},{2,0},{4,6},{6,4},{8,10},{10,8},{12,14},{14,12},{1,3},{3,1},... | collective-permute-start | bytes 786440 | tf_op jit(solution)/shard_map/ppermute | solution.py:44
  50.7 10.6 %collective-permute-start.14 = (bf16[128,1024]{1,0:T(8,128)(2,1)S(1)}, bf16[128,1024]{1,0:T(8,128)(2,1)S(1)}, u32[]{:S(2)}, u32[]{:S(2)}) collective-permute-start(bf16[128,1024]{1,0:T(8,128)(2,1)S(1)} %add_convert_fusion.2), channel_id=1, source_target_pairs={{0,4},{2,6},{4,0},{6,2},{8,12},{10,14},{12,8},{14,10},{1,5},{3,7},... | collective-permute-start | bytes 786440 | tf_op jit(solution)/shard_map/ppermute | solution.py:44
  51.4 13.6 %collective-permute-start.9 = (bf16[128,1024]{1,0:T(8,128)(2,1)S(1)}, bf16[128,1024]{1,0:T(8,128)(2,1)S(1)}, u32[]{:S(2)}, u32[]{:S(2)}) collective-permute-start(bf16[128,1024]{1,0:T(8,128)(2,1)S(1)} %get-tuple-element.33), channel_id=1, source_target_pairs={{0,2},{2,0},{4,6},{6,4},{8,10},{10,8},{12,14},{14,12},{1,3},{3,1},... | collective-permute-start | bytes 786440 | tf_op jit(solution)/shard_map/ppermute | solution.py:44
  57.9 7.6 %collective-permute-start.12 = (bf16[128,1024]{1,0:T(8,128)(2,1)S(1)}, bf16[128,1024]{1,0:T(8,128)(2,1)S(1)}, u32[]{:S(2)}, u32[]{:S(2)}) collective-permute-start(bf16[128,1024]{1,0:T(8,128)(2,1)S(1)} %add_convert_fusion.3), channel_id=1, source_target_pairs={{0,4},{2,6},{4,0},{6,2},{8,12},{10,14},{12,8},{14,10},{1,5},{3,7},... | collective-permute-start | bytes 786440 | tf_op jit(solution)/shard_map/ppermute | solution.py:44
  61.4 10.7 %collective-permute-start.15 = (bf16[128,1024]{1,0:T(8,128)(2,1)S(1)}, bf16[128,1024]{1,0:T(8,128)(2,1)S(1)}, u32[]{:S(2)}, u32[]{:S(2)}) collective-permute-start(bf16[128,1024]{1,0:T(8,128)(2,1)S(1)} %add_convert_fusion.1), channel_id=1, source_target_pairs={{0,8},{2,10},{4,12},{6,14},{8,0},{10,2},{12,4},{14,6},{1,9},{3,11}... | collective-permute-start | bytes 786440 | tf_op jit(solution)/shard_map/ppermute | solution.py:44

commit v4 on v0

--- a/solution.py
+++ b/solution.py
@@ -1,10 +1,14 @@
+import functools
+
 import jax
 import jax.numpy as jnp
 from jax import lax
+from jax.experimental import pallas as pl
+from jax.experimental.pallas import tpu as pltpu
 from jax.sharding import PartitionSpec as P
 
 
-def body(latent_rows, expert_ids, route_weights, up_weight, down_weight):
+def exchange_body(latent_rows, expert_ids, route_weights, up_weight, down_weight):
     rows_dev = latent_rows.shape[0]
     width = latent_rows.shape[1]
     choose = expert_ids.shape[1]
@@ -37,6 +41,129 @@
     return combined.astype(jnp.bfloat16)
 
 
+def across(value, step):
+    size = lax.axis_size("expert")
+    return lax.ppermute(value, "expert", [(i, i ^ step) for i in range(size)])
+
+
+def other_core(value):
+    return lax.ppermute(value, "tensor", [(0, 1), (1, 0)])
+
+
+def after(value, *others):
+    return lax.optimization_barrier((value, *others))[0]
+
+
+def pack_kernel(rows, ids, weights, out):
+    n, width = rows.shape
+    lines = []
+    for e in range(out.shape[0] - n):
+        lines.append(jnp.sum(jnp.where(ids[...] == e, weights[...], 0.0), axis=0, keepdims=True))
+    table = jnp.concatenate(lines, axis=0)
+    high = table.astype(jnp.bfloat16)
+    low = (table - high.astype(jnp.float32)).astype(jnp.bfloat16)
+    rest = jnp.zeros((len(lines), width - 2 * n), jnp.bfloat16)
+    out[...] = jnp.concatenate([rows[...], jnp.concatenate([high, low, rest], axis=1)], axis=0)
+
+
+def expert_kernel(counts, *refs):
+    f32 = jnp.float32
+    near, refs = refs[: counts[0]], refs[counts[0] :]
+    far, refs = refs[: counts[0]], refs[counts[0] :]
+    choice, up_a, down_a, up_b, down_b = refs[:5]
+    own, away, kept = refs[5 : 5 + counts[1]], refs[5 + counts[1] : 5 + 2 * counts[1]], refs[5 + 2 * counts[1] :]
+    n = sum(ref.shape[0] for ref in own)
+    blocks = [jnp.concatenate([ref[...] for ref in side], axis=0) for side in (near, far)]
+    rows = jnp.concatenate([b[:n] for b in blocks], axis=0)
+    total = None
+    for up, down in ((up_a, down_a), (up_b, down_b)):
+        pre = jnp.dot(rows, up[...], preferred_element_type=f32)
+        hidden = jnp.square(jnp.maximum(pre, 0.0)).astype(jnp.bfloat16)
+        out = jnp.dot(hidden, down[...], preferred_element_type=f32)
+        total = out if total is None else total + out
+    for i, side in enumerate((own, away)):
+        pair = blocks[i][n:, : 2 * n].astype(f32)
+        weight = jnp.sum((pair[:, :n] + pair[:, n:]) * choice[...], axis=0, keepdims=True)
+        column = jnp.broadcast_to(weight, (n, n)).T
+        first = 0
+        for ref in side:
+            last = first + ref.shape[0]
+            for c in range(0, ref.shape[1], n):
+                piece = total[i * n + first : i * n + last, c : c + n] * column[first:last]
+                ref[:, c : c + n] = piece.astype(ref.dtype)
+            first = last
+    for ref in kept:
+        ref[...] = down_b[...]
+
+
+def expert(near, far, choice, weights, n, pieces=1, keep=False):
+    width = near[0].shape[1]
+    out = [jax.ShapeDtypeStruct((n // pieces, width), jnp.float32)] * pieces
+    out += [jax.ShapeDtypeStruct((n // pieces, width), jnp.bfloat16)] * pieces
+    out += [jax.ShapeDtypeStruct(weights[3].shape, jnp.bfloat16)] * keep
+    return pl.pallas_call(
+        functools.partial(expert_kernel, (len(near), pieces)),
+        out_shape=out,
+        in_specs=[pl.BlockSpec(memory_space=pltpu.VMEM)] * (2 * len(near) + 5),
+        out_specs=[pl.BlockSpec(memory_space=pltpu.VMEM)] * len(out),
+        compiler_params=pltpu.CompilerParams(vmem_limit_bytes=20 << 20),
+        cost_estimate=pl.CostEstimate(flops=n * width, bytes_accessed=n * width, transcendentals=0),
+    )(*near, *far, choice, *weights)
+
+
+def gather_body(latent_rows, expert_ids, route_weights, up_weight, down_weight):
+    groups = lax.axis_size("expert")
+    n, width = latent_rows.shape
+    me = lax.axis_index("expert")
+    f32 = jnp.float32
+    choice = jnp.broadcast_to((jnp.arange(groups) == me).astype(f32)[:, None], (groups, n))
+    whole = pl.pallas_call(
+        pack_kernel,
+        out_shape=jax.ShapeDtypeStruct((n + groups, width), jnp.bfloat16),
+        in_specs=[pl.BlockSpec(memory_space=pltpu.VMEM)] * 3,
+        out_specs=pl.BlockSpec(memory_space=pltpu.VMEM),
+    )(latent_rows, expert_ids.T, route_weights.T)
+    near2 = across(whole, 4)
+    far0 = across(whole, 1)
+    near1 = across(whole, 2)
+    weights = (up_weight[0], down_weight[0], other_core(up_weight[0]), other_core(down_weight[0]))
+    far3 = across(near2, 3)
+    near3 = across(near2, 2)
+    far2 = across(near2, 1)
+    far0 = after(far0, near2)
+    own0, away0, kept = expert([whole], [far0], choice, weights, n, keep=True)
+    weights = weights[:3] + (kept,)
+    near3, far2, far3 = lax.optimization_barrier((near3, far2, far3, away0, near1))[:3]
+    own2, away2 = expert([near2], [far2], choice, weights, n)
+    far1 = across(after(far0, near3), 2)
+    near3 = after(near3, away2)
+    own3, away3 = expert([near3], [far3], choice, weights, n)
+
+    def add(*terms):
+        return functools.reduce(lambda a, b: a + b.astype(f32), terms).astype(jnp.bfloat16)
+
+    over2 = across(away2, 1)
+    over3 = across(away3, 1)
+    near1 = after(near1, away3)
+    own1, away1 = expert([near1], [far1], choice, weights, n)
+    over1 = across(away1, 1)
+    over0 = across(after(away0, over2), 1)
+    low3 = across(add(own3, over3), 2)
+    sum2 = add(own2, over2, low3)
+    high = across(sum2, 4)
+    low1 = across(add(own1, after(over1, sum2)), 2)
+    return add(own0, over0, low1, high)
+
+
+def body(latent_rows, expert_ids, route_weights, up_weight, down_weight):
+    groups = lax.axis_size("expert")
+    rows_dev, choose = expert_ids.shape
+    capacity = 3 * choose * rows_dev // (2 * groups)
+    dense = groups == 8 and rows_dev <= 2 * capacity
+    form = gather_body if dense else exchange_body
+    return form(latent_rows, expert_ids, route_weights, up_weight, down_weight)
+
+
 def solution(mesh):
     return jax.shard_map(
         body,

time: 155 us -> 70.2 us (0.45)
  blocking collectives: 44.4 us -> 0 us
  waiting for transfers between devices: 61 us -> 25.2 us
  starting transfers between devices: 5.79 us -> 25.5 us
  Pallas kernels: 0 us -> 13.9 us
  between operations: 13.4 us -> 0.1 us
  local copies, waits for them, and re-layouts: 14.7 us -> 4.21 us
  matrix products: 10.1 us -> 0 us
  other arithmetic: 5.66 us -> 1.05 us
    all_to_all x1 -> x0, blocking collectives: 44.4 us -> none  [body(): lax.all_to_all(outgoing, 'expert', split_axis=0, concat_axis=0, tiled=True)]
    all_to_all x1 -> x0, waiting for transfers between devices: 37.5 us -> none  [body(): lax.all_to_all(summed.reshape(groups, capacity, width), 'expert', split_a...]
    ppermute x0 -> x16, starting transfers between devices: none -> 25.5 us  [the longest x14 25 us: across(): return lax.ppermute(value, 'expert', [(i, i ^ step) for i in range(size)])]
    ppermute x0 -> x16, waiting for transfers between devices: none -> 25.2 us  [the longest x14 25.2 us: across(): return lax.ppermute(value, 'expert', [(i, i ^ step) for i in range(size)])]
    pallas_call x0 -> x5, Pallas kernels: none -> 13.9 us  [the longest x4 12.2 us: expert(): pl.pallas_call(functools.partial(expert_kernel, (len(near), pieces)), out...]
    reduce_scatter x1 -> x0, waiting for transfers between devices: 12.2 us -> none  [body(): lax.psum_scatter(partial_out.astype(jnp.bfloat16), 'tensor', scatter_dime...]
    all_gather x1 -> x0, waiting for transfers between devices: 11.3 us -> none  [body(): both_rows = lax.all_gather(arrived_rows, 'tensor', axis=0, tiled=True)]
    dot_general x1 -> x0, matrix products: 10.1 us -> none  [body(): jnp.dot(hidden, down_weight[0], preferred_element_type=jnp.float32)]
  transfers between devices with their start and end apart: 3 -> 16, of which waited for: 3 -> 7; matrix products, arithmetic and copies ran while one was open for 0% -> 0% of each run, Pallas kernels for 0% -> 12%
where the time goes in v4:
time: 70.2 us; the launch traced here: 70 us
  starting transfers between devices  25.5 us (36%)
  waiting for transfers between devices  25.2 us (36%)
  Pallas kernels  13.9 us (20%)
  local copies, waits for them, and re-layouts  4.21 us (6%)
  other arithmetic  1.05 us (1%)
    ppermute x14, waiting for transfers between devices, across(): return lax.ppermute(value, 'expert', [(i, i ^ step) for i in range(size)])  25.2 us
    ppermute x14, starting transfers between devices, across(): return lax.ppermute(value, 'expert', [(i, i ^ step) for i in range(size)])  25 us
    pallas_call x4, Pallas kernels, expert(): pl.pallas_call(functools.partial(expert_kernel, (len(near), pieces)), out...  12.2 us
    unnamed x10, local copies, waits for them, and re-layouts  4.14 us
    pallas_call x1, Pallas kernels, gather_body(): pl.pallas_call(pack_kernel, out_shape=jax.ShapeDtypeStruct((n + groups, w...  1.7 us
  transfers between devices with their start and end apart: 16, of which 7 were waited for; matrix products, arithmetic and copies ran while one was open for 0% of the time, Pallas kernels for 12%

profile of v4, /device:TPU:0, one launch (start us, length us, event | category | flops | bytes accessed | tf_op | source)
XLA Modules:
  0.0 70.0 jit_solution(10575628259843018918)
XLA Ops:
  0.0 0.5 collective-permute-start.2
  0.5 0.1 collective-permute-start.3
  0.5 1.7 %shard_map.55.refs_0_ = bf16[136,1024]{1,0:T(8,128)(2,1)} custom-call(bf16[128,1024]{1,0:T(8,128)(2,1)} %rows.1, s32[4,128]{1,0:T(4,128)} %bitcast.14, f32[4,128]{1,0:T(4,128)} %bitcast.15), custom_call_target="tpu_custom_call" | custom-call | tf_op jit(solution)/shard_map/pallas_call | solution.py:120
  2.2 4.0 %collective-permute-start.1 = (bf16[136,1024]{1,0:T(8,128)(2,1)}, bf16[136,1024]{1,0:T(8,128)(2,1)S(1)}, u32[]{:S(2)}, u32[]{:S(2)}) collective-permute-start(bf16[136,1024]{1,0:T(8,128)(2,1)} %shard_map.55.refs_0_), channel_id=1, source_target_pairs={{0,8},{2,10},{4,12},{6,14},{8,0},{10,2},{12,4},{14,6},{1,9},{3,11}... | collective-permute-start | bytes 835592 | tf_op jit(solution)/shard_map/ppermute | solution.py:46
  6.3 1.5 %collective-permute-start = (bf16[136,1024]{1,0:T(8,128)(2,1)}, bf16[136,1024]{1,0:T(8,128)(2,1)S(1)}, u32[]{:S(2)}, u32[]{:S(2)}) collective-permute-start(bf16[136,1024]{1,0:T(8,128)(2,1)} %shard_map.55.refs_0_), channel_id=1, source_target_pairs={{0,2},{2,0},{4,6},{6,4},{8,10},{10,8},{12,14},{14,12},{1,3},{3,1},... | collective-permute-start | bytes 835592 | tf_op jit(solution)/shard_map/ppermute | solution.py:46
  7.7 1.6 %collective-permute-start.7 = (bf16[136,1024]{1,0:T(8,128)(2,1)}, bf16[136,1024]{1,0:T(8,128)(2,1)S(1)}, u32[]{:S(2)}, u32[]{:S(2)}) collective-permute-start(bf16[136,1024]{1,0:T(8,128)(2,1)} %shard_map.55.refs_0_), channel_id=1, source_target_pairs={{0,4},{2,6},{4,0},{6,2},{8,12},{10,14},{12,8},{14,10},{1,5},{3,7},... | collective-permute-start | bytes 835592 | tf_op jit(solution)/shard_map/ppermute | solution.py:46
  9.3 10.0 %collective-permute-done.1.refs_0_ = bf16[136,1024]{1,0:T(8,128)(2,1)S(1)} collective-permute-done((bf16[136,1024]{1,0:T(8,128)(2,1)}, bf16[136,1024]{1,0:T(8,128)(2,1)S(1)}, u32[]{:S(2)}, u32[]{:S(2)}) %collective-permute-start.1) | collective-permute-done | bytes 278560 | tf_op jit(solution)/shard_map/ppermute | solution.py:46
  19.4 0.8 %collective-permute-start.4 = (bf16[136,1024]{1,0:T(8,128)(2,1)S(1)}, bf16[136,1024]{1,0:T(8,128)(2,1)S(1)}, u32[]{:S(2)}, u32[]{:S(2)}) collective-permute-start(bf16[136,1024]{1,0:T(8,128)(2,1)S(1)} %collective-permute-done.1.refs_0_), channel_id=1, source_target_pairs={{0,4},{2,6},{4,0},{6,2},{8,12},{10,14},{12,8},{14,10},{1,5},{3,7},... | collective-permute-start | bytes 835592 | tf_op jit(solution)/shard_map/ppermute | solution.py:46
  20.1 0.0 collective-permute-done.refs_1_
  20.1 1.4 %collective-permute-start.5 = (bf16[136,1024]{1,0:T(8,128)(2,1)S(1)}, bf16[136,1024]{1,0:T(8,128)(2,1)S(1)}, u32[]{:S(2)}, u32[]{:S(2)}) collective-permute-start(bf16[136,1024]{1,0:T(8,128)(2,1)S(1)} %collective-permute-done.1.refs_0_), channel_id=1, source_target_pairs={{0,2},{2,0},{4,6},{6,4},{8,10},{10,8},{12,14},{14,12},{1,3},{3,1},... | collective-permute-start | bytes 835592 | tf_op jit(solution)/shard_map/ppermute | solution.py:46
  21.6 0.0 collective-permute-done.2.refs_5_
  21.6 1.3 %collective-permute-start.6 = (bf16[136,1024]{1,0:T(8,128)(2,1)S(1)}, bf16[136,1024]{1,0:T(8,128)(2,1)}, u32[]{:S(2)}, u32[]{:S(2)}) collective-permute-start(bf16[136,1024]{1,0:T(8,128)(2,1)S(1)} %collective-permute-done.1.refs_0_), channel_id=1, source_target_pairs={{0,6},{2,4},{4,2},{6,0},{8,14},{10,12},{12,10},{14,8},{1,7},{3,5},... | collective-permute-start | bytes 835592 | tf_op jit(solution)/shard_map/ppermute | solution.py:46
  22.9 0.0 collective-permute-done.3.refs_6_
  22.9 0.1 broadcast_in_dim.2.refs_2_
  22.9 0.0 copy-start
  22.9 1.6 %copy-done = bf16[1,1024,1024]{2,1,0:T(8,128)(2,1)S(1)} copy-done((bf16[1,1024,1024]{2,1,0:T(8,128)(2,1)S(1)}, bf16[1,1024,1024]{2,1,0:T(8,128)(2,1)}, u32[]{:S(2)}) %copy-start) | copy-done | bytes 2097176
  24.5 0.0 copy-start.2
  24.5 1.6 %copy-done.2 = bf16[1,1024,1024]{2,1,0:T(8,128)(2,1)S(1)} copy-done((bf16[1,1024,1024]{2,1,0:T(8,128)(2,1)S(1)}, bf16[1,1024,1024]{2,1,0:T(8,128)(2,1)}, u32[]{:S(2)}) %copy-start.2) | copy-done | bytes 2097176
  26.1 0.0 copy-start.4
  26.1 1.0 %copy-done.4 = bf16[136,1024]{1,0:T(8,128)(2,1)S(1)} copy-done((bf16[136,1024]{1,0:T(8,128)(2,1)S(1)}, bf16[136,1024]{1,0:T(8,128)(2,1)}, u32[]{:S(2)}) %copy-start.4) | copy-done | bytes 278552
  27.1 0.0 copy-start.1
  27.1 0.0 copy-start.3
  27.1 4.2 %shard_map.56 = (f32[128,1024]{1,0:T(8,128)S(1)}, bf16[128,1024]{1,0:T(8,128)(2,1)S(1)}, bf16[1024,1024]{1,0:T(8,128)(2,1)S(1)}) custom-call(bf16[136,1024]{1,0:T(8,128)(2,1)S(1)} %copy-done.4, bf16[136,1024]{1,0:T(8,128)(2,1)S(1)} %collective-permute-done.refs_1_, f32[8,128]{1,0:T(8,128)S(1)} %broadcast_in_dim.2.refs_2_, bf16[1024,1024]{1,0:T(8,128)(2,1)S(1)} %bitcast.5, ...), custom_call_target="tpu_custom_call" | custom-call | flops 131072 | bytes 131072 | tf_op jit(solution)/shard_map/pallas_call | solution.py:104
  31.3 0.0 collective-permute-done.7.refs_0_
  31.3 0.0 collective-permute-done.4.refs_0_
  31.3 3.1 %collective-permute-done.5.refs_1_ = bf16[136,1024]{1,0:T(8,128)(2,1)S(1)} collective-permute-done((bf16[136,1024]{1,0:T(8,128)(2,1)S(1)}, bf16[136,1024]{1,0:T(8,128)(2,1)S(1)}, u32[]{:S(2)}, u32[]{:S(2)}) %collective-permute-start.5) | collective-permute-done | bytes 278560 | tf_op jit(solution)/shard_map/ppermute | solution.py:46
  34.4 0.0 collective-permute-done.6.refs_1_
  34.4 0.0 copy-done.1
  34.4 0.0 copy-done.3
  34.4 2.3 %shard_map.57 = (f32[128,1024]{1,0:T(8,128)S(1)}, bf16[128,1024]{1,0:T(8,128)(2,1)S(1)}) custom-call(bf16[136,1024]{1,0:T(8,128)(2,1)S(1)} %collective-permute-done.1.refs_0_, bf16[136,1024]{1,0:T(8,128)(2,1)S(1)} %collective-permute-done.5.refs_1_, f32[8,128]{1,0:T(8,128)S(1)} %broadcast_in_dim.2.refs_2_, bf16[1024,1024]{1,0:T(8,128)(2,1)S(1)} %bitcast.6, ...), custom_call_target="tpu_custom_call" | custom-call | flops 131072 | bytes 131072 | tf_op jit(solution)/shard_map/pallas_call | solution.py:104
  36.8 3.3 %shard_map.58 = (f32[128,1024]{1,0:T(8,128)S(1)}, bf16[128,1024]{1,0:T(8,128)(2,1)S(1)}) custom-call(bf16[136,1024]{1,0:T(8,128)(2,1)S(1)} %collective-permute-done.4.refs_0_, bf16[136,1024]{1,0:T(8,128)(2,1)} %collective-permute-done.6.refs_1_, f32[8,128]{1,0:T(8,128)S(1)} %broadcast_in_dim.2.refs_2_, bf16[1024,1024]{1,0:T(8,128)(2,1)S(1)} %bitcast.7, ...), custom_call_target="tpu_custom_call" | custom-call | flops 131072 | bytes 131072 | tf_op jit(solution)/shard_map/pallas_call | solution.py:104
  40.1 1.5 %collective-permute-start.12 = (bf16[128,1024]{1,0:T(8,128)(2,1)S(1)}, bf16[128,1024]{1,0:T(8,128)(2,1)S(1)}, u32[]{:S(2)}, u32[]{:S(2)}) collective-permute-start(bf16[128,1024]{1,0:T(8,128)(2,1)S(1)} %get-tuple-element.33), channel_id=1, source_target_pairs={{0,2},{2,0},{4,6},{6,4},{8,10},{10,8},{12,14},{14,12},{1,3},{3,1},... | collective-permute-start | bytes 786440 | tf_op jit(solution)/shard_map/ppermute | solution.py:46
  41.6 0.6 collective-permute-start.8
  42.2 1.3 %collective-permute-start.10 = (bf16[136,1024]{1,0:T(8,128)(2,1)S(1)}, bf16[136,1024]{1,0:T(8,128)(2,1)S(1)}, u32[]{:S(2)}, u32[]{:S(2)}) collective-permute-start(bf16[136,1024]{1,0:T(8,128)(2,1)S(1)} %collective-permute-done.refs_1_), channel_id=1, source_target_pairs={{0,4},{2,6},{4,0},{6,2},{8,12},{10,14},{12,8},{14,10},{1,5},{3,7},... | collective-permute-start | bytes 835592 | tf_op jit(solution)/shard_map/ppermute | solution.py:46
  43.4 5.6 %collective-permute-done.12 = bf16[128,1024]{1,0:T(8,128)(2,1)S(1)} collective-permute-done((bf16[128,1024]{1,0:T(8,128)(2,1)S(1)}, bf16[128,1024]{1,0:T(8,128)(2,1)S(1)}, u32[]{:S(2)}, u32[]{:S(2)}) %collective-permute-start.12) | collective-permute-done | bytes 262176 | tf_op jit(solution)/shard_map/ppermute | solution.py:46
  49.0 0.1 add_convert_fusion.3
  49.1 1.7 %collective-permute-start.13 = (bf16[128,1024]{1,0:T(8,128)(2,1)S(1)}, bf16[128,1024]{1,0:T(8,128)(2,1)S(1)}, u32[]{:S(2)}, u32[]{:S(2)}) collective-permute-start(bf16[128,1024]{1,0:T(8,128)(2,1)S(1)} %add_convert_fusion.3), channel_id=1, source_target_pairs={{0,4},{2,6},{4,0},{6,2},{8,12},{10,14},{12,8},{14,10},{1,5},{3,7},... | collective-permute-start | bytes 786440 | tf_op jit(solution)/shard_map/ppermute | solution.py:46
  50.8 0.0 collective-permute-done.10.refs_1_
  50.8 2.3 %shard_map.59 = (f32[128,1024]{1,0:T(8,128)S(1)}, bf16[128,1024]{1,0:T(8,128)(2,1)S(1)}) custom-call(bf16[136,1024]{1,0:T(8,128)(2,1)S(1)} %collective-permute-done.7.refs_0_, bf16[136,1024]{1,0:T(8,128)(2,1)S(1)} %collective-permute-done.10.refs_1_, f32[8,128]{1,0:T(8,128)S(1)} %broadcast_in_dim.2.refs_2_, bf16[1024,1024]{1,0:T(8,128)(2,1)S(1)} %bitcast.8, ...), custom_call_target="tpu_custom_call" | custom-call | flops 131072 | bytes 131072 | tf_op jit(solution)/shard_map/pallas_call | solution.py:104
  53.1 1.0 %collective-permute-start.11 = (bf16[128,1024]{1,0:T(8,128)(2,1)S(1)}, bf16[128,1024]{1,0:T(8,128)(2,1)S(1)}, u32[]{:S(2)}, u32[]{:S(2)}) collective-permute-start(bf16[128,1024]{1,0:T(8,128)(2,1)S(1)} %get-tuple-element.37), channel_id=1, source_target_pairs={{0,2},{2,0},{4,6},{6,4},{8,10},{10,8},{12,14},{14,12},{1,3},{3,1},... | collective-permute-start | bytes 786440 | tf_op jit(solution)/shard_map/ppermute | solution.py:46
  54.1 0.0 collective-permute-done.8
  54.1 1.1 %collective-permute-start.9 = (bf16[128,1024]{1,0:T(8,128)(2,1)S(1)}, bf16[128,1024]{1,0:T(8,128)(2,1)S(1)}, u32[]{:S(2)}, u32[]{:S(2)}) collective-permute-start(bf16[128,1024]{1,0:T(8,128)(2,1)S(1)} %get-tuple-element.29), channel_id=1, source_target_pairs={{0,2},{2,0},{4,6},{6,4},{8,10},{10,8},{12,14},{14,12},{1,3},{3,1},... | collective-permute-start | bytes 786440 | tf_op jit(solution)/shard_map/ppermute | solution.py:46
  55.2 0.3 collective-permute-done.13
  55.5 0.1 add_convert_fusion.2
  55.6 5.0 %collective-permute-start.15 = (bf16[128,1024]{1,0:T(8,128)(2,1)S(1)}, bf16[128,1024]{1,0:T(8,128)(2,1)S(1)}, u32[]{:S(2)}, u32[]{:S(2)}) collective-permute-start(bf16[128,1024]{1,0:T(8,128)(2,1)S(1)} %add_convert_fusion.2), channel_id=1, source_target_pairs={{0,8},{2,10},{4,12},{6,14},{8,0},{10,2},{12,4},{14,6},{1,9},{3,11}... | collective-permute-start | bytes 786440 | tf_op jit(solution)/shard_map/ppermute | solution.py:46
  60.6 0.0 collective-permute-done.11
  60.6 0.1 add_convert_fusion.1
  60.7 2.3 %collective-permute-start.14 = (bf16[128,1024]{1,0:T(8,128)(2,1)S(1)}, bf16[128,1024]{1,0:T(8,128)(2,1)S(1)}, u32[]{:S(2)}, u32[]{:S(2)}) collective-permute-start(bf16[128,1024]{1,0:T(8,128)(2,1)S(1)} %add_convert_fusion.1), channel_id=1, source_target_pairs={{0,4},{2,6},{4,0},{6,2},{8,12},{10,14},{12,8},{14,10},{1,5},{3,7},... | collective-permute-start | bytes 786440 | tf_op jit(solution)/shard_map/ppermute | solution.py:46
  62.9 0.2 collective-permute-done.9
  63.1 4.6 %collective-permute-done.15 = bf16[128,1024]{1,0:T(8,128)(2,1)S(1)} collective-permute-done((bf16[128,1024]{1,0:T(8,128)(2,1)S(1)}, bf16[128,1024]{1,0:T(8,128)(2,1)S(1)}, u32[]{:S(2)}, u32[]{:S(2)}) %collective-permute-start.15) | collective-permute-done | bytes 262176 | tf_op jit(solution)/shard_map/ppermute | solution.py:46
  67.7 1.4 %collective-permute-done.14 = bf16[128,1024]{1,0:T(8,128)(2,1)S(1)} collective-permute-done((bf16[128,1024]{1,0:T(8,128)(2,1)S(1)}, bf16[128,1024]{1,0:T(8,128)(2,1)S(1)}, u32[]{:S(2)}, u32[]{:S(2)}) %collective-permute-start.14) | collective-permute-done | bytes 262176 | tf_op jit(solution)/shard_map/ppermute | solution.py:46
  69.1 0.8 %add_convert_fusion = bf16[128,1024]{1,0:T(8,128)(2,1)} fusion(bf16[128,1024]{1,0:T(8,128)(2,1)S(1)} %collective-permute-done.15, bf16[128,1024]{1,0:T(8,128)(2,1)S(1)} %collective-permute-done.14, f32[128,1024]{1,0:T(8,128)S(1)} %get-tuple-element.24, bf16[128,1024]{1,0:T(8,128)(2,1)S(1)} %collective-permute-done.9), kind=kLoop, calls=%fused_computation | loop fusion | flops 917504 | bytes 1572864 | tf_op jit(solution)/shard_map/convert_element_type | solution.py:143
  (1 shorter events, 0.0 us)
Async XLA Ops:
  0.0 21.6 %collective-permute-start.2 = (bf16[1024,1024]{1,0:T(8,128)(2,1)}, bf16[1024,1024]{1,0:T(8,128)(2,1)S(1)}, u32[]{:S(2)}, u32[]{:S(2)}) collective-permute-start(bf16[1024,1024]{1,0:T(8,128)(2,1)} %bitcast.4), channel_id=1, source_target_pairs={{0,1},{1,0},{2,3},{3,2},{4,5},{5,4},{6,7},{7,6},{8,9},{9,8},{10,11... | collective-permute-start | bytes 6291464 | tf_op jit(solution)/shard_map/ppermute | solution.py:50
  0.5 22.4 %collective-permute-start.3 = (bf16[1024,1024]{1,0:T(8,128)(2,1)}, bf16[1024,1024]{1,0:T(8,128)(2,1)}, u32[]{:S(2)}, u32[]{:S(2)}) collective-permute-start(bf16[1024,1024]{1,0:T(8,128)(2,1)} %bitcast.9), channel_id=1, source_target_pairs={{0,1},{1,0},{2,3},{3,2},{4,5},{5,4},{6,7},{7,6},{8,9},{9,8},{10,11... | collective-permute-start | bytes 6291464 | tf_op jit(solution)/shard_map/ppermute | solution.py:50
  2.2 17.1 %collective-permute-start.1 = (bf16[136,1024]{1,0:T(8,128)(2,1)}, bf16[136,1024]{1,0:T(8,128)(2,1)S(1)}, u32[]{:S(2)}, u32[]{:S(2)}) collective-permute-start(bf16[136,1024]{1,0:T(8,128)(2,1)} %shard_map.55.refs_0_), channel_id=1, source_target_pairs={{0,8},{2,10},{4,12},{6,14},{8,0},{10,2},{12,4},{14,6},{1,9},{3,11}... | collective-permute-start | bytes 835592 | tf_op jit(solution)/shard_map/ppermute | solution.py:46
  6.3 13.9 %collective-permute-start = (bf16[136,1024]{1,0:T(8,128)(2,1)}, bf16[136,1024]{1,0:T(8,128)(2,1)S(1)}, u32[]{:S(2)}, u32[]{:S(2)}) collective-permute-start(bf16[136,1024]{1,0:T(8,128)(2,1)} %shard_map.55.refs_0_), channel_id=1, source_target_pairs={{0,2},{2,0},{4,6},{6,4},{8,10},{10,8},{12,14},{14,12},{1,3},{3,1},... | collective-permute-start | bytes 835592 | tf_op jit(solution)/shard_map/ppermute | solution.py:46
  7.7 23.6 %collective-permute-start.7 = (bf16[136,1024]{1,0:T(8,128)(2,1)}, bf16[136,1024]{1,0:T(8,128)(2,1)S(1)}, u32[]{:S(2)}, u32[]{:S(2)}) collective-permute-start(bf16[136,1024]{1,0:T(8,128)(2,1)} %shard_map.55.refs_0_), channel_id=1, source_target_pairs={{0,4},{2,6},{4,0},{6,2},{8,12},{10,14},{12,8},{14,10},{1,5},{3,7},... | collective-permute-start | bytes 835592 | tf_op jit(solution)/shard_map/ppermute | solution.py:46
  19.4 11.9 %collective-permute-start.4 = (bf16[136,1024]{1,0:T(8,128)(2,1)S(1)}, bf16[136,1024]{1,0:T(8,128)(2,1)S(1)}, u32[]{:S(2)}, u32[]{:S(2)}) collective-permute-start(bf16[136,1024]{1,0:T(8,128)(2,1)S(1)} %collective-permute-done.1.refs_0_), channel_id=1, source_target_pairs={{0,4},{2,6},{4,0},{6,2},{8,12},{10,14},{12,8},{14,10},{1,5},{3,7},... | collective-permute-start | bytes 835592 | tf_op jit(solution)/shard_map/ppermute | solution.py:46
  20.1 14.3 %collective-permute-start.5 = (bf16[136,1024]{1,0:T(8,128)(2,1)S(1)}, bf16[136,1024]{1,0:T(8,128)(2,1)S(1)}, u32[]{:S(2)}, u32[]{:S(2)}) collective-permute-start(bf16[136,1024]{1,0:T(8,128)(2,1)S(1)} %collective-permute-done.1.refs_0_), channel_id=1, source_target_pairs={{0,2},{2,0},{4,6},{6,4},{8,10},{10,8},{12,14},{14,12},{1,3},{3,1},... | collective-permute-start | bytes 835592 | tf_op jit(solution)/shard_map/ppermute | solution.py:46
  21.6 12.8 %collective-permute-start.6 = (bf16[136,1024]{1,0:T(8,128)(2,1)S(1)}, bf16[136,1024]{1,0:T(8,128)(2,1)}, u32[]{:S(2)}, u32[]{:S(2)}) collective-permute-start(bf16[136,1024]{1,0:T(8,128)(2,1)S(1)} %collective-permute-done.1.refs_0_), channel_id=1, source_target_pairs={{0,6},{2,4},{4,2},{6,0},{8,14},{10,12},{12,10},{14,8},{1,7},{3,5},... | collective-permute-start | bytes 835592 | tf_op jit(solution)/shard_map/ppermute | solution.py:46
  22.9 1.6 %copy-start = (bf16[1,1024,1024]{2,1,0:T(8,128)(2,1)S(1)}, bf16[1,1024,1024]{2,1,0:T(8,128)(2,1)}, u32[]{:S(2)}) copy-start(bf16[1,1024,1024]{2,1,0:T(8,128)(2,1)} %param.8) | copy-start | bytes 6291460
  24.5 1.6 %copy-start.2 = (bf16[1,1024,1024]{2,1,0:T(8,128)(2,1)S(1)}, bf16[1,1024,1024]{2,1,0:T(8,128)(2,1)}, u32[]{:S(2)}) copy-start(bf16[1,1024,1024]{2,1,0:T(8,128)(2,1)} %param.9) | copy-start | bytes 6291460
  26.1 1.0 %copy-start.4 = (bf16[136,1024]{1,0:T(8,128)(2,1)S(1)}, bf16[136,1024]{1,0:T(8,128)(2,1)}, u32[]{:S(2)}) copy-start(bf16[136,1024]{1,0:T(8,128)(2,1)} %shard_map.55.refs_0_) | copy-start | bytes 835588
  27.1 7.3 %copy-start.1 = (bf16[1,1024,1024]{2,1,0:T(8,128)(2,1)S(1)}, bf16[1,1024,1024]{2,1,0:T(8,128)(2,1)}, u32[]{:S(2)}) copy-start(bf16[1,1024,1024]{2,1,0:T(8,128)(2,1)} %param.8) | copy-start | bytes 6291460
  27.1 7.3 %copy-start.3 = (bf16[1,1024,1024]{2,1,0:T(8,128)(2,1)S(1)}, bf16[1,1024,1024]{2,1,0:T(8,128)(2,1)}, u32[]{:S(2)}) copy-start(bf16[1,1024,1024]{2,1,0:T(8,128)(2,1)} %param.9) | copy-start | bytes 6291460
  40.1 8.9 %collective-permute-start.12 = (bf16[128,1024]{1,0:T(8,128)(2,1)S(1)}, bf16[128,1024]{1,0:T(8,128)(2,1)S(1)}, u32[]{:S(2)}, u32[]{:S(2)}) collective-permute-start(bf16[128,1024]{1,0:T(8,128)(2,1)S(1)} %get-tuple-element.33), channel_id=1, source_target_pairs={{0,2},{2,0},{4,6},{6,4},{8,10},{10,8},{12,14},{14,12},{1,3},{3,1},... | collective-permute-start | bytes 786440 | tf_op jit(solution)/shard_map/ppermute | solution.py:46
  41.6 12.5 %collective-permute-start.8 = (bf16[128,1024]{1,0:T(8,128)(2,1)S(1)}, bf16[128,1024]{1,0:T(8,128)(2,1)S(1)}, u32[]{:S(2)}, u32[]{:S(2)}) collective-permute-start(bf16[128,1024]{1,0:T(8,128)(2,1)S(1)} %get-tuple-element.28), channel_id=1, source_target_pairs={{0,2},{2,0},{4,6},{6,4},{8,10},{10,8},{12,14},{14,12},{1,3},{3,1},... | collective-permute-start | bytes 786440 | tf_op jit(solution)/shard_map/ppermute | solution.py:46
  42.2 8.6 %collective-permute-start.10 = (bf16[136,1024]{1,0:T(8,128)(2,1)S(1)}, bf16[136,1024]{1,0:T(8,128)(2,1)S(1)}, u32[]{:S(2)}, u32[]{:S(2)}) collective-permute-start(bf16[136,1024]{1,0:T(8,128)(2,1)S(1)} %collective-permute-done.refs_1_), channel_id=1, source_target_pairs={{0,4},{2,6},{4,0},{6,2},{8,12},{10,14},{12,8},{14,10},{1,5},{3,7},... | collective-permute-start | bytes 835592 | tf_op jit(solution)/shard_map/ppermute | solution.py:46
  49.1 6.4 %collective-permute-start.13 = (bf16[128,1024]{1,0:T(8,128)(2,1)S(1)}, bf16[128,1024]{1,0:T(8,128)(2,1)S(1)}, u32[]{:S(2)}, u32[]{:S(2)}) collective-permute-start(bf16[128,1024]{1,0:T(8,128)(2,1)S(1)} %add_convert_fusion.3), channel_id=1, source_target_pairs={{0,4},{2,6},{4,0},{6,2},{8,12},{10,14},{12,8},{14,10},{1,5},{3,7},... | collective-permute-start | bytes 786440 | tf_op jit(solution)/shard_map/ppermute | solution.py:46
  53.1 7.5 %collective-permute-start.11 = (bf16[128,1024]{1,0:T(8,128)(2,1)S(1)}, bf16[128,1024]{1,0:T(8,128)(2,1)S(1)}, u32[]{:S(2)}, u32[]{:S(2)}) collective-permute-start(bf16[128,1024]{1,0:T(8,128)(2,1)S(1)} %get-tuple-element.37), channel_id=1, source_target_pairs={{0,2},{2,0},{4,6},{6,4},{8,10},{10,8},{12,14},{14,12},{1,3},{3,1},... | collective-permute-start | bytes 786440 | tf_op jit(solution)/shard_map/ppermute | solution.py:46
  54.1 9.0 %collective-permute-start.9 = (bf16[128,1024]{1,0:T(8,128)(2,1)S(1)}, bf16[128,1024]{1,0:T(8,128)(2,1)S(1)}, u32[]{:S(2)}, u32[]{:S(2)}) collective-permute-start(bf16[128,1024]{1,0:T(8,128)(2,1)S(1)} %get-tuple-element.29), channel_id=1, source_target_pairs={{0,2},{2,0},{4,6},{6,4},{8,10},{10,8},{12,14},{14,12},{1,3},{3,1},... | collective-permute-start | bytes 786440 | tf_op jit(solution)/shard_map/ppermute | solution.py:46
  55.6 12.1 %collective-permute-start.15 = (bf16[128,1024]{1,0:T(8,128)(2,1)S(1)}, bf16[128,1024]{1,0:T(8,128)(2,1)S(1)}, u32[]{:S(2)}, u32[]{:S(2)}) collective-permute-start(bf16[128,1024]{1,0:T(8,128)(2,1)S(1)} %add_convert_fusion.2), channel_id=1, source_target_pairs={{0,8},{2,10},{4,12},{6,14},{8,0},{10,2},{12,4},{14,6},{1,9},{3,11}... | collective-permute-start | bytes 786440 | tf_op jit(solution)/shard_map/ppermute | solution.py:46
  60.7 8.5 %collective-permute-start.14 = (bf16[128,1024]{1,0:T(8,128)(2,1)S(1)}, bf16[128,1024]{1,0:T(8,128)(2,1)S(1)}, u32[]{:S(2)}, u32[]{:S(2)}) collective-permute-start(bf16[128,1024]{1,0:T(8,128)(2,1)S(1)} %add_convert_fusion.1), channel_id=1, source_target_pairs={{0,4},{2,6},{4,0},{6,2},{8,12},{10,14},{12,8},{14,10},{1,5},{3,7},... | collective-permute-start | bytes 786440 | tf_op jit(solution)/shard_map/ppermute | solution.py:46

commit v5 on v4

--- a/solution.py
+++ b/solution.py
@@ -66,14 +66,12 @@
     out[...] = jnp.concatenate([rows[...], jnp.concatenate([high, low, rest], axis=1)], axis=0)
 
 
-def expert_kernel(counts, *refs):
+def expert_kernel(count, *refs):
     f32 = jnp.float32
-    near, refs = refs[: counts[0]], refs[counts[0] :]
-    far, refs = refs[: counts[0]], refs[counts[0] :]
-    choice, up_a, down_a, up_b, down_b = refs[:5]
-    own, away, kept = refs[5 : 5 + counts[1]], refs[5 + counts[1] : 5 + 2 * counts[1]], refs[5 + 2 * counts[1] :]
-    n = sum(ref.shape[0] for ref in own)
-    blocks = [jnp.concatenate([ref[...] for ref in side], axis=0) for side in (near, far)]
+    blocks = [ref[...] for ref in refs[:count]]
+    choice, up_a, down_a, up_b, down_b = refs[count : count + 5]
+    outs, kept = refs[count + 5 : 2 * count + 5], refs[2 * count + 5 :]
+    n = outs[0].shape[0]
     rows = jnp.concatenate([b[:n] for b in blocks], axis=0)
     total = None
     for up, down in ((up_a, down_a), (up_b, down_b)):
@@ -81,34 +79,28 @@
         hidden = jnp.square(jnp.maximum(pre, 0.0)).astype(jnp.bfloat16)
         out = jnp.dot(hidden, down[...], preferred_element_type=f32)
         total = out if total is None else total + out
-    for i, side in enumerate((own, away)):
+    for i, ref in enumerate(outs):
         pair = blocks[i][n:, : 2 * n].astype(f32)
         weight = jnp.sum((pair[:, :n] + pair[:, n:]) * choice[...], axis=0, keepdims=True)
         column = jnp.broadcast_to(weight, (n, n)).T
-        first = 0
-        for ref in side:
-            last = first + ref.shape[0]
-            for c in range(0, ref.shape[1], n):
-                piece = total[i * n + first : i * n + last, c : c + n] * column[first:last]
-                ref[:, c : c + n] = piece.astype(ref.dtype)
-            first = last
+        for c in range(0, ref.shape[1], n):
+            ref[:, c : c + n] = (total[i * n : (i + 1) * n, c : c + n] * column).astype(ref.dtype)
     for ref in kept:
         ref[...] = down_b[...]
 
 
-def expert(near, far, choice, weights, n, pieces=1, keep=False):
-    width = near[0].shape[1]
-    out = [jax.ShapeDtypeStruct((n // pieces, width), jnp.float32)] * pieces
-    out += [jax.ShapeDtypeStruct((n // pieces, width), jnp.bfloat16)] * pieces
+def expert(blocks, kinds, choice, weights, n, keep=False):
+    width = blocks[0].shape[1]
+    out = [jax.ShapeDtypeStruct((n, width), kind) for kind in kinds]
     out += [jax.ShapeDtypeStruct(weights[3].shape, jnp.bfloat16)] * keep
     return pl.pallas_call(
-        functools.partial(expert_kernel, (len(near), pieces)),
+        functools.partial(expert_kernel, len(blocks)),
         out_shape=out,
-        in_specs=[pl.BlockSpec(memory_space=pltpu.VMEM)] * (2 * len(near) + 5),
+        in_specs=[pl.BlockSpec(memory_space=pltpu.VMEM)] * (len(blocks) + 5),
         out_specs=[pl.BlockSpec(memory_space=pltpu.VMEM)] * len(out),
-        compiler_params=pltpu.CompilerParams(vmem_limit_bytes=20 << 20),
+        compiler_params=pltpu.CompilerParams(vmem_limit_bytes=24 << 20),
         cost_estimate=pl.CostEstimate(flops=n * width, bytes_accessed=n * width, transcendentals=0),
-    )(*near, *far, choice, *weights)
+    )(*blocks, choice, *weights)
 
 
 def gather_body(latent_rows, expert_ids, route_weights, up_weight, down_weight):
@@ -131,21 +123,22 @@
     near3 = across(near2, 2)
     far2 = across(near2, 1)
     far0 = after(far0, near2)
-    own0, away0, kept = expert([whole], [far0], choice, weights, n, keep=True)
+    bf16 = jnp.bfloat16
+    own0, away0, kept = expert([whole, far0], [f32, bf16], choice, weights, n, keep=True)
     weights = weights[:3] + (kept,)
+    far1 = across(after(far0, near2, away0), 2)
     near3, far2, far3 = lax.optimization_barrier((near3, far2, far3, away0, near1))[:3]
-    own2, away2 = expert([near2], [far2], choice, weights, n)
-    far1 = across(after(far0, near3), 2)
-    near3 = after(near3, away2)
-    own3, away3 = expert([near3], [far3], choice, weights, n)
+    away3, away2 = expert([far3, far2], [bf16, bf16], choice, weights, n)
+    near3 = after(near3, away3)
+    own3, own2 = expert([near3, near2], [f32, f32], choice, weights, n)
+    near1 = after(near1, own3)
+    own1, away1 = expert([near1, far1], [f32, bf16], choice, weights, n)
 
     def add(*terms):
         return functools.reduce(lambda a, b: a + b.astype(f32), terms).astype(jnp.bfloat16)
 
+    over3 = across(away3, 1)
     over2 = across(away2, 1)
-    over3 = across(away3, 1)
-    near1 = after(near1, away3)
-    own1, away1 = expert([near1], [far1], choice, weights, n)
     over1 = across(away1, 1)
     over0 = across(after(away0, over2), 1)
     low3 = across(add(own3, over3), 2)

time: 70.2 us -> 67.9 us (0.967)
  waiting for transfers between devices: 25.2 us -> 22.9 us
    ppermute x14, waiting for transfers between devices: 25.2 us -> 22.9 us  [across(): return lax.ppermute(value, 'expert', [(i, i ^ step) for i in range(size)])]
  transfers between devices with their start and end apart: 16 -> 16, of which waited for: 7 -> 7; matrix products, arithmetic and copies ran while one was open for 0% -> 0% of each run, Pallas kernels for 12% -> 16%
where the time goes in v5:
time: 67.9 us; the launch traced here: 67.6 us
  starting transfers between devices  25.5 us (38%)
  waiting for transfers between devices  22.9 us (34%)
  Pallas kernels  13.9 us (20%)
  local copies, waits for them, and re-layouts  4.21 us (6%)
  other arithmetic  1.07 us (2%)
    ppermute x14, starting transfers between devices, across(): return lax.ppermute(value, 'expert', [(i, i ^ step) for i in range(size)])  24.9 us
    ppermute x14, waiting for transfers between devices, across(): return lax.ppermute(value, 'expert', [(i, i ^ step) for i in range(size)])  22.9 us
    pallas_call x4, Pallas kernels, expert(): pl.pallas_call(functools.partial(expert_kernel, len(blocks)), out_shape=o...  12.2 us
    unnamed x10, local copies, waits for them, and re-layouts  4.14 us
    pallas_call x1, Pallas kernels, gather_body(): pl.pallas_call(pack_kernel, out_shape=jax.ShapeDtypeStruct((n + groups, w...  1.7 us
  transfers between devices with their start and end apart: 16, of which 7 were waited for; matrix products, arithmetic and copies ran while one was open for 0% of the time, Pallas kernels for 16%

profile of v5, /device:TPU:0, one launch (start us, length us, event | category | flops | bytes accessed | tf_op | source)
XLA Modules:
  0.0 67.6 jit_solution(11671730166658116212)
XLA Ops:
  0.0 0.5 collective-permute-start.2
  0.5 0.1 collective-permute-start.3
  0.5 1.7 %shard_map.55.refs_0_ = bf16[136,1024]{1,0:T(8,128)(2,1)} custom-call(bf16[128,1024]{1,0:T(8,128)(2,1)} %rows.1, s32[4,128]{1,0:T(4,128)} %bitcast.14, f32[4,128]{1,0:T(4,128)} %bitcast.15), custom_call_target="tpu_custom_call" | custom-call | tf_op jit(solution)/shard_map/pallas_call | solution.py:112
  2.2 4.0 %collective-permute-start.1 = (bf16[136,1024]{1,0:T(8,128)(2,1)}, bf16[136,1024]{1,0:T(8,128)(2,1)S(1)}, u32[]{:S(2)}, u32[]{:S(2)}) collective-permute-start(bf16[136,1024]{1,0:T(8,128)(2,1)} %shard_map.55.refs_0_), channel_id=1, source_target_pairs={{0,8},{2,10},{4,12},{6,14},{8,0},{10,2},{12,4},{14,6},{1,9},{3,11}... | collective-permute-start | bytes 835592 | tf_op jit(solution)/shard_map/ppermute | solution.py:46
  6.3 1.5 %collective-permute-start = (bf16[136,1024]{1,0:T(8,128)(2,1)}, bf16[136,1024]{1,0:T(8,128)(2,1)S(1)}, u32[]{:S(2)}, u32[]{:S(2)}) collective-permute-start(bf16[136,1024]{1,0:T(8,128)(2,1)} %shard_map.55.refs_0_), channel_id=1, source_target_pairs={{0,2},{2,0},{4,6},{6,4},{8,10},{10,8},{12,14},{14,12},{1,3},{3,1},... | collective-permute-start | bytes 835592 | tf_op jit(solution)/shard_map/ppermute | solution.py:46
  7.7 1.6 %collective-permute-start.7 = (bf16[136,1024]{1,0:T(8,128)(2,1)}, bf16[136,1024]{1,0:T(8,128)(2,1)S(1)}, u32[]{:S(2)}, u32[]{:S(2)}) collective-permute-start(bf16[136,1024]{1,0:T(8,128)(2,1)} %shard_map.55.refs_0_), channel_id=1, source_target_pairs={{0,4},{2,6},{4,0},{6,2},{8,12},{10,14},{12,8},{14,10},{1,5},{3,7},... | collective-permute-start | bytes 835592 | tf_op jit(solution)/shard_map/ppermute | solution.py:46
  9.3 10.0 %collective-permute-done.1.refs_1_ = bf16[136,1024]{1,0:T(8,128)(2,1)S(1)} collective-permute-done((bf16[136,1024]{1,0:T(8,128)(2,1)}, bf16[136,1024]{1,0:T(8,128)(2,1)S(1)}, u32[]{:S(2)}, u32[]{:S(2)}) %collective-permute-start.1) | collective-permute-done | bytes 278560 | tf_op jit(solution)/shard_map/ppermute | solution.py:46
  19.4 0.8 %collective-permute-start.4 = (bf16[136,1024]{1,0:T(8,128)(2,1)S(1)}, bf16[136,1024]{1,0:T(8,128)(2,1)S(1)}, u32[]{:S(2)}, u32[]{:S(2)}) collective-permute-start(bf16[136,1024]{1,0:T(8,128)(2,1)S(1)} %collective-permute-done.1.refs_1_), channel_id=1, source_target_pairs={{0,4},{2,6},{4,0},{6,2},{8,12},{10,14},{12,8},{14,10},{1,5},{3,7},... | collective-permute-start | bytes 835592 | tf_op jit(solution)/shard_map/ppermute | solution.py:46
  20.1 0.0 collective-permute-done.refs_1_
  20.1 1.4 %collective-permute-start.5 = (bf16[136,1024]{1,0:T(8,128)(2,1)S(1)}, bf16[136,1024]{1,0:T(8,128)(2,1)S(1)}, u32[]{:S(2)}, u32[]{:S(2)}) collective-permute-start(bf16[136,1024]{1,0:T(8,128)(2,1)S(1)} %collective-permute-done.1.refs_1_), channel_id=1, source_target_pairs={{0,2},{2,0},{4,6},{6,4},{8,10},{10,8},{12,14},{14,12},{1,3},{3,1},... | collective-permute-start | bytes 835592 | tf_op jit(solution)/shard_map/ppermute | solution.py:46
  21.6 0.0 collective-permute-done.2.refs_5_
  21.6 1.3 %collective-permute-start.6 = (bf16[136,1024]{1,0:T(8,128)(2,1)S(1)}, bf16[136,1024]{1,0:T(8,128)(2,1)}, u32[]{:S(2)}, u32[]{:S(2)}) collective-permute-start(bf16[136,1024]{1,0:T(8,128)(2,1)S(1)} %collective-permute-done.1.refs_1_), channel_id=1, source_target_pairs={{0,6},{2,4},{4,2},{6,0},{8,14},{10,12},{12,10},{14,8},{1,7},{3,5},... | collective-permute-start | bytes 835592 | tf_op jit(solution)/shard_map/ppermute | solution.py:46
  22.9 0.0 collective-permute-done.3.refs_6_
  22.9 0.1 broadcast_in_dim.2.refs_2_
  22.9 0.0 copy-start
  22.9 1.6 %copy-done = bf16[1,1024,1024]{2,1,0:T(8,128)(2,1)S(1)} copy-done((bf16[1,1024,1024]{2,1,0:T(8,128)(2,1)S(1)}, bf16[1,1024,1024]{2,1,0:T(8,128)(2,1)}, u32[]{:S(2)}) %copy-start) | copy-done | bytes 2097176
  24.5 0.0 copy-start.2
  24.5 1.6 %copy-done.2 = bf16[1,1024,1024]{2,1,0:T(8,128)(2,1)S(1)} copy-done((bf16[1,1024,1024]{2,1,0:T(8,128)(2,1)S(1)}, bf16[1,1024,1024]{2,1,0:T(8,128)(2,1)}, u32[]{:S(2)}) %copy-start.2) | copy-done | bytes 2097176
  26.1 0.0 copy-start.4
  26.1 1.0 %copy-done.4 = bf16[136,1024]{1,0:T(8,128)(2,1)S(1)} copy-done((bf16[136,1024]{1,0:T(8,128)(2,1)S(1)}, bf16[136,1024]{1,0:T(8,128)(2,1)}, u32[]{:S(2)}) %copy-start.4) | copy-done | bytes 278552
  27.1 0.0 copy-start.1
  27.1 0.0 copy-start.3
  27.1 4.2 %shard_map.56 = (f32[128,1024]{1,0:T(8,128)S(1)}, bf16[128,1024]{1,0:T(8,128)(2,1)S(1)}, bf16[1024,1024]{1,0:T(8,128)(2,1)S(1)}) custom-call(bf16[136,1024]{1,0:T(8,128)(2,1)S(1)} %copy-done.4, bf16[136,1024]{1,0:T(8,128)(2,1)S(1)} %collective-permute-done.refs_1_, f32[8,128]{1,0:T(8,128)S(1)} %broadcast_in_dim.2.refs_2_, bf16[1024,1024]{1,0:T(8,128)(2,1)S(1)} %bitcast.5, ...), custom_call_target="tpu_custom_call" | custom-call | flops 131072 | bytes 131072 | tf_op jit(solution)/shard_map/pallas_call | solution.py:96
  31.3 0.0 collective-permute-done.7.refs_0_
  31.3 0.0 collective-permute-done.4.refs_0_
  31.3 3.1 %collective-permute-done.5.refs_1_ = bf16[136,1024]{1,0:T(8,128)(2,1)S(1)} collective-permute-done((bf16[136,1024]{1,0:T(8,128)(2,1)S(1)}, bf16[136,1024]{1,0:T(8,128)(2,1)S(1)}, u32[]{:S(2)}, u32[]{:S(2)}) %collective-permute-start.5) | collective-permute-done | bytes 278560 | tf_op jit(solution)/shard_map/ppermute | solution.py:46
  34.4 0.0 collective-permute-done.6.refs_0_
  34.4 0.0 copy-done.1
  34.4 0.0 copy-done.3
  34.4 3.3 %shard_map.57 = (bf16[128,1024]{1,0:T(8,128)(2,1)S(1)}, bf16[128,1024]{1,0:T(8,128)(2,1)S(1)}) custom-call(bf16[136,1024]{1,0:T(8,128)(2,1)} %collective-permute-done.6.refs_0_, bf16[136,1024]{1,0:T(8,128)(2,1)S(1)} %collective-permute-done.5.refs_1_, f32[8,128]{1,0:T(8,128)S(1)} %broadcast_in_dim.2.refs_2_, bf16[1024,1024]{1,0:T(8,128)(2,1)S(1)} %bitcast.6, ...), custom_call_target="tpu_custom_call" | custom-call | flops 131072 | bytes 131072 | tf_op jit(solution)/shard_map/pallas_call | solution.py:96
  37.7 1.5 %collective-permute-start.12 = (bf16[128,1024]{1,0:T(8,128)(2,1)S(1)}, bf16[128,1024]{1,0:T(8,128)(2,1)S(1)}, u32[]{:S(2)}, u32[]{:S(2)}) collective-permute-start(bf16[128,1024]{1,0:T(8,128)(2,1)S(1)} %get-tuple-element.32), channel_id=1, source_target_pairs={{0,2},{2,0},{4,6},{6,4},{8,10},{10,8},{12,14},{14,12},{1,3},{3,1},... | collective-permute-start | bytes 786440 | tf_op jit(solution)/shard_map/ppermute | solution.py:46
  39.2 0.6 collective-permute-start.8
  39.8 1.3 %collective-permute-start.10 = (bf16[136,1024]{1,0:T(8,128)(2,1)S(1)}, bf16[136,1024]{1,0:T(8,128)(2,1)S(1)}, u32[]{:S(2)}, u32[]{:S(2)}) collective-permute-start(bf16[136,1024]{1,0:T(8,128)(2,1)S(1)} %collective-permute-done.refs_1_), channel_id=1, source_target_pairs={{0,4},{2,6},{4,0},{6,2},{8,12},{10,14},{12,8},{14,10},{1,5},{3,7},... | collective-permute-start | bytes 835592 | tf_op jit(solution)/shard_map/ppermute | solution.py:46
  41.1 2.3 %shard_map.58 = (f32[128,1024]{1,0:T(8,128)S(1)}, f32[128,1024]{1,0:T(8,128)S(1)}) custom-call(bf16[136,1024]{1,0:T(8,128)(2,1)S(1)} %collective-permute-done.4.refs_0_, bf16[136,1024]{1,0:T(8,128)(2,1)S(1)} %collective-permute-done.1.refs_1_, f32[8,128]{1,0:T(8,128)S(1)} %broadcast_in_dim.2.refs_2_, bf16[1024,1024]{1,0:T(8,128)(2,1)S(1)} %bitcast.7, ...), custom_call_target="tpu_custom_call" | custom-call | flops 131072 | bytes 131072 | tf_op jit(solution)/shard_map/pallas_call | solution.py:96
  43.4 3.3 %collective-permute-done.12 = bf16[128,1024]{1,0:T(8,128)(2,1)S(1)} collective-permute-done((bf16[128,1024]{1,0:T(8,128)(2,1)S(1)}, bf16[128,1024]{1,0:T(8,128)(2,1)S(1)}, u32[]{:S(2)}, u32[]{:S(2)}) %collective-permute-start.12) | collective-permute-done | bytes 262176 | tf_op jit(solution)/shard_map/ppermute | solution.py:46
  46.7 0.1 add_convert_fusion.3
  46.7 1.7 %collective-permute-start.13 = (bf16[128,1024]{1,0:T(8,128)(2,1)S(1)}, bf16[128,1024]{1,0:T(8,128)(2,1)S(1)}, u32[]{:S(2)}, u32[]{:S(2)}) collective-permute-start(bf16[128,1024]{1,0:T(8,128)(2,1)S(1)} %add_convert_fusion.3), channel_id=1, source_target_pairs={{0,4},{2,6},{4,0},{6,2},{8,12},{10,14},{12,8},{14,10},{1,5},{3,7},... | collective-permute-start | bytes 786440 | tf_op jit(solution)/shard_map/ppermute | solution.py:46
  48.4 0.0 collective-permute-done.10.refs_1_
  48.4 2.3 %shard_map.59 = (f32[128,1024]{1,0:T(8,128)S(1)}, bf16[128,1024]{1,0:T(8,128)(2,1)S(1)}) custom-call(bf16[136,1024]{1,0:T(8,128)(2,1)S(1)} %collective-permute-done.7.refs_0_, bf16[136,1024]{1,0:T(8,128)(2,1)S(1)} %collective-permute-done.10.refs_1_, f32[8,128]{1,0:T(8,128)S(1)} %broadcast_in_dim.2.refs_2_, bf16[1024,1024]{1,0:T(8,128)(2,1)S(1)} %bitcast.8, ...), custom_call_target="tpu_custom_call" | custom-call | flops 131072 | bytes 131072 | tf_op jit(solution)/shard_map/pallas_call | solution.py:96
  50.8 1.0 %collective-permute-start.11 = (bf16[128,1024]{1,0:T(8,128)(2,1)S(1)}, bf16[128,1024]{1,0:T(8,128)(2,1)S(1)}, u32[]{:S(2)}, u32[]{:S(2)}) collective-permute-start(bf16[128,1024]{1,0:T(8,128)(2,1)S(1)} %get-tuple-element.38), channel_id=1, source_target_pairs={{0,2},{2,0},{4,6},{6,4},{8,10},{10,8},{12,14},{14,12},{1,3},{3,1},... | collective-permute-start | bytes 786440 | tf_op jit(solution)/shard_map/ppermute | solution.py:46
  51.7 0.0 collective-permute-done.8
  51.7 1.1 %collective-permute-start.9 = (bf16[128,1024]{1,0:T(8,128)(2,1)S(1)}, bf16[128,1024]{1,0:T(8,128)(2,1)S(1)}, u32[]{:S(2)}, u32[]{:S(2)}) collective-permute-start(bf16[128,1024]{1,0:T(8,128)(2,1)S(1)} %get-tuple-element.30), channel_id=1, source_target_pairs={{0,2},{2,0},{4,6},{6,4},{8,10},{10,8},{12,14},{14,12},{1,3},{3,1},... | collective-permute-start | bytes 786440 | tf_op jit(solution)/shard_map/ppermute | solution.py:46
  52.9 0.3 collective-permute-done.13
  53.2 0.1 add_convert_fusion.2
  53.3 5.0 %collective-permute-start.15 = (bf16[128,1024]{1,0:T(8,128)(2,1)S(1)}, bf16[128,1024]{1,0:T(8,128)(2,1)S(1)}, u32[]{:S(2)}, u32[]{:S(2)}) collective-permute-start(bf16[128,1024]{1,0:T(8,128)(2,1)S(1)} %add_convert_fusion.2), channel_id=1, source_target_pairs={{0,8},{2,10},{4,12},{6,14},{8,0},{10,2},{12,4},{14,6},{1,9},{3,11}... | collective-permute-start | bytes 786440 | tf_op jit(solution)/shard_map/ppermute | solution.py:46
  58.3 0.0 collective-permute-done.11
  58.3 0.1 add_convert_fusion.1
  58.3 2.3 %collective-permute-start.14 = (bf16[128,1024]{1,0:T(8,128)(2,1)S(1)}, bf16[128,1024]{1,0:T(8,128)(2,1)S(1)}, u32[]{:S(2)}, u32[]{:S(2)}) collective-permute-start(bf16[128,1024]{1,0:T(8,128)(2,1)S(1)} %add_convert_fusion.1), channel_id=1, source_target_pairs={{0,4},{2,6},{4,0},{6,2},{8,12},{10,14},{12,8},{14,10},{1,5},{3,7},... | collective-permute-start | bytes 786440 | tf_op jit(solution)/shard_map/ppermute | solution.py:46
  60.6 0.2 collective-permute-done.9
  60.8 4.6 %collective-permute-done.15 = bf16[128,1024]{1,0:T(8,128)(2,1)S(1)} collective-permute-done((bf16[128,1024]{1,0:T(8,128)(2,1)S(1)}, bf16[128,1024]{1,0:T(8,128)(2,1)S(1)}, u32[]{:S(2)}, u32[]{:S(2)}) %collective-permute-start.15) | collective-permute-done | bytes 262176 | tf_op jit(solution)/shard_map/ppermute | solution.py:46
  65.4 1.4 %collective-permute-done.14 = bf16[128,1024]{1,0:T(8,128)(2,1)S(1)} collective-permute-done((bf16[128,1024]{1,0:T(8,128)(2,1)S(1)}, bf16[128,1024]{1,0:T(8,128)(2,1)S(1)}, u32[]{:S(2)}, u32[]{:S(2)}) %collective-permute-start.14) | collective-permute-done | bytes 262176 | tf_op jit(solution)/shard_map/ppermute | solution.py:46
  66.8 0.8 %add_convert_fusion = bf16[128,1024]{1,0:T(8,128)(2,1)} fusion(bf16[128,1024]{1,0:T(8,128)(2,1)S(1)} %collective-permute-done.15, bf16[128,1024]{1,0:T(8,128)(2,1)S(1)} %collective-permute-done.14, f32[128,1024]{1,0:T(8,128)S(1)} %get-tuple-element.24, bf16[128,1024]{1,0:T(8,128)(2,1)S(1)} %collective-permute-done.9), kind=kLoop, calls=%fused_computation | loop fusion | flops 917504 | bytes 1572864 | tf_op jit(solution)/shard_map/convert_element_type | solution.py:138
  (1 shorter events, 0.0 us)
Async XLA Ops:
  0.0 21.6 %collective-permute-start.2 = (bf16[1024,1024]{1,0:T(8,128)(2,1)}, bf16[1024,1024]{1,0:T(8,128)(2,1)S(1)}, u32[]{:S(2)}, u32[]{:S(2)}) collective-permute-start(bf16[1024,1024]{1,0:T(8,128)(2,1)} %bitcast.4), channel_id=1, source_target_pairs={{0,1},{1,0},{2,3},{3,2},{4,5},{5,4},{6,7},{7,6},{8,9},{9,8},{10,11... | collective-permute-start | bytes 6291464 | tf_op jit(solution)/shard_map/ppermute | solution.py:50
  0.5 22.4 %collective-permute-start.3 = (bf16[1024,1024]{1,0:T(8,128)(2,1)}, bf16[1024,1024]{1,0:T(8,128)(2,1)}, u32[]{:S(2)}, u32[]{:S(2)}) collective-permute-start(bf16[1024,1024]{1,0:T(8,128)(2,1)} %bitcast.9), channel_id=1, source_target_pairs={{0,1},{1,0},{2,3},{3,2},{4,5},{5,4},{6,7},{7,6},{8,9},{9,8},{10,11... | collective-permute-start | bytes 6291464 | tf_op jit(solution)/shard_map/ppermute | solution.py:50
  2.2 17.1 %collective-permute-start.1 = (bf16[136,1024]{1,0:T(8,128)(2,1)}, bf16[136,1024]{1,0:T(8,128)(2,1)S(1)}, u32[]{:S(2)}, u32[]{:S(2)}) collective-permute-start(bf16[136,1024]{1,0:T(8,128)(2,1)} %shard_map.55.refs_0_), channel_id=1, source_target_pairs={{0,8},{2,10},{4,12},{6,14},{8,0},{10,2},{12,4},{14,6},{1,9},{3,11}... | collective-permute-start | bytes 835592 | tf_op jit(solution)/shard_map/ppermute | solution.py:46
  6.3 13.9 %collective-permute-start = (bf16[136,1024]{1,0:T(8,128)(2,1)}, bf16[136,1024]{1,0:T(8,128)(2,1)S(1)}, u32[]{:S(2)}, u32[]{:S(2)}) collective-permute-start(bf16[136,1024]{1,0:T(8,128)(2,1)} %shard_map.55.refs_0_), channel_id=1, source_target_pairs={{0,2},{2,0},{4,6},{6,4},{8,10},{10,8},{12,14},{14,12},{1,3},{3,1},... | collective-permute-start | bytes 835592 | tf_op jit(solution)/shard_map/ppermute | solution.py:46
  7.7 23.6 %collective-permute-start.7 = (bf16[136,1024]{1,0:T(8,128)(2,1)}, bf16[136,1024]{1,0:T(8,128)(2,1)S(1)}, u32[]{:S(2)}, u32[]{:S(2)}) collective-permute-start(bf16[136,1024]{1,0:T(8,128)(2,1)} %shard_map.55.refs_0_), channel_id=1, source_target_pairs={{0,4},{2,6},{4,0},{6,2},{8,12},{10,14},{12,8},{14,10},{1,5},{3,7},... | collective-permute-start | bytes 835592 | tf_op jit(solution)/shard_map/ppermute | solution.py:46
  19.4 11.9 %collective-permute-start.4 = (bf16[136,1024]{1,0:T(8,128)(2,1)S(1)}, bf16[136,1024]{1,0:T(8,128)(2,1)S(1)}, u32[]{:S(2)}, u32[]{:S(2)}) collective-permute-start(bf16[136,1024]{1,0:T(8,128)(2,1)S(1)} %collective-permute-done.1.refs_1_), channel_id=1, source_target_pairs={{0,4},{2,6},{4,0},{6,2},{8,12},{10,14},{12,8},{14,10},{1,5},{3,7},... | collective-permute-start | bytes 835592 | tf_op jit(solution)/shard_map/ppermute | solution.py:46
  20.1 14.3 %collective-permute-start.5 = (bf16[136,1024]{1,0:T(8,128)(2,1)S(1)}, bf16[136,1024]{1,0:T(8,128)(2,1)S(1)}, u32[]{:S(2)}, u32[]{:S(2)}) collective-permute-start(bf16[136,1024]{1,0:T(8,128)(2,1)S(1)} %collective-permute-done.1.refs_1_), channel_id=1, source_target_pairs={{0,2},{2,0},{4,6},{6,4},{8,10},{10,8},{12,14},{14,12},{1,3},{3,1},... | collective-permute-start | bytes 835592 | tf_op jit(solution)/shard_map/ppermute | solution.py:46
  21.6 12.8 %collective-permute-start.6 = (bf16[136,1024]{1,0:T(8,128)(2,1)S(1)}, bf16[136,1024]{1,0:T(8,128)(2,1)}, u32[]{:S(2)}, u32[]{:S(2)}) collective-permute-start(bf16[136,1024]{1,0:T(8,128)(2,1)S(1)} %collective-permute-done.1.refs_1_), channel_id=1, source_target_pairs={{0,6},{2,4},{4,2},{6,0},{8,14},{10,12},{12,10},{14,8},{1,7},{3,5},... | collective-permute-start | bytes 835592 | tf_op jit(solution)/shard_map/ppermute | solution.py:46
  22.9 1.6 %copy-start = (bf16[1,1024,1024]{2,1,0:T(8,128)(2,1)S(1)}, bf16[1,1024,1024]{2,1,0:T(8,128)(2,1)}, u32[]{:S(2)}) copy-start(bf16[1,1024,1024]{2,1,0:T(8,128)(2,1)} %param.8) | copy-start | bytes 6291460
  24.5 1.6 %copy-start.2 = (bf16[1,1024,1024]{2,1,0:T(8,128)(2,1)S(1)}, bf16[1,1024,1024]{2,1,0:T(8,128)(2,1)}, u32[]{:S(2)}) copy-start(bf16[1,1024,1024]{2,1,0:T(8,128)(2,1)} %param.9) | copy-start | bytes 6291460
  26.1 1.0 %copy-start.4 = (bf16[136,1024]{1,0:T(8,128)(2,1)S(1)}, bf16[136,1024]{1,0:T(8,128)(2,1)}, u32[]{:S(2)}) copy-start(bf16[136,1024]{1,0:T(8,128)(2,1)} %shard_map.55.refs_0_) | copy-start | bytes 835588
  27.1 7.3 %copy-start.1 = (bf16[1,1024,1024]{2,1,0:T(8,128)(2,1)S(1)}, bf16[1,1024,1024]{2,1,0:T(8,128)(2,1)}, u32[]{:S(2)}) copy-start(bf16[1,1024,1024]{2,1,0:T(8,128)(2,1)} %param.8) | copy-start | bytes 6291460
  27.1 7.3 %copy-start.3 = (bf16[1,1024,1024]{2,1,0:T(8,128)(2,1)S(1)}, bf16[1,1024,1024]{2,1,0:T(8,128)(2,1)}, u32[]{:S(2)}) copy-start(bf16[1,1024,1024]{2,1,0:T(8,128)(2,1)} %param.9) | copy-start | bytes 6291460
  37.7 8.9 %collective-permute-start.12 = (bf16[128,1024]{1,0:T(8,128)(2,1)S(1)}, bf16[128,1024]{1,0:T(8,128)(2,1)S(1)}, u32[]{:S(2)}, u32[]{:S(2)}) collective-permute-start(bf16[128,1024]{1,0:T(8,128)(2,1)S(1)} %get-tuple-element.32), channel_id=1, source_target_pairs={{0,2},{2,0},{4,6},{6,4},{8,10},{10,8},{12,14},{14,12},{1,3},{3,1},... | collective-permute-start | bytes 786440 | tf_op jit(solution)/shard_map/ppermute | solution.py:46
  39.2 12.5 %collective-permute-start.8 = (bf16[128,1024]{1,0:T(8,128)(2,1)S(1)}, bf16[128,1024]{1,0:T(8,128)(2,1)S(1)}, u32[]{:S(2)}, u32[]{:S(2)}) collective-permute-start(bf16[128,1024]{1,0:T(8,128)(2,1)S(1)} %get-tuple-element.29), channel_id=1, source_target_pairs={{0,2},{2,0},{4,6},{6,4},{8,10},{10,8},{12,14},{14,12},{1,3},{3,1},... | collective-permute-start | bytes 786440 | tf_op jit(solution)/shard_map/ppermute | solution.py:46
  39.8 8.6 %collective-permute-start.10 = (bf16[136,1024]{1,0:T(8,128)(2,1)S(1)}, bf16[136,1024]{1,0:T(8,128)(2,1)S(1)}, u32[]{:S(2)}, u32[]{:S(2)}) collective-permute-start(bf16[136,1024]{1,0:T(8,128)(2,1)S(1)} %collective-permute-done.refs_1_), channel_id=1, source_target_pairs={{0,4},{2,6},{4,0},{6,2},{8,12},{10,14},{12,8},{14,10},{1,5},{3,7},... | collective-permute-start | bytes 835592 | tf_op jit(solution)/shard_map/ppermute | solution.py:46
  46.7 6.4 %collective-permute-start.13 = (bf16[128,1024]{1,0:T(8,128)(2,1)S(1)}, bf16[128,1024]{1,0:T(8,128)(2,1)S(1)}, u32[]{:S(2)}, u32[]{:S(2)}) collective-permute-start(bf16[128,1024]{1,0:T(8,128)(2,1)S(1)} %add_convert_fusion.3), channel_id=1, source_target_pairs={{0,4},{2,6},{4,0},{6,2},{8,12},{10,14},{12,8},{14,10},{1,5},{3,7},... | collective-permute-start | bytes 786440 | tf_op jit(solution)/shard_map/ppermute | solution.py:46
  50.8 7.5 %collective-permute-start.11 = (bf16[128,1024]{1,0:T(8,128)(2,1)S(1)}, bf16[128,1024]{1,0:T(8,128)(2,1)S(1)}, u32[]{:S(2)}, u32[]{:S(2)}) collective-permute-start(bf16[128,1024]{1,0:T(8,128)(2,1)S(1)} %get-tuple-element.38), channel_id=1, source_target_pairs={{0,2},{2,0},{4,6},{6,4},{8,10},{10,8},{12,14},{14,12},{1,3},{3,1},... | collective-permute-start | bytes 786440 | tf_op jit(solution)/shard_map/ppermute | solution.py:46
  51.7 9.1 %collective-permute-start.9 = (bf16[128,1024]{1,0:T(8,128)(2,1)S(1)}, bf16[128,1024]{1,0:T(8,128)(2,1)S(1)}, u32[]{:S(2)}, u32[]{:S(2)}) collective-permute-start(bf16[128,1024]{1,0:T(8,128)(2,1)S(1)} %get-tuple-element.30), channel_id=1, source_target_pairs={{0,2},{2,0},{4,6},{6,4},{8,10},{10,8},{12,14},{14,12},{1,3},{3,1},... | collective-permute-start | bytes 786440 | tf_op jit(solution)/shard_map/ppermute | solution.py:46
  53.3 12.1 %collective-permute-start.15 = (bf16[128,1024]{1,0:T(8,128)(2,1)S(1)}, bf16[128,1024]{1,0:T(8,128)(2,1)S(1)}, u32[]{:S(2)}, u32[]{:S(2)}) collective-permute-start(bf16[128,1024]{1,0:T(8,128)(2,1)S(1)} %add_convert_fusion.2), channel_id=1, source_target_pairs={{0,8},{2,10},{4,12},{6,14},{8,0},{10,2},{12,4},{14,6},{1,9},{3,11}... | collective-permute-start | bytes 786440 | tf_op jit(solution)/shard_map/ppermute | solution.py:46
  58.3 8.4 %collective-permute-start.14 = (bf16[128,1024]{1,0:T(8,128)(2,1)S(1)}, bf16[128,1024]{1,0:T(8,128)(2,1)S(1)}, u32[]{:S(2)}, u32[]{:S(2)}) collective-permute-start(bf16[128,1024]{1,0:T(8,128)(2,1)S(1)} %add_convert_fusion.1), channel_id=1, source_target_pairs={{0,4},{2,6},{4,0},{6,2},{8,12},{10,14},{12,8},{14,10},{1,5},{3,7},... | collective-permute-start | bytes 786440 | tf_op jit(solution)/shard_map/ppermute | solution.py:46

commit v6 on v5

--- a/solution.py
+++ b/solution.py
@@ -54,7 +54,7 @@
     return lax.optimization_barrier((value, *others))[0]
 
 
-def pack_kernel(rows, ids, weights, out):
+def pack_kernel(rows, ids, weights, out, strip):
     n, width = rows.shape
     lines = []
     for e in range(out.shape[0] - n):
@@ -63,12 +63,14 @@
     high = table.astype(jnp.bfloat16)
     low = (table - high.astype(jnp.float32)).astype(jnp.bfloat16)
     rest = jnp.zeros((len(lines), width - 2 * n), jnp.bfloat16)
+    strip[...] = jnp.concatenate([high, low], axis=1)
     out[...] = jnp.concatenate([rows[...], jnp.concatenate([high, low, rest], axis=1)], axis=0)
 
 
-def expert_kernel(count, *refs):
+def expert_kernel(count, apart, *refs):
     f32 = jnp.float32
     blocks = [ref[...] for ref in refs[:count]]
+    strips, refs = [ref[...] for ref in refs[count : count + apart]], refs[:count] + refs[count + apart :]
     choice, up_a, down_a, up_b, down_b = refs[count : count + 5]
     outs, kept = refs[count + 5 : 2 * count + 5], refs[2 * count + 5 :]
     n = outs[0].shape[0]
@@ -80,7 +82,7 @@
         out = jnp.dot(hidden, down[...], preferred_element_type=f32)
         total = out if total is None else total + out
     for i, ref in enumerate(outs):
-        pair = blocks[i][n:, : 2 * n].astype(f32)
+        pair = (strips[i] if strips else blocks[i][n:, : 2 * n]).astype(f32)
         weight = jnp.sum((pair[:, :n] + pair[:, n:]) * choice[...], axis=0, keepdims=True)
         column = jnp.broadcast_to(weight, (n, n)).T
         for c in range(0, ref.shape[1], n):
@@ -89,18 +91,18 @@
         ref[...] = down_b[...]
 
 
-def expert(blocks, kinds, choice, weights, n, keep=False):
+def expert(blocks, kinds, choice, weights, n, keep=False, strips=()):
     width = blocks[0].shape[1]
     out = [jax.ShapeDtypeStruct((n, width), kind) for kind in kinds]
     out += [jax.ShapeDtypeStruct(weights[3].shape, jnp.bfloat16)] * keep
     return pl.pallas_call(
-        functools.partial(expert_kernel, len(blocks)),
+        functools.partial(expert_kernel, len(blocks), len(strips)),
         out_shape=out,
-        in_specs=[pl.BlockSpec(memory_space=pltpu.VMEM)] * (len(blocks) + 5),
+        in_specs=[pl.BlockSpec(memory_space=pltpu.VMEM)] * (len(blocks) + len(strips) + 5),
         out_specs=[pl.BlockSpec(memory_space=pltpu.VMEM)] * len(out),
         compiler_params=pltpu.CompilerParams(vmem_limit_bytes=24 << 20),
         cost_estimate=pl.CostEstimate(flops=n * width, bytes_accessed=n * width, transcendentals=0),
-    )(*blocks, choice, *weights)
+    )(*blocks, *strips, choice, *weights)
 
 
 def gather_body(latent_rows, expert_ids, route_weights, up_weight, down_weight):
@@ -109,28 +111,36 @@
     me = lax.axis_index("expert")
     f32 = jnp.float32
     choice = jnp.broadcast_to((jnp.arange(groups) == me).astype(f32)[:, None], (groups, n))
-    whole = pl.pallas_call(
+    whole, strip = pl.pallas_call(
         pack_kernel,
-        out_shape=jax.ShapeDtypeStruct((n + groups, width), jnp.bfloat16),
+        out_shape=[
+            jax.ShapeDtypeStruct((n + groups, width), jnp.bfloat16),
+            jax.ShapeDtypeStruct((groups, 2 * n), jnp.bfloat16),
+        ],
         in_specs=[pl.BlockSpec(memory_space=pltpu.VMEM)] * 3,
-        out_specs=pl.BlockSpec(memory_space=pltpu.VMEM),
+        out_specs=[pl.BlockSpec(memory_space=pltpu.VMEM)] * 2,
     )(latent_rows, expert_ids.T, route_weights.T)
-    near2 = across(whole, 4)
+    near2 = across(latent_rows, 4)
+    strip2 = across(strip, 4)
     far0 = across(whole, 1)
     near1 = across(whole, 2)
     weights = (up_weight[0], down_weight[0], other_core(up_weight[0]), other_core(down_weight[0]))
+    bf16 = jnp.bfloat16
+    own0, kept = expert([whole], [f32], choice, weights, n, keep=True)
+    near2 = after(near2, own0)
     far3 = across(near2, 3)
     near3 = across(near2, 2)
     far2 = across(near2, 1)
+    line = after(strip2, near2)
+    line3far, line3, line2far = [across(line, step) for step in (3, 2, 1)]
+    weights = weights[:3] + (kept,)
     far0 = after(far0, near2)
-    bf16 = jnp.bfloat16
-    own0, away0, kept = expert([whole, far0], [f32, bf16], choice, weights, n, keep=True)
-    weights = weights[:3] + (kept,)
+    (away0,) = expert([far0], [bf16], choice, weights, n)
     far1 = across(after(far0, near2, away0), 2)
     near3, far2, far3 = lax.optimization_barrier((near3, far2, far3, away0, near1))[:3]
-    away3, away2 = expert([far3, far2], [bf16, bf16], choice, weights, n)
+    away3, away2 = expert([far3, far2], [bf16, bf16], choice, weights, n, strips=[line3far, line2far])
     near3 = after(near3, away3)
-    own3, own2 = expert([near3, near2], [f32, f32], choice, weights, n)
+    own3, own2 = expert([near3, near2], [f32, f32], choice, weights, n, strips=[line3, strip2])
     near1 = after(near1, own3)
     own1, away1 = expert([near1, far1], [f32, bf16], choice, weights, n)
 

time: 67.9 us -> 66.6 us (0.981)
    pallas_call x5 -> x6, Pallas kernels: 13.9 us -> 13.4 us  [the longest x5 11.7 us: expert(): pl.pallas_call(functools.partial(expert_kernel, len(blocks), len(strips))...]
    ppermute x14 -> x18, waiting for transfers between devices: 22.9 us -> 22.5 us  [across(): return lax.ppermute(value, 'expert', [(i, i ^ step) for i in range(size)])]
    ppermute x14 -> x18, starting transfers between devices: 24.9 us -> 24.6 us  [across(): return lax.ppermute(value, 'expert', [(i, i ^ step) for i in range(size)])]
  transfers between devices with their start and end apart: 16 -> 20, of which waited for: 7 -> 9; matrix products, arithmetic and copies ran while one was open for 0% -> 0% of each run, Pallas kernels for 16% -> 17%
where the time goes in v6:
time: 66.6 us; the launch traced here: 66.3 us
  starting transfers between devices  25.1 us (38%)
  waiting for transfers between devices  22.5 us (34%)
  Pallas kernels  13.4 us (20%)
  local copies, waits for them, and re-layouts  4.21 us (6%)
  other arithmetic  1.07 us (2%)
    ppermute x18, starting transfers between devices, across(): return lax.ppermute(value, 'expert', [(i, i ^ step) for i in range(size)])  24.6 us
    ppermute x18, waiting for transfers between devices, across(): return lax.ppermute(value, 'expert', [(i, i ^ step) for i in range(size)])  22.5 us
    pallas_call x5, Pallas kernels, expert(): pl.pallas_call(functools.partial(expert_kernel, len(blocks), len(strips))...  11.7 us
    unnamed x10, local copies, waits for them, and re-layouts  4.14 us
    pallas_call x1, Pallas kernels, gather_body(): pl.pallas_call(pack_kernel, out_shape=[jax.ShapeDtypeStruct((n + groups,...  1.72 us
  transfers between devices with their start and end apart: 20, of which 9 were waited for; matrix products, arithmetic and copies ran while one was open for 0% of the time, Pallas kernels for 17%

profile of v6, /device:TPU:0, one launch (start us, length us, event | category | flops | bytes accessed | tf_op | source)
XLA Modules:
  0.0 66.3 jit_solution(11005816327417549297)
XLA Ops:
  0.0 0.5 collective-permute-start
  0.5 0.1 collective-permute-start.1
  0.5 4.0 %collective-permute-start.3 = (bf16[128,1024]{1,0:T(8,128)(2,1)}, bf16[128,1024]{1,0:T(8,128)(2,1)S(1)}, u32[]{:S(2)}, u32[]{:S(2)}) collective-permute-start(bf16[128,1024]{1,0:T(8,128)(2,1)} %rows.1), channel_id=1, source_target_pairs={{0,8},{2,10},{4,12},{6,14},{8,0},{10,2},{12,4},{14,6},{1,9},{3,11}... | collective-permute-start | bytes 786440 | tf_op jit(solution)/shard_map/ppermute | solution.py:46
  4.5 1.7 %shard_map.55 = (bf16[136,1024]{1,0:T(8,128)(2,1)}, bf16[8,256]{1,0:T(8,128)(2,1)}) custom-call(bf16[128,1024]{1,0:T(8,128)(2,1)} %rows.1, s32[4,128]{1,0:T(4,128)} %bitcast.16, f32[4,128]{1,0:T(4,128)} %bitcast.17), custom_call_target="tpu_custom_call" | custom-call | tf_op jit(solution)/shard_map/pallas_call | solution.py:114
  6.3 1.5 %collective-permute-start.2 = (bf16[136,1024]{1,0:T(8,128)(2,1)}, bf16[136,1024]{1,0:T(8,128)(2,1)S(1)}, u32[]{:S(2)}, u32[]{:S(2)}) collective-permute-start(bf16[136,1024]{1,0:T(8,128)(2,1)} %get-tuple-element.26.refs_0_), channel_id=1, source_target_pairs={{0,2},{2,0},{4,6},{6,4},{8,10},{10,8},{12,14},{14,12},{1,3},{3,1},... | collective-permute-start | bytes 835592 | tf_op jit(solution)/shard_map/ppermute | solution.py:46
  7.8 1.6 %collective-permute-start.7 = (bf16[136,1024]{1,0:T(8,128)(2,1)}, bf16[136,1024]{1,0:T(8,128)(2,1)S(1)}, u32[]{:S(2)}, u32[]{:S(2)}) collective-permute-start(bf16[136,1024]{1,0:T(8,128)(2,1)} %get-tuple-element.26.refs_0_), channel_id=1, source_target_pairs={{0,4},{2,6},{4,0},{6,2},{8,12},{10,14},{12,8},{14,10},{1,5},{3,7},... | collective-permute-start | bytes 835592 | tf_op jit(solution)/shard_map/ppermute | solution.py:46
  9.3 0.0 collective-permute-done.refs_4_.refs_7_.refs_5_
  9.3 1.7 %collective-permute-start.8 = (bf16[8,256]{1,0:T(8,128)(2,1)}, bf16[8,256]{1,0:T(8,128)(2,1)S(1)}, u32[]{:S(2)}, u32[]{:S(2)}) collective-permute-start(bf16[8,256]{1,0:T(8,128)(2,1)} %get-tuple-element.33), channel_id=1, source_target_pairs={{0,8},{2,10},{4,12},{6,14},{8,0},{10,2},{12,4},{14,6},{1,9},{3,11}... | collective-permute-start | bytes 12296 | tf_op jit(solution)/shard_map/ppermute | solution.py:46
  11.0 0.0 collective-permute-done.1.refs_5_
  11.0 0.1 broadcast_in_dim.2.refs_1_.refs_4_.refs_2_
  11.1 0.0 copy-start
  11.1 1.6 %copy-done = bf16[1,1024,1024]{2,1,0:T(8,128)(2,1)S(1)} copy-done((bf16[1,1024,1024]{2,1,0:T(8,128)(2,1)S(1)}, bf16[1,1024,1024]{2,1,0:T(8,128)(2,1)}, u32[]{:S(2)}) %copy-start) | copy-done | bytes 2097176
  12.7 0.0 copy-start.2
  12.7 1.6 %copy-done.2 = bf16[1,1024,1024]{2,1,0:T(8,128)(2,1)S(1)} copy-done((bf16[1,1024,1024]{2,1,0:T(8,128)(2,1)S(1)}, bf16[1,1024,1024]{2,1,0:T(8,128)(2,1)}, u32[]{:S(2)}) %copy-start.2) | copy-done | bytes 2097176
  14.3 0.0 copy-start.4
  14.3 1.0 %copy-done.4 = bf16[136,1024]{1,0:T(8,128)(2,1)S(1)} copy-done((bf16[136,1024]{1,0:T(8,128)(2,1)S(1)}, bf16[136,1024]{1,0:T(8,128)(2,1)}, u32[]{:S(2)}) %copy-start.4) | copy-done | bytes 278552
  15.3 0.0 copy-start.1
  15.3 0.0 copy-start.3
  15.3 3.2 %shard_map.56 = (f32[128,1024]{1,0:T(8,128)S(1)}, bf16[1024,1024]{1,0:T(8,128)(2,1)S(1)}) custom-call(bf16[136,1024]{1,0:T(8,128)(2,1)S(1)} %copy-done.4, f32[8,128]{1,0:T(8,128)S(1)} %broadcast_in_dim.2.refs_1_.refs_4_.refs_2_, bf16[1024,1024]{1,0:T(8,128)(2,1)S(1)} %bitcast.5, bf16[1024,1024]{1,0:T(8,128)(2,1)S(1)} %bitcast.11, ...), custom_call_target="tpu_custom_call" | custom-call | flops 131072 | bytes 131072 | tf_op jit(solution)/shard_map/pallas_call | solution.py:98
  18.5 0.0 collective-permute-done.3.refs_1_
  18.5 1.6 %collective-permute-start.4 = (bf16[128,1024]{1,0:T(8,128)(2,1)S(1)}, bf16[128,1024]{1,0:T(8,128)(2,1)S(1)}, u32[]{:S(2)}, u32[]{:S(2)}) collective-permute-start(bf16[128,1024]{1,0:T(8,128)(2,1)S(1)} %collective-permute-done.3.refs_1_), channel_id=1, source_target_pairs={{0,4},{2,6},{4,0},{6,2},{8,12},{10,14},{12,8},{14,10},{1,5},{3,7},... | collective-permute-start | bytes 786440 | tf_op jit(solution)/shard_map/ppermute | solution.py:46
  20.1 1.5 %collective-permute-start.5 = (bf16[128,1024]{1,0:T(8,128)(2,1)S(1)}, bf16[128,1024]{1,0:T(8,128)(2,1)S(1)}, u32[]{:S(2)}, u32[]{:S(2)}) collective-permute-start(bf16[128,1024]{1,0:T(8,128)(2,1)S(1)} %collective-permute-done.3.refs_1_), channel_id=1, source_target_pairs={{0,2},{2,0},{4,6},{6,4},{8,10},{10,8},{12,14},{14,12},{1,3},{3,1},... | collective-permute-start | bytes 786440 | tf_op jit(solution)/shard_map/ppermute | solution.py:46
  21.6 0.0 collective-permute-done.8.refs_3_
  21.6 0.4 collective-permute-start.6
  22.0 0.0 collective-permute-done.2.refs_0_
  22.0 2.5 %collective-permute-start.9 = (bf16[8,256]{1,0:T(8,128)(2,1)S(1)}, bf16[8,256]{1,0:T(8,128)(2,1)S(1)}, u32[]{:S(2)}, u32[]{:S(2)}) collective-permute-start(bf16[8,256]{1,0:T(8,128)(2,1)S(1)} %collective-permute-done.8.refs_3_), channel_id=1, source_target_pairs={{0,6},{2,4},{4,2},{6,0},{8,14},{10,12},{12,10},{14,8},{1,7},{3,5},... | collective-permute-start | bytes 12296 | tf_op jit(solution)/shard_map/ppermute | solution.py:46
  24.6 0.0 collective-permute-done.7.refs_0_
  24.6 0.5 collective-permute-start.10
  25.1 0.0 copy-done.1
  25.1 0.0 copy-done.3
  25.1 1.3 %shard_map.57 = bf16[128,1024]{1,0:T(8,128)(2,1)S(1)} custom-call(bf16[136,1024]{1,0:T(8,128)(2,1)S(1)} %collective-permute-done.2.refs_0_, f32[8,128]{1,0:T(8,128)S(1)} %broadcast_in_dim.2.refs_1_.refs_4_.refs_2_, bf16[1024,1024]{1,0:T(8,128)(2,1)S(1)} %bitcast.6, bf16[1024,1024]{1,0:T(8,128)(2,1)S(1)} %bitcast.12, ...), custom_call_target="tpu_custom_call" | custom-call | flops 131072 | bytes 131072 | tf_op jit(solution)/shard_map/pallas_call | solution.py:98
  26.5 1.3 %collective-permute-done.4.refs_0_ = bf16[128,1024]{1,0:T(8,128)(2,1)S(1)} collective-permute-done((bf16[128,1024]{1,0:T(8,128)(2,1)S(1)}, bf16[128,1024]{1,0:T(8,128)(2,1)S(1)}, u32[]{:S(2)}, u32[]{:S(2)}) %collective-permute-start.4) | collective-permute-done | bytes 262176 | tf_op jit(solution)/shard_map/ppermute | solution.py:46
  27.7 5.9 %collective-permute-done.5.refs_1_ = bf16[128,1024]{1,0:T(8,128)(2,1)S(1)} collective-permute-done((bf16[128,1024]{1,0:T(8,128)(2,1)S(1)}, bf16[128,1024]{1,0:T(8,128)(2,1)S(1)}, u32[]{:S(2)}, u32[]{:S(2)}) %collective-permute-start.5) | collective-permute-done | bytes 262176 | tf_op jit(solution)/shard_map/ppermute | solution.py:46
  33.7 0.0 collective-permute-done.6.refs_0_
  33.7 0.0 collective-permute-done.9.refs_2_
  33.7 0.0 collective-permute-done.10.refs_3_
  33.7 2.4 %shard_map.58 = (bf16[128,1024]{1,0:T(8,128)(2,1)S(1)}, bf16[128,1024]{1,0:T(8,128)(2,1)S(1)}) custom-call(bf16[128,1024]{1,0:T(8,128)(2,1)S(1)} %collective-permute-done.6.refs_0_, bf16[128,1024]{1,0:T(8,128)(2,1)S(1)} %collective-permute-done.5.refs_1_, bf16[8,256]{1,0:T(8,128)(2,1)S(1)} %collective-permute-done.9.refs_2_, ...), custom_call_target="tpu_custom_call" | custom-call | flops 131072 | bytes 131072 | tf_op jit(solution)/shard_map/pallas_call | solution.py:98
  36.1 1.6 %collective-permute-start.16 = (bf16[128,1024]{1,0:T(8,128)(2,1)S(1)}, bf16[128,1024]{1,0:T(8,128)(2,1)S(1)}, u32[]{:S(2)}, u32[]{:S(2)}) collective-permute-start(bf16[128,1024]{1,0:T(8,128)(2,1)S(1)} %get-tuple-element.38), channel_id=1, source_target_pairs={{0,2},{2,0},{4,6},{6,4},{8,10},{10,8},{12,14},{14,12},{1,3},{3,1},... | collective-permute-start | bytes 786440 | tf_op jit(solution)/shard_map/ppermute | solution.py:46
  37.6 0.5 collective-permute-start.13
  38.1 1.6 %collective-permute-start.14 = (bf16[136,1024]{1,0:T(8,128)(2,1)S(1)}, bf16[136,1024]{1,0:T(8,128)(2,1)S(1)}, u32[]{:S(2)}, u32[]{:S(2)}) collective-permute-start(bf16[136,1024]{1,0:T(8,128)(2,1)S(1)} %collective-permute-done.2.refs_0_), channel_id=1, source_target_pairs={{0,4},{2,6},{4,0},{6,2},{8,12},{10,14},{12,8},{14,10},{1,5},{3,7},... | collective-permute-start | bytes 835592 | tf_op jit(solution)/shard_map/ppermute | solution.py:46
  39.7 0.5 collective-permute-start.11
  40.2 1.2 %collective-permute-done.13.refs_2_ = bf16[8,256]{1,0:T(8,128)(2,1)S(1)} collective-permute-done((bf16[8,256]{1,0:T(8,128)(2,1)S(1)}, bf16[8,256]{1,0:T(8,128)(2,1)S(1)}, u32[]{:S(2)}, u32[]{:S(2)}) %collective-permute-start.13) | collective-permute-done | bytes 4128 | tf_op jit(solution)/shard_map/ppermute | solution.py:46
  41.4 2.4 %shard_map.59 = (f32[128,1024]{1,0:T(8,128)S(1)}, f32[128,1024]{1,0:T(8,128)S(1)}) custom-call(bf16[128,1024]{1,0:T(8,128)(2,1)S(1)} %collective-permute-done.4.refs_0_, bf16[128,1024]{1,0:T(8,128)(2,1)S(1)} %collective-permute-done.3.refs_1_, bf16[8,256]{1,0:T(8,128)(2,1)S(1)} %collective-permute-done.13.refs_2_, ...), custom_call_target="tpu_custom_call" | custom-call | flops 131072 | bytes 131072 | tf_op jit(solution)/shard_map/pallas_call | solution.py:98
  43.7 1.7 %collective-permute-done.16 = bf16[128,1024]{1,0:T(8,128)(2,1)S(1)} collective-permute-done((bf16[128,1024]{1,0:T(8,128)(2,1)S(1)}, bf16[128,1024]{1,0:T(8,128)(2,1)S(1)}, u32[]{:S(2)}, u32[]{:S(2)}) %collective-permute-start.16) | collective-permute-done | bytes 262176 | tf_op jit(solution)/shard_map/ppermute | solution.py:46
  45.4 0.1 add_convert_fusion.3
  45.5 1.2 %collective-permute-start.17 = (bf16[128,1024]{1,0:T(8,128)(2,1)S(1)}, bf16[128,1024]{1,0:T(8,128)(2,1)S(1)}, u32[]{:S(2)}, u32[]{:S(2)}) collective-permute-start(bf16[128,1024]{1,0:T(8,128)(2,1)S(1)} %add_convert_fusion.3), channel_id=1, source_target_pairs={{0,4},{2,6},{4,0},{6,2},{8,12},{10,14},{12,8},{14,10},{1,5},{3,7},... | collective-permute-start | bytes 786440 | tf_op jit(solution)/shard_map/ppermute | solution.py:46
  46.6 0.0 collective-permute-done.14.refs_1_
  46.6 2.4 %shard_map.60 = (f32[128,1024]{1,0:T(8,128)S(1)}, bf16[128,1024]{1,0:T(8,128)(2,1)S(1)}) custom-call(bf16[136,1024]{1,0:T(8,128)(2,1)S(1)} %collective-permute-done.7.refs_0_, bf16[136,1024]{1,0:T(8,128)(2,1)S(1)} %collective-permute-done.14.refs_1_, f32[8,128]{1,0:T(8,128)S(1)} %broadcast_in_dim.2.refs_1_.refs_4_.refs_2_, bf16[1024,1024]{1,0:T(8,128)(2,1)S(1)} %bitcast.9, ...), custom_call_target="tpu_custom_call" | custom-call | flops 131072 | bytes 131072 | tf_op jit(solution)/shard_map/pallas_call | solution.py:98
  49.0 2.0 %collective-permute-start.15 = (bf16[128,1024]{1,0:T(8,128)(2,1)S(1)}, bf16[128,1024]{1,0:T(8,128)(2,1)S(1)}, u32[]{:S(2)}, u32[]{:S(2)}) collective-permute-start(bf16[128,1024]{1,0:T(8,128)(2,1)S(1)} %get-tuple-element.44), channel_id=1, source_target_pairs={{0,2},{2,0},{4,6},{6,4},{8,10},{10,8},{12,14},{14,12},{1,3},{3,1},... | collective-permute-start | bytes 786440 | tf_op jit(solution)/shard_map/ppermute | solution.py:46
  51.0 0.0 collective-permute-done.11
  51.0 0.1 collective-permute-start.12
  51.1 1.8 %collective-permute-done.17 = bf16[128,1024]{1,0:T(8,128)(2,1)S(1)} collective-permute-done((bf16[128,1024]{1,0:T(8,128)(2,1)S(1)}, bf16[128,1024]{1,0:T(8,128)(2,1)S(1)}, u32[]{:S(2)}, u32[]{:S(2)}) %collective-permute-start.17) | collective-permute-done | bytes 262176 | tf_op jit(solution)/shard_map/ppermute | solution.py:46
  52.9 0.1 add_convert_fusion.2
  53.0 0.2 collective-permute-start.19
  53.2 3.7 %collective-permute-done.15 = bf16[128,1024]{1,0:T(8,128)(2,1)S(1)} collective-permute-done((bf16[128,1024]{1,0:T(8,128)(2,1)S(1)}, bf16[128,1024]{1,0:T(8,128)(2,1)S(1)}, u32[]{:S(2)}, u32[]{:S(2)}) %collective-permute-start.15) | collective-permute-done | bytes 262176 | tf_op jit(solution)/shard_map/ppermute | solution.py:46
  57.0 0.1 add_convert_fusion.1
  57.1 1.6 %collective-permute-start.18 = (bf16[128,1024]{1,0:T(8,128)(2,1)S(1)}, bf16[128,1024]{1,0:T(8,128)(2,1)S(1)}, u32[]{:S(2)}, u32[]{:S(2)}) collective-permute-start(bf16[128,1024]{1,0:T(8,128)(2,1)S(1)} %add_convert_fusion.1), channel_id=1, source_target_pairs={{0,4},{2,6},{4,0},{6,2},{8,12},{10,14},{12,8},{14,10},{1,5},{3,7},... | collective-permute-start | bytes 786440 | tf_op jit(solution)/shard_map/ppermute | solution.py:46
  58.6 1.2 %collective-permute-done.12 = bf16[128,1024]{1,0:T(8,128)(2,1)S(1)} collective-permute-done((bf16[128,1024]{1,0:T(8,128)(2,1)S(1)}, bf16[128,1024]{1,0:T(8,128)(2,1)S(1)}, u32[]{:S(2)}, u32[]{:S(2)}) %collective-permute-start.12) | collective-permute-done | bytes 262176 | tf_op jit(solution)/shard_map/ppermute | solution.py:46
  59.8 3.5 %collective-permute-done.19 = bf16[128,1024]{1,0:T(8,128)(2,1)S(1)} collective-permute-done((bf16[128,1024]{1,0:T(8,128)(2,1)S(1)}, bf16[128,1024]{1,0:T(8,128)(2,1)S(1)}, u32[]{:S(2)}, u32[]{:S(2)}) %collective-permute-start.19) | collective-permute-done | bytes 262176 | tf_op jit(solution)/shard_map/ppermute | solution.py:46
  63.3 2.2 %collective-permute-done.18 = bf16[128,1024]{1,0:T(8,128)(2,1)S(1)} collective-permute-done((bf16[128,1024]{1,0:T(8,128)(2,1)S(1)}, bf16[128,1024]{1,0:T(8,128)(2,1)S(1)}, u32[]{:S(2)}, u32[]{:S(2)}) %collective-permute-start.18) | collective-permute-done | bytes 262176 | tf_op jit(solution)/shard_map/ppermute | solution.py:46
  65.5 0.9 %add_convert_fusion = bf16[128,1024]{1,0:T(8,128)(2,1)} fusion(bf16[128,1024]{1,0:T(8,128)(2,1)S(1)} %collective-permute-done.19, bf16[128,1024]{1,0:T(8,128)(2,1)S(1)} %collective-permute-done.18, f32[128,1024]{1,0:T(8,128)S(1)} %get-tuple-element.27, bf16[128,1024]{1,0:T(8,128)(2,1)S(1)} %collective-permute-done.12), kind=kLoop, calls=%fused_computation | loop fusion | flops 917504 | bytes 1572864 | tf_op jit(solution)/shard_map/convert_element_type | solution.py:148
  (1 shorter events, 0.0 us)
Async XLA Ops:
  0.0 9.3 %collective-permute-start = (bf16[1024,1024]{1,0:T(8,128)(2,1)}, bf16[1024,1024]{1,0:T(8,128)(2,1)S(1)}, u32[]{:S(2)}, u32[]{:S(2)}) collective-permute-start(bf16[1024,1024]{1,0:T(8,128)(2,1)} %bitcast.4), channel_id=1, source_target_pairs={{0,1},{1,0},{2,3},{3,2},{4,5},{5,4},{6,7},{7,6},{8,9},{9,8},{10,11... | collective-permute-start | bytes 6291464 | tf_op jit(solution)/shard_map/ppermute | solution.py:50
  0.5 10.6 %collective-permute-start.1 = (bf16[1024,1024]{1,0:T(8,128)(2,1)}, bf16[1024,1024]{1,0:T(8,128)(2,1)}, u32[]{:S(2)}, u32[]{:S(2)}) collective-permute-start(bf16[1024,1024]{1,0:T(8,128)(2,1)} %bitcast.10), channel_id=1, source_target_pairs={{0,1},{1,0},{2,3},{3,2},{4,5},{5,4},{6,7},{7,6},{8,9},{9,8},{10,11... | collective-permute-start | bytes 6291464 | tf_op jit(solution)/shard_map/ppermute | solution.py:50
  0.5 18.0 %collective-permute-start.3 = (bf16[128,1024]{1,0:T(8,128)(2,1)}, bf16[128,1024]{1,0:T(8,128)(2,1)S(1)}, u32[]{:S(2)}, u32[]{:S(2)}) collective-permute-start(bf16[128,1024]{1,0:T(8,128)(2,1)} %rows.1), channel_id=1, source_target_pairs={{0,8},{2,10},{4,12},{6,14},{8,0},{10,2},{12,4},{14,6},{1,9},{3,11}... | collective-permute-start | bytes 786440 | tf_op jit(solution)/shard_map/ppermute | solution.py:46
  6.3 15.8 %collective-permute-start.2 = (bf16[136,1024]{1,0:T(8,128)(2,1)}, bf16[136,1024]{1,0:T(8,128)(2,1)S(1)}, u32[]{:S(2)}, u32[]{:S(2)}) collective-permute-start(bf16[136,1024]{1,0:T(8,128)(2,1)} %get-tuple-element.26.refs_0_), channel_id=1, source_target_pairs={{0,2},{2,0},{4,6},{6,4},{8,10},{10,8},{12,14},{14,12},{1,3},{3,1},... | collective-permute-start | bytes 835592 | tf_op jit(solution)/shard_map/ppermute | solution.py:46
  7.8 16.8 %collective-permute-start.7 = (bf16[136,1024]{1,0:T(8,128)(2,1)}, bf16[136,1024]{1,0:T(8,128)(2,1)S(1)}, u32[]{:S(2)}, u32[]{:S(2)}) collective-permute-start(bf16[136,1024]{1,0:T(8,128)(2,1)} %get-tuple-element.26.refs_0_), channel_id=1, source_target_pairs={{0,4},{2,6},{4,0},{6,2},{8,12},{10,14},{12,8},{14,10},{1,5},{3,7},... | collective-permute-start | bytes 835592 | tf_op jit(solution)/shard_map/ppermute | solution.py:46
  9.3 12.3 %collective-permute-start.8 = (bf16[8,256]{1,0:T(8,128)(2,1)}, bf16[8,256]{1,0:T(8,128)(2,1)S(1)}, u32[]{:S(2)}, u32[]{:S(2)}) collective-permute-start(bf16[8,256]{1,0:T(8,128)(2,1)} %get-tuple-element.33), channel_id=1, source_target_pairs={{0,8},{2,10},{4,12},{6,14},{8,0},{10,2},{12,4},{14,6},{1,9},{3,11}... | collective-permute-start | bytes 12296 | tf_op jit(solution)/shard_map/ppermute | solution.py:46
  11.1 1.6 %copy-start = (bf16[1,1024,1024]{2,1,0:T(8,128)(2,1)S(1)}, bf16[1,1024,1024]{2,1,0:T(8,128)(2,1)}, u32[]{:S(2)}) copy-start(bf16[1,1024,1024]{2,1,0:T(8,128)(2,1)} %param.8) | copy-start | bytes 6291460
  12.7 1.6 %copy-start.2 = (bf16[1,1024,1024]{2,1,0:T(8,128)(2,1)S(1)}, bf16[1,1024,1024]{2,1,0:T(8,128)(2,1)}, u32[]{:S(2)}) copy-start(bf16[1,1024,1024]{2,1,0:T(8,128)(2,1)} %param.9) | copy-start | bytes 6291460
  14.3 1.0 %copy-start.4 = (bf16[136,1024]{1,0:T(8,128)(2,1)S(1)}, bf16[136,1024]{1,0:T(8,128)(2,1)}, u32[]{:S(2)}) copy-start(bf16[136,1024]{1,0:T(8,128)(2,1)} %get-tuple-element.26.refs_0_) | copy-start | bytes 835588
  15.3 9.8 %copy-start.1 = (bf16[1,1024,1024]{2,1,0:T(8,128)(2,1)S(1)}, bf16[1,1024,1024]{2,1,0:T(8,128)(2,1)}, u32[]{:S(2)}) copy-start(bf16[1,1024,1024]{2,1,0:T(8,128)(2,1)} %param.8) | copy-start | bytes 6291460
  15.3 9.8 %copy-start.3 = (bf16[1,1024,1024]{2,1,0:T(8,128)(2,1)S(1)}, bf16[1,1024,1024]{2,1,0:T(8,128)(2,1)}, u32[]{:S(2)}) copy-start(bf16[1,1024,1024]{2,1,0:T(8,128)(2,1)} %param.9) | copy-start | bytes 6291460
  18.5 9.3 %collective-permute-start.4 = (bf16[128,1024]{1,0:T(8,128)(2,1)S(1)}, bf16[128,1024]{1,0:T(8,128)(2,1)S(1)}, u32[]{:S(2)}, u32[]{:S(2)}) collective-permute-start(bf16[128,1024]{1,0:T(8,128)(2,1)S(1)} %collective-permute-done.3.refs_1_), channel_id=1, source_target_pairs={{0,4},{2,6},{4,0},{6,2},{8,12},{10,14},{12,8},{14,10},{1,5},{3,7},... | collective-permute-start | bytes 786440 | tf_op jit(solution)/shard_map/ppermute | solution.py:46
  20.1 13.5 %collective-permute-start.5 = (bf16[128,1024]{1,0:T(8,128)(2,1)S(1)}, bf16[128,1024]{1,0:T(8,128)(2,1)S(1)}, u32[]{:S(2)}, u32[]{:S(2)}) collective-permute-start(bf16[128,1024]{1,0:T(8,128)(2,1)S(1)} %collective-permute-done.3.refs_1_), channel_id=1, source_target_pairs={{0,2},{2,0},{4,6},{6,4},{8,10},{10,8},{12,14},{14,12},{1,3},{3,1},... | collective-permute-start | bytes 786440 | tf_op jit(solution)/shard_map/ppermute | solution.py:46
  21.6 12.0 %collective-permute-start.6 = (bf16[128,1024]{1,0:T(8,128)(2,1)S(1)}, bf16[128,1024]{1,0:T(8,128)(2,1)S(1)}, u32[]{:S(2)}, u32[]{:S(2)}) collective-permute-start(bf16[128,1024]{1,0:T(8,128)(2,1)S(1)} %collective-permute-done.3.refs_1_), channel_id=1, source_target_pairs={{0,6},{2,4},{4,2},{6,0},{8,14},{10,12},{12,10},{14,8},{1,7},{3,5},... | collective-permute-start | bytes 786440 | tf_op jit(solution)/shard_map/ppermute | solution.py:46
  22.0 11.6 %collective-permute-start.9 = (bf16[8,256]{1,0:T(8,128)(2,1)S(1)}, bf16[8,256]{1,0:T(8,128)(2,1)S(1)}, u32[]{:S(2)}, u32[]{:S(2)}) collective-permute-start(bf16[8,256]{1,0:T(8,128)(2,1)S(1)} %collective-permute-done.8.refs_3_), channel_id=1, source_target_pairs={{0,6},{2,4},{4,2},{6,0},{8,14},{10,12},{12,10},{14,8},{1,7},{3,5},... | collective-permute-start | bytes 12296 | tf_op jit(solution)/shard_map/ppermute | solution.py:46
  24.6 9.2 %collective-permute-start.10 = (bf16[8,256]{1,0:T(8,128)(2,1)S(1)}, bf16[8,256]{1,0:T(8,128)(2,1)S(1)}, u32[]{:S(2)}, u32[]{:S(2)}) collective-permute-start(bf16[8,256]{1,0:T(8,128)(2,1)S(1)} %collective-permute-done.8.refs_3_), channel_id=1, source_target_pairs={{0,2},{2,0},{4,6},{6,4},{8,10},{10,8},{12,14},{14,12},{1,3},{3,1},... | collective-permute-start | bytes 12296 | tf_op jit(solution)/shard_map/ppermute | solution.py:46
  36.1 9.3 %collective-permute-start.16 = (bf16[128,1024]{1,0:T(8,128)(2,1)S(1)}, bf16[128,1024]{1,0:T(8,128)(2,1)S(1)}, u32[]{:S(2)}, u32[]{:S(2)}) collective-permute-start(bf16[128,1024]{1,0:T(8,128)(2,1)S(1)} %get-tuple-element.38), channel_id=1, source_target_pairs={{0,2},{2,0},{4,6},{6,4},{8,10},{10,8},{12,14},{14,12},{1,3},{3,1},... | collective-permute-start | bytes 786440 | tf_op jit(solution)/shard_map/ppermute | solution.py:46
  37.6 3.7 %collective-permute-start.13 = (bf16[8,256]{1,0:T(8,128)(2,1)S(1)}, bf16[8,256]{1,0:T(8,128)(2,1)S(1)}, u32[]{:S(2)}, u32[]{:S(2)}) collective-permute-start(bf16[8,256]{1,0:T(8,128)(2,1)S(1)} %collective-permute-done.8.refs_3_), channel_id=1, source_target_pairs={{0,4},{2,6},{4,0},{6,2},{8,12},{10,14},{12,8},{14,10},{1,5},{3,7},... | collective-permute-start | bytes 12296 | tf_op jit(solution)/shard_map/ppermute | solution.py:46
  38.1 8.6 %collective-permute-start.14 = (bf16[136,1024]{1,0:T(8,128)(2,1)S(1)}, bf16[136,1024]{1,0:T(8,128)(2,1)S(1)}, u32[]{:S(2)}, u32[]{:S(2)}) collective-permute-start(bf16[136,1024]{1,0:T(8,128)(2,1)S(1)} %collective-permute-done.2.refs_0_), channel_id=1, source_target_pairs={{0,4},{2,6},{4,0},{6,2},{8,12},{10,14},{12,8},{14,10},{1,5},{3,7},... | collective-permute-start | bytes 835592 | tf_op jit(solution)/shard_map/ppermute | solution.py:46
  39.7 11.4 %collective-permute-start.11 = (bf16[128,1024]{1,0:T(8,128)(2,1)S(1)}, bf16[128,1024]{1,0:T(8,128)(2,1)S(1)}, u32[]{:S(2)}, u32[]{:S(2)}) collective-permute-start(bf16[128,1024]{1,0:T(8,128)(2,1)S(1)} %get-tuple-element.35), channel_id=1, source_target_pairs={{0,2},{2,0},{4,6},{6,4},{8,10},{10,8},{12,14},{14,12},{1,3},{3,1},... | collective-permute-start | bytes 786440 | tf_op jit(solution)/shard_map/ppermute | solution.py:46
  45.5 7.5 %collective-permute-start.17 = (bf16[128,1024]{1,0:T(8,128)(2,1)S(1)}, bf16[128,1024]{1,0:T(8,128)(2,1)S(1)}, u32[]{:S(2)}, u32[]{:S(2)}) collective-permute-start(bf16[128,1024]{1,0:T(8,128)(2,1)S(1)} %add_convert_fusion.3), channel_id=1, source_target_pairs={{0,4},{2,6},{4,0},{6,2},{8,12},{10,14},{12,8},{14,10},{1,5},{3,7},... | collective-permute-start | bytes 786440 | tf_op jit(solution)/shard_map/ppermute | solution.py:46
  49.0 8.0 %collective-permute-start.15 = (bf16[128,1024]{1,0:T(8,128)(2,1)S(1)}, bf16[128,1024]{1,0:T(8,128)(2,1)S(1)}, u32[]{:S(2)}, u32[]{:S(2)}) collective-permute-start(bf16[128,1024]{1,0:T(8,128)(2,1)S(1)} %get-tuple-element.44), channel_id=1, source_target_pairs={{0,2},{2,0},{4,6},{6,4},{8,10},{10,8},{12,14},{14,12},{1,3},{3,1},... | collective-permute-start | bytes 786440 | tf_op jit(solution)/shard_map/ppermute | solution.py:46
  51.0 8.8 %collective-permute-start.12 = (bf16[128,1024]{1,0:T(8,128)(2,1)S(1)}, bf16[128,1024]{1,0:T(8,128)(2,1)S(1)}, u32[]{:S(2)}, u32[]{:S(2)}) collective-permute-start(bf16[128,1024]{1,0:T(8,128)(2,1)S(1)} %shard_map.57), channel_id=1, source_target_pairs={{0,2},{2,0},{4,6},{6,4},{8,10},{10,8},{12,14},{14,12},{1,3},{3,1},... | collective-permute-start | bytes 786440 | tf_op jit(solution)/shard_map/ppermute | solution.py:46
  53.0 10.3 %collective-permute-start.19 = (bf16[128,1024]{1,0:T(8,128)(2,1)S(1)}, bf16[128,1024]{1,0:T(8,128)(2,1)S(1)}, u32[]{:S(2)}, u32[]{:S(2)}) collective-permute-start(bf16[128,1024]{1,0:T(8,128)(2,1)S(1)} %add_convert_fusion.2), channel_id=1, source_target_pairs={{0,8},{2,10},{4,12},{6,14},{8,0},{10,2},{12,4},{14,6},{1,9},{3,11}... | collective-permute-start | bytes 786440 | tf_op jit(solution)/shard_map/ppermute | solution.py:46
  57.1 8.4 %collective-permute-start.18 = (bf16[128,1024]{1,0:T(8,128)(2,1)S(1)}, bf16[128,1024]{1,0:T(8,128)(2,1)S(1)}, u32[]{:S(2)}, u32[]{:S(2)}) collective-permute-start(bf16[128,1024]{1,0:T(8,128)(2,1)S(1)} %add_convert_fusion.1), channel_id=1, source_target_pairs={{0,4},{2,6},{4,0},{6,2},{8,12},{10,14},{12,8},{14,10},{1,5},{3,7},... | collective-permute-start | bytes 786440 | tf_op jit(solution)/shard_map/ppermute | solution.py:46

commit v7 on v6

--- a/solution.py
+++ b/solution.py
@@ -138,8 +138,11 @@
     (away0,) = expert([far0], [bf16], choice, weights, n)
     far1 = across(after(far0, near2, away0), 2)
     near3, far2, far3 = lax.optimization_barrier((near3, far2, far3, away0, near1))[:3]
-    away3, away2 = expert([far3, far2], [bf16, bf16], choice, weights, n, strips=[line3far, line2far])
-    near3 = after(near3, away3)
+    far3 = after(far3, line2far)
+    (away3,) = expert([far3], [bf16], choice, weights, n, strips=[line3far])
+    far2 = after(far2, away3)
+    (away2,) = expert([far2], [bf16], choice, weights, n, strips=[line2far])
+    near3 = after(near3, away2)
     own3, own2 = expert([near3, near2], [f32, f32], choice, weights, n, strips=[line3, strip2])
     near1 = after(near1, own3)
     own1, away1 = expert([near1, far1], [f32, bf16], choice, weights, n)

time: 66.6 us -> 65.3 us (0.980)
  waiting for transfers between devices: 22.5 us -> 21 us
    ppermute x18, waiting for transfers between devices: 22.5 us -> 21 us  [across(): return lax.ppermute(value, 'expert', [(i, i ^ step) for i in range(size)])]
    pallas_call x5 -> x6, Pallas kernels: 11.7 us -> 12 us  [expert(): pl.pallas_call(functools.partial(expert_kernel, len(blocks), len(strips))...]
  transfers between devices with their start and end apart: 20 -> 20, of which waited for: 9 -> 8; matrix products, arithmetic and copies ran while one was open for 0% -> 0% of each run, Pallas kernels for 17% -> 19%
where the time goes in v7:
time: 65.3 us; the launch traced here: 65.1 us
  starting transfers between devices  25 us (38%)
  waiting for transfers between devices  21 us (32%)
  Pallas kernels  13.7 us (21%)
  local copies, waits for them, and re-layouts  4.21 us (6%)
  other arithmetic  1.09 us (2%)
    ppermute x18, starting transfers between devices, across(): return lax.ppermute(value, 'expert', [(i, i ^ step) for i in range(size)])  24.5 us
    ppermute x18, waiting for transfers between devices, across(): return lax.ppermute(value, 'expert', [(i, i ^ step) for i in range(size)])  21 us
    pallas_call x6, Pallas kernels, expert(): pl.pallas_call(functools.partial(expert_kernel, len(blocks), len(strips))...  12 us
    unnamed x10, local copies, waits for them, and re-layouts  4.14 us
    pallas_call x1, Pallas kernels, gather_body(): pl.pallas_call(pack_kernel, out_shape=[jax.ShapeDtypeStruct((n + groups,...  1.71 us
  transfers between devices with their start and end apart: 20, of which 8 were waited for; matrix products, arithmetic and copies ran while one was open for 0% of the time, Pallas kernels for 19%

profile of v7, /device:TPU:0, one launch (start us, length us, event | category | flops | bytes accessed | tf_op | source)
XLA Modules:
  0.0 65.1 jit_solution(16179094781284082250)
XLA Ops:
  0.0 0.5 collective-permute-start
  0.5 0.1 collective-permute-start.1
  0.5 4.0 %collective-permute-start.3 = (bf16[128,1024]{1,0:T(8,128)(2,1)}, bf16[128,1024]{1,0:T(8,128)(2,1)S(1)}, u32[]{:S(2)}, u32[]{:S(2)}) collective-permute-start(bf16[128,1024]{1,0:T(8,128)(2,1)} %rows.1), channel_id=1, source_target_pairs={{0,8},{2,10},{4,12},{6,14},{8,0},{10,2},{12,4},{14,6},{1,9},{3,11}... | collective-permute-start | bytes 786440 | tf_op jit(solution)/shard_map/ppermute | solution.py:46
  4.5 1.7 %shard_map.55 = (bf16[136,1024]{1,0:T(8,128)(2,1)}, bf16[8,256]{1,0:T(8,128)(2,1)}) custom-call(bf16[128,1024]{1,0:T(8,128)(2,1)} %rows.1, s32[4,128]{1,0:T(4,128)} %bitcast.18, f32[4,128]{1,0:T(4,128)} %bitcast.19), custom_call_target="tpu_custom_call" | custom-call | tf_op jit(solution)/shard_map/pallas_call | solution.py:114
  6.3 1.5 %collective-permute-start.2 = (bf16[136,1024]{1,0:T(8,128)(2,1)}, bf16[136,1024]{1,0:T(8,128)(2,1)S(1)}, u32[]{:S(2)}, u32[]{:S(2)}) collective-permute-start(bf16[136,1024]{1,0:T(8,128)(2,1)} %get-tuple-element.26.refs_0_), channel_id=1, source_target_pairs={{0,2},{2,0},{4,6},{6,4},{8,10},{10,8},{12,14},{14,12},{1,3},{3,1},... | collective-permute-start | bytes 835592 | tf_op jit(solution)/shard_map/ppermute | solution.py:46
  7.7 1.6 %collective-permute-start.7 = (bf16[136,1024]{1,0:T(8,128)(2,1)}, bf16[136,1024]{1,0:T(8,128)(2,1)S(1)}, u32[]{:S(2)}, u32[]{:S(2)}) collective-permute-start(bf16[136,1024]{1,0:T(8,128)(2,1)} %get-tuple-element.26.refs_0_), channel_id=1, source_target_pairs={{0,4},{2,6},{4,0},{6,2},{8,12},{10,14},{12,8},{14,10},{1,5},{3,7},... | collective-permute-start | bytes 835592 | tf_op jit(solution)/shard_map/ppermute | solution.py:46
  9.3 0.0 collective-permute-done.refs_4_.refs_5_.refs_7_
  9.3 1.7 %collective-permute-start.8 = (bf16[8,256]{1,0:T(8,128)(2,1)}, bf16[8,256]{1,0:T(8,128)(2,1)S(1)}, u32[]{:S(2)}, u32[]{:S(2)}) collective-permute-start(bf16[8,256]{1,0:T(8,128)(2,1)} %get-tuple-element.33), channel_id=1, source_target_pairs={{0,8},{2,10},{4,12},{6,14},{8,0},{10,2},{12,4},{14,6},{1,9},{3,11}... | collective-permute-start | bytes 12296 | tf_op jit(solution)/shard_map/ppermute | solution.py:46
  11.0 0.0 collective-permute-done.1.refs_5_
  11.0 0.1 broadcast_in_dim.2.refs_1_.refs_2_.refs_4_
  11.1 0.0 copy-start
  11.1 1.6 %copy-done = bf16[1,1024,1024]{2,1,0:T(8,128)(2,1)S(1)} copy-done((bf16[1,1024,1024]{2,1,0:T(8,128)(2,1)S(1)}, bf16[1,1024,1024]{2,1,0:T(8,128)(2,1)}, u32[]{:S(2)}) %copy-start) | copy-done | bytes 2097176
  12.7 0.0 copy-start.2
  12.7 1.6 %copy-done.2 = bf16[1,1024,1024]{2,1,0:T(8,128)(2,1)S(1)} copy-done((bf16[1,1024,1024]{2,1,0:T(8,128)(2,1)S(1)}, bf16[1,1024,1024]{2,1,0:T(8,128)(2,1)}, u32[]{:S(2)}) %copy-start.2) | copy-done | bytes 2097176
  14.3 0.0 copy-start.4
  14.3 1.0 %copy-done.4 = bf16[136,1024]{1,0:T(8,128)(2,1)S(1)} copy-done((bf16[136,1024]{1,0:T(8,128)(2,1)S(1)}, bf16[136,1024]{1,0:T(8,128)(2,1)}, u32[]{:S(2)}) %copy-start.4) | copy-done | bytes 278552
  15.3 0.0 copy-start.1
  15.3 0.0 copy-start.3
  15.3 3.2 %shard_map.56 = (f32[128,1024]{1,0:T(8,128)S(1)}, bf16[1024,1024]{1,0:T(8,128)(2,1)S(1)}) custom-call(bf16[136,1024]{1,0:T(8,128)(2,1)S(1)} %copy-done.4, f32[8,128]{1,0:T(8,128)S(1)} %broadcast_in_dim.2.refs_1_.refs_2_.refs_4_, bf16[1024,1024]{1,0:T(8,128)(2,1)S(1)} %bitcast.5, bf16[1024,1024]{1,0:T(8,128)(2,1)S(1)} %bitcast.12, ...), custom_call_target="tpu_custom_call" | custom-call | flops 131072 | bytes 131072 | tf_op jit(solution)/shard_map/pallas_call | solution.py:98
  18.5 0.0 collective-permute-done.3.refs_1_
  18.5 1.6 %collective-permute-start.4 = (bf16[128,1024]{1,0:T(8,128)(2,1)S(1)}, bf16[128,1024]{1,0:T(8,128)(2,1)S(1)}, u32[]{:S(2)}, u32[]{:S(2)}) collective-permute-start(bf16[128,1024]{1,0:T(8,128)(2,1)S(1)} %collective-permute-done.3.refs_1_), channel_id=1, source_target_pairs={{0,4},{2,6},{4,0},{6,2},{8,12},{10,14},{12,8},{14,10},{1,5},{3,7},... | collective-permute-start | bytes 786440 | tf_op jit(solution)/shard_map/ppermute | solution.py:46
  20.1 1.5 %collective-permute-start.5 = (bf16[128,1024]{1,0:T(8,128)(2,1)S(1)}, bf16[128,1024]{1,0:T(8,128)(2,1)S(1)}, u32[]{:S(2)}, u32[]{:S(2)}) collective-permute-start(bf16[128,1024]{1,0:T(8,128)(2,1)S(1)} %collective-permute-done.3.refs_1_), channel_id=1, source_target_pairs={{0,2},{2,0},{4,6},{6,4},{8,10},{10,8},{12,14},{14,12},{1,3},{3,1},... | collective-permute-start | bytes 786440 | tf_op jit(solution)/shard_map/ppermute | solution.py:46
  21.6 0.0 collective-permute-done.8.refs_3_
  21.6 0.4 collective-permute-start.6
  22.0 0.0 collective-permute-done.2.refs_0_
  22.0 1.5 %collective-permute-start.9 = (bf16[8,256]{1,0:T(8,128)(2,1)S(1)}, bf16[8,256]{1,0:T(8,128)(2,1)S(1)}, u32[]{:S(2)}, u32[]{:S(2)}) collective-permute-start(bf16[8,256]{1,0:T(8,128)(2,1)S(1)} %collective-permute-done.8.refs_3_), channel_id=1, source_target_pairs={{0,2},{2,0},{4,6},{6,4},{8,10},{10,8},{12,14},{14,12},{1,3},{3,1},... | collective-permute-start | bytes 12296 | tf_op jit(solution)/shard_map/ppermute | solution.py:46
  23.5 0.0 collective-permute-done.7.refs_0_
  23.5 1.6 %collective-permute-start.10 = (bf16[8,256]{1,0:T(8,128)(2,1)S(1)}, bf16[8,256]{1,0:T(8,128)(2,1)S(1)}, u32[]{:S(2)}, u32[]{:S(2)}) collective-permute-start(bf16[8,256]{1,0:T(8,128)(2,1)S(1)} %collective-permute-done.8.refs_3_), channel_id=1, source_target_pairs={{0,6},{2,4},{4,2},{6,0},{8,14},{10,12},{12,10},{14,8},{1,7},{3,5},... | collective-permute-start | bytes 12296 | tf_op jit(solution)/shard_map/ppermute | solution.py:46
  25.1 0.0 copy-done.1
  25.1 0.0 copy-done.3
  25.1 1.3 %shard_map.57 = bf16[128,1024]{1,0:T(8,128)(2,1)S(1)} custom-call(bf16[136,1024]{1,0:T(8,128)(2,1)S(1)} %collective-permute-done.2.refs_0_, f32[8,128]{1,0:T(8,128)S(1)} %broadcast_in_dim.2.refs_1_.refs_2_.refs_4_, bf16[1024,1024]{1,0:T(8,128)(2,1)S(1)} %bitcast.6, bf16[1024,1024]{1,0:T(8,128)(2,1)S(1)} %bitcast.13, ...), custom_call_target="tpu_custom_call" | custom-call | flops 131072 | bytes 131072 | tf_op jit(solution)/shard_map/pallas_call | solution.py:98
  26.5 1.3 %collective-permute-done.4.refs_0_ = bf16[128,1024]{1,0:T(8,128)(2,1)S(1)} collective-permute-done((bf16[128,1024]{1,0:T(8,128)(2,1)S(1)}, bf16[128,1024]{1,0:T(8,128)(2,1)S(1)}, u32[]{:S(2)}, u32[]{:S(2)}) %collective-permute-start.4) | collective-permute-done | bytes 262176 | tf_op jit(solution)/shard_map/ppermute | solution.py:46
  27.7 5.9 %collective-permute-done.5.refs_0_ = bf16[128,1024]{1,0:T(8,128)(2,1)S(1)} collective-permute-done((bf16[128,1024]{1,0:T(8,128)(2,1)S(1)}, bf16[128,1024]{1,0:T(8,128)(2,1)S(1)}, u32[]{:S(2)}, u32[]{:S(2)}) %collective-permute-start.5) | collective-permute-done | bytes 262176 | tf_op jit(solution)/shard_map/ppermute | solution.py:46
  33.7 0.0 collective-permute-done.6.refs_0_
  33.7 0.0 collective-permute-done.9.refs_1_
  33.7 0.0 collective-permute-done.10.refs_1_
  33.7 1.3 %shard_map.58 = bf16[128,1024]{1,0:T(8,128)(2,1)S(1)} custom-call(bf16[128,1024]{1,0:T(8,128)(2,1)S(1)} %collective-permute-done.6.refs_0_, bf16[8,256]{1,0:T(8,128)(2,1)S(1)} %collective-permute-done.10.refs_1_, f32[8,128]{1,0:T(8,128)S(1)} %broadcast_in_dim.2.refs_1_.refs_2_.refs_4_, bf16[1024,1024]{1,0:T(8,128)(2,1)S(1)} %bitcast.7, ...), custom_call_target="tpu_custom_call" | custom-call | flops 131072 | bytes 131072 | tf_op jit(solution)/shard_map/pallas_call | solution.py:98
  35.0 1.6 %collective-permute-start.16 = (bf16[128,1024]{1,0:T(8,128)(2,1)S(1)}, bf16[128,1024]{1,0:T(8,128)(2,1)S(1)}, u32[]{:S(2)}, u32[]{:S(2)}) collective-permute-start(bf16[128,1024]{1,0:T(8,128)(2,1)S(1)} %shard_map.58), channel_id=1, source_target_pairs={{0,2},{2,0},{4,6},{6,4},{8,10},{10,8},{12,14},{14,12},{1,3},{3,1},... | collective-permute-start | bytes 786440 | tf_op jit(solution)/shard_map/ppermute | solution.py:46
  36.6 0.5 collective-permute-start.13
  37.1 1.6 %collective-permute-start.14 = (bf16[136,1024]{1,0:T(8,128)(2,1)S(1)}, bf16[136,1024]{1,0:T(8,128)(2,1)S(1)}, u32[]{:S(2)}, u32[]{:S(2)}) collective-permute-start(bf16[136,1024]{1,0:T(8,128)(2,1)S(1)} %collective-permute-done.2.refs_0_), channel_id=1, source_target_pairs={{0,4},{2,6},{4,0},{6,2},{8,12},{10,14},{12,8},{14,10},{1,5},{3,7},... | collective-permute-start | bytes 835592 | tf_op jit(solution)/shard_map/ppermute | solution.py:46
  38.6 1.3 %shard_map.59 = bf16[128,1024]{1,0:T(8,128)(2,1)S(1)} custom-call(bf16[128,1024]{1,0:T(8,128)(2,1)S(1)} %collective-permute-done.5.refs_0_, bf16[8,256]{1,0:T(8,128)(2,1)S(1)} %collective-permute-done.9.refs_1_, f32[8,128]{1,0:T(8,128)S(1)} %broadcast_in_dim.2.refs_1_.refs_2_.refs_4_, bf16[1024,1024]{1,0:T(8,128)(2,1)S(1)} %bitcast.8, ...), custom_call_target="tpu_custom_call" | custom-call | flops 131072 | bytes 131072 | tf_op jit(solution)/shard_map/pallas_call | solution.py:98
  40.0 0.6 collective-permute-start.11
  40.6 0.0 collective-permute-done.13.refs_2_
  40.6 2.4 %shard_map.60 = (f32[128,1024]{1,0:T(8,128)S(1)}, f32[128,1024]{1,0:T(8,128)S(1)}) custom-call(bf16[128,1024]{1,0:T(8,128)(2,1)S(1)} %collective-permute-done.4.refs_0_, bf16[128,1024]{1,0:T(8,128)(2,1)S(1)} %collective-permute-done.3.refs_1_, bf16[8,256]{1,0:T(8,128)(2,1)S(1)} %collective-permute-done.13.refs_2_, ...), custom_call_target="tpu_custom_call" | custom-call | flops 131072 | bytes 131072 | tf_op jit(solution)/shard_map/pallas_call | solution.py:98
  42.9 1.4 %collective-permute-done.16 = bf16[128,1024]{1,0:T(8,128)(2,1)S(1)} collective-permute-done((bf16[128,1024]{1,0:T(8,128)(2,1)S(1)}, bf16[128,1024]{1,0:T(8,128)(2,1)S(1)}, u32[]{:S(2)}, u32[]{:S(2)}) %collective-permute-start.16) | collective-permute-done | bytes 262176 | tf_op jit(solution)/shard_map/ppermute | solution.py:46
  44.3 0.1 add_convert_fusion.3
  44.4 1.2 %collective-permute-start.17 = (bf16[128,1024]{1,0:T(8,128)(2,1)S(1)}, bf16[128,1024]{1,0:T(8,128)(2,1)S(1)}, u32[]{:S(2)}, u32[]{:S(2)}) collective-permute-start(bf16[128,1024]{1,0:T(8,128)(2,1)S(1)} %add_convert_fusion.3), channel_id=1, source_target_pairs={{0,4},{2,6},{4,0},{6,2},{8,12},{10,14},{12,8},{14,10},{1,5},{3,7},... | collective-permute-start | bytes 786440 | tf_op jit(solution)/shard_map/ppermute | solution.py:46
  45.6 0.0 collective-permute-done.14.refs_1_
  45.6 2.4 %shard_map.61 = (f32[128,1024]{1,0:T(8,128)S(1)}, bf16[128,1024]{1,0:T(8,128)(2,1)S(1)}) custom-call(bf16[136,1024]{1,0:T(8,128)(2,1)S(1)} %collective-permute-done.7.refs_0_, bf16[136,1024]{1,0:T(8,128)(2,1)S(1)} %collective-permute-done.14.refs_1_, f32[8,128]{1,0:T(8,128)S(1)} %broadcast_in_dim.2.refs_1_.refs_2_.refs_4_, bf16[1024,1024]{1,0:T(8,128)(2,1)S(1)} %bitcast.10, ...), custom_call_target="tpu_custom_call" | custom-call | flops 131072 | bytes 131072 | tf_op jit(solution)/shard_map/pallas_call | solution.py:98
  48.0 1.3 %collective-permute-start.15 = (bf16[128,1024]{1,0:T(8,128)(2,1)S(1)}, bf16[128,1024]{1,0:T(8,128)(2,1)S(1)}, u32[]{:S(2)}, u32[]{:S(2)}) collective-permute-start(bf16[128,1024]{1,0:T(8,128)(2,1)S(1)} %get-tuple-element.44), channel_id=1, source_target_pairs={{0,2},{2,0},{4,6},{6,4},{8,10},{10,8},{12,14},{14,12},{1,3},{3,1},... | collective-permute-start | bytes 786440 | tf_op jit(solution)/shard_map/ppermute | solution.py:46
  49.3 0.0 collective-permute-done.11
  49.3 0.8 %collective-permute-start.12 = (bf16[128,1024]{1,0:T(8,128)(2,1)S(1)}, bf16[128,1024]{1,0:T(8,128)(2,1)S(1)}, u32[]{:S(2)}, u32[]{:S(2)}) collective-permute-start(bf16[128,1024]{1,0:T(8,128)(2,1)S(1)} %shard_map.57), channel_id=1, source_target_pairs={{0,2},{2,0},{4,6},{6,4},{8,10},{10,8},{12,14},{14,12},{1,3},{3,1},... | collective-permute-start | bytes 786440 | tf_op jit(solution)/shard_map/ppermute | solution.py:46
  50.1 1.6 %collective-permute-done.17 = bf16[128,1024]{1,0:T(8,128)(2,1)S(1)} collective-permute-done((bf16[128,1024]{1,0:T(8,128)(2,1)S(1)}, bf16[128,1024]{1,0:T(8,128)(2,1)S(1)}, u32[]{:S(2)}, u32[]{:S(2)}) %collective-permute-start.17) | collective-permute-done | bytes 262176 | tf_op jit(solution)/shard_map/ppermute | solution.py:46
  51.7 0.1 add_convert_fusion.2
  51.9 0.1 collective-permute-start.19
  51.9 4.0 %collective-permute-done.15 = bf16[128,1024]{1,0:T(8,128)(2,1)S(1)} collective-permute-done((bf16[128,1024]{1,0:T(8,128)(2,1)S(1)}, bf16[128,1024]{1,0:T(8,128)(2,1)S(1)}, u32[]{:S(2)}, u32[]{:S(2)}) %collective-permute-start.15) | collective-permute-done | bytes 262176 | tf_op jit(solution)/shard_map/ppermute | solution.py:46
  55.9 0.1 add_convert_fusion.1
  56.0 1.6 %collective-permute-start.18 = (bf16[128,1024]{1,0:T(8,128)(2,1)S(1)}, bf16[128,1024]{1,0:T(8,128)(2,1)S(1)}, u32[]{:S(2)}, u32[]{:S(2)}) collective-permute-start(bf16[128,1024]{1,0:T(8,128)(2,1)S(1)} %add_convert_fusion.1), channel_id=1, source_target_pairs={{0,4},{2,6},{4,0},{6,2},{8,12},{10,14},{12,8},{14,10},{1,5},{3,7},... | collective-permute-start | bytes 786440 | tf_op jit(solution)/shard_map/ppermute | solution.py:46
  57.6 1.1 %collective-permute-done.12 = bf16[128,1024]{1,0:T(8,128)(2,1)S(1)} collective-permute-done((bf16[128,1024]{1,0:T(8,128)(2,1)S(1)}, bf16[128,1024]{1,0:T(8,128)(2,1)S(1)}, u32[]{:S(2)}, u32[]{:S(2)}) %collective-permute-start.12) | collective-permute-done | bytes 262176 | tf_op jit(solution)/shard_map/ppermute | solution.py:46
  58.7 3.4 %collective-permute-done.19 = bf16[128,1024]{1,0:T(8,128)(2,1)S(1)} collective-permute-done((bf16[128,1024]{1,0:T(8,128)(2,1)S(1)}, bf16[128,1024]{1,0:T(8,128)(2,1)S(1)}, u32[]{:S(2)}, u32[]{:S(2)}) %collective-permute-start.19) | collective-permute-done | bytes 262176 | tf_op jit(solution)/shard_map/ppermute | solution.py:46
  62.1 2.1 %collective-permute-done.18 = bf16[128,1024]{1,0:T(8,128)(2,1)S(1)} collective-permute-done((bf16[128,1024]{1,0:T(8,128)(2,1)S(1)}, bf16[128,1024]{1,0:T(8,128)(2,1)S(1)}, u32[]{:S(2)}, u32[]{:S(2)}) %collective-permute-start.18) | collective-permute-done | bytes 262176 | tf_op jit(solution)/shard_map/ppermute | solution.py:46
  64.3 0.9 %add_convert_fusion = bf16[128,1024]{1,0:T(8,128)(2,1)} fusion(bf16[128,1024]{1,0:T(8,128)(2,1)S(1)} %collective-permute-done.19, bf16[128,1024]{1,0:T(8,128)(2,1)S(1)} %collective-permute-done.18, f32[128,1024]{1,0:T(8,128)S(1)} %get-tuple-element.27, bf16[128,1024]{1,0:T(8,128)(2,1)S(1)} %collective-permute-done.12), kind=kLoop, calls=%fused_computation | loop fusion | flops 917504 | bytes 1572864 | tf_op jit(solution)/shard_map/convert_element_type | solution.py:151
  (1 shorter events, 0.0 us)
Async XLA Ops:
  0.0 9.3 %collective-permute-start = (bf16[1024,1024]{1,0:T(8,128)(2,1)}, bf16[1024,1024]{1,0:T(8,128)(2,1)S(1)}, u32[]{:S(2)}, u32[]{:S(2)}) collective-permute-start(bf16[1024,1024]{1,0:T(8,128)(2,1)} %bitcast.4), channel_id=1, source_target_pairs={{0,1},{1,0},{2,3},{3,2},{4,5},{5,4},{6,7},{7,6},{8,9},{9,8},{10,11... | collective-permute-start | bytes 6291464 | tf_op jit(solution)/shard_map/ppermute | solution.py:50
  0.5 10.6 %collective-permute-start.1 = (bf16[1024,1024]{1,0:T(8,128)(2,1)}, bf16[1024,1024]{1,0:T(8,128)(2,1)}, u32[]{:S(2)}, u32[]{:S(2)}) collective-permute-start(bf16[1024,1024]{1,0:T(8,128)(2,1)} %bitcast.11), channel_id=1, source_target_pairs={{0,1},{1,0},{2,3},{3,2},{4,5},{5,4},{6,7},{7,6},{8,9},{9,8},{10,11... | collective-permute-start | bytes 6291464 | tf_op jit(solution)/shard_map/ppermute | solution.py:50
  0.5 18.0 %collective-permute-start.3 = (bf16[128,1024]{1,0:T(8,128)(2,1)}, bf16[128,1024]{1,0:T(8,128)(2,1)S(1)}, u32[]{:S(2)}, u32[]{:S(2)}) collective-permute-start(bf16[128,1024]{1,0:T(8,128)(2,1)} %rows.1), channel_id=1, source_target_pairs={{0,8},{2,10},{4,12},{6,14},{8,0},{10,2},{12,4},{14,6},{1,9},{3,11}... | collective-permute-start | bytes 786440 | tf_op jit(solution)/shard_map/ppermute | solution.py:46
  6.3 15.8 %collective-permute-start.2 = (bf16[136,1024]{1,0:T(8,128)(2,1)}, bf16[136,1024]{1,0:T(8,128)(2,1)S(1)}, u32[]{:S(2)}, u32[]{:S(2)}) collective-permute-start(bf16[136,1024]{1,0:T(8,128)(2,1)} %get-tuple-element.26.refs_0_), channel_id=1, source_target_pairs={{0,2},{2,0},{4,6},{6,4},{8,10},{10,8},{12,14},{14,12},{1,3},{3,1},... | collective-permute-start | bytes 835592 | tf_op jit(solution)/shard_map/ppermute | solution.py:46
  7.7 15.8 %collective-permute-start.7 = (bf16[136,1024]{1,0:T(8,128)(2,1)}, bf16[136,1024]{1,0:T(8,128)(2,1)S(1)}, u32[]{:S(2)}, u32[]{:S(2)}) collective-permute-start(bf16[136,1024]{1,0:T(8,128)(2,1)} %get-tuple-element.26.refs_0_), channel_id=1, source_target_pairs={{0,4},{2,6},{4,0},{6,2},{8,12},{10,14},{12,8},{14,10},{1,5},{3,7},... | collective-permute-start | bytes 835592 | tf_op jit(solution)/shard_map/ppermute | solution.py:46
  9.3 12.3 %collective-permute-start.8 = (bf16[8,256]{1,0:T(8,128)(2,1)}, bf16[8,256]{1,0:T(8,128)(2,1)S(1)}, u32[]{:S(2)}, u32[]{:S(2)}) collective-permute-start(bf16[8,256]{1,0:T(8,128)(2,1)} %get-tuple-element.33), channel_id=1, source_target_pairs={{0,8},{2,10},{4,12},{6,14},{8,0},{10,2},{12,4},{14,6},{1,9},{3,11}... | collective-permute-start | bytes 12296 | tf_op jit(solution)/shard_map/ppermute | solution.py:46
  11.1 1.6 %copy-start = (bf16[1,1024,1024]{2,1,0:T(8,128)(2,1)S(1)}, bf16[1,1024,1024]{2,1,0:T(8,128)(2,1)}, u32[]{:S(2)}) copy-start(bf16[1,1024,1024]{2,1,0:T(8,128)(2,1)} %param.8) | copy-start | bytes 6291460
  12.7 1.6 %copy-start.2 = (bf16[1,1024,1024]{2,1,0:T(8,128)(2,1)S(1)}, bf16[1,1024,1024]{2,1,0:T(8,128)(2,1)}, u32[]{:S(2)}) copy-start(bf16[1,1024,1024]{2,1,0:T(8,128)(2,1)} %param.9) | copy-start | bytes 6291460
  14.3 1.0 %copy-start.4 = (bf16[136,1024]{1,0:T(8,128)(2,1)S(1)}, bf16[136,1024]{1,0:T(8,128)(2,1)}, u32[]{:S(2)}) copy-start(bf16[136,1024]{1,0:T(8,128)(2,1)} %get-tuple-element.26.refs_0_) | copy-start | bytes 835588
  15.3 9.8 %copy-start.1 = (bf16[1,1024,1024]{2,1,0:T(8,128)(2,1)S(1)}, bf16[1,1024,1024]{2,1,0:T(8,128)(2,1)}, u32[]{:S(2)}) copy-start(bf16[1,1024,1024]{2,1,0:T(8,128)(2,1)} %param.8) | copy-start | bytes 6291460
  15.3 9.8 %copy-start.3 = (bf16[1,1024,1024]{2,1,0:T(8,128)(2,1)S(1)}, bf16[1,1024,1024]{2,1,0:T(8,128)(2,1)}, u32[]{:S(2)}) copy-start(bf16[1,1024,1024]{2,1,0:T(8,128)(2,1)} %param.9) | copy-start | bytes 6291460
  18.5 9.3 %collective-permute-start.4 = (bf16[128,1024]{1,0:T(8,128)(2,1)S(1)}, bf16[128,1024]{1,0:T(8,128)(2,1)S(1)}, u32[]{:S(2)}, u32[]{:S(2)}) collective-permute-start(bf16[128,1024]{1,0:T(8,128)(2,1)S(1)} %collective-permute-done.3.refs_1_), channel_id=1, source_target_pairs={{0,4},{2,6},{4,0},{6,2},{8,12},{10,14},{12,8},{14,10},{1,5},{3,7},... | collective-permute-start | bytes 786440 | tf_op jit(solution)/shard_map/ppermute | solution.py:46
  20.1 13.5 %collective-permute-start.5 = (bf16[128,1024]{1,0:T(8,128)(2,1)S(1)}, bf16[128,1024]{1,0:T(8,128)(2,1)S(1)}, u32[]{:S(2)}, u32[]{:S(2)}) collective-permute-start(bf16[128,1024]{1,0:T(8,128)(2,1)S(1)} %collective-permute-done.3.refs_1_), channel_id=1, source_target_pairs={{0,2},{2,0},{4,6},{6,4},{8,10},{10,8},{12,14},{14,12},{1,3},{3,1},... | collective-permute-start | bytes 786440 | tf_op jit(solution)/shard_map/ppermute | solution.py:46
  21.6 12.0 %collective-permute-start.6 = (bf16[128,1024]{1,0:T(8,128)(2,1)S(1)}, bf16[128,1024]{1,0:T(8,128)(2,1)S(1)}, u32[]{:S(2)}, u32[]{:S(2)}) collective-permute-start(bf16[128,1024]{1,0:T(8,128)(2,1)S(1)} %collective-permute-done.3.refs_1_), channel_id=1, source_target_pairs={{0,6},{2,4},{4,2},{6,0},{8,14},{10,12},{12,10},{14,8},{1,7},{3,5},... | collective-permute-start | bytes 786440 | tf_op jit(solution)/shard_map/ppermute | solution.py:46
  22.0 11.7 %collective-permute-start.9 = (bf16[8,256]{1,0:T(8,128)(2,1)S(1)}, bf16[8,256]{1,0:T(8,128)(2,1)S(1)}, u32[]{:S(2)}, u32[]{:S(2)}) collective-permute-start(bf16[8,256]{1,0:T(8,128)(2,1)S(1)} %collective-permute-done.8.refs_3_), channel_id=1, source_target_pairs={{0,2},{2,0},{4,6},{6,4},{8,10},{10,8},{12,14},{14,12},{1,3},{3,1},... | collective-permute-start | bytes 12296 | tf_op jit(solution)/shard_map/ppermute | solution.py:46
  23.5 10.2 %collective-permute-start.10 = (bf16[8,256]{1,0:T(8,128)(2,1)S(1)}, bf16[8,256]{1,0:T(8,128)(2,1)S(1)}, u32[]{:S(2)}, u32[]{:S(2)}) collective-permute-start(bf16[8,256]{1,0:T(8,128)(2,1)S(1)} %collective-permute-done.8.refs_3_), channel_id=1, source_target_pairs={{0,6},{2,4},{4,2},{6,0},{8,14},{10,12},{12,10},{14,8},{1,7},{3,5},... | collective-permute-start | bytes 12296 | tf_op jit(solution)/shard_map/ppermute | solution.py:46
  35.0 9.3 %collective-permute-start.16 = (bf16[128,1024]{1,0:T(8,128)(2,1)S(1)}, bf16[128,1024]{1,0:T(8,128)(2,1)S(1)}, u32[]{:S(2)}, u32[]{:S(2)}) collective-permute-start(bf16[128,1024]{1,0:T(8,128)(2,1)S(1)} %shard_map.58), channel_id=1, source_target_pairs={{0,2},{2,0},{4,6},{6,4},{8,10},{10,8},{12,14},{14,12},{1,3},{3,1},... | collective-permute-start | bytes 786440 | tf_op jit(solution)/shard_map/ppermute | solution.py:46
  36.6 4.0 %collective-permute-start.13 = (bf16[8,256]{1,0:T(8,128)(2,1)S(1)}, bf16[8,256]{1,0:T(8,128)(2,1)S(1)}, u32[]{:S(2)}, u32[]{:S(2)}) collective-permute-start(bf16[8,256]{1,0:T(8,128)(2,1)S(1)} %collective-permute-done.8.refs_3_), channel_id=1, source_target_pairs={{0,4},{2,6},{4,0},{6,2},{8,12},{10,14},{12,8},{14,10},{1,5},{3,7},... | collective-permute-start | bytes 12296 | tf_op jit(solution)/shard_map/ppermute | solution.py:46
  37.1 8.6 %collective-permute-start.14 = (bf16[136,1024]{1,0:T(8,128)(2,1)S(1)}, bf16[136,1024]{1,0:T(8,128)(2,1)S(1)}, u32[]{:S(2)}, u32[]{:S(2)}) collective-permute-start(bf16[136,1024]{1,0:T(8,128)(2,1)S(1)} %collective-permute-done.2.refs_0_), channel_id=1, source_target_pairs={{0,4},{2,6},{4,0},{6,2},{8,12},{10,14},{12,8},{14,10},{1,5},{3,7},... | collective-permute-start | bytes 835592 | tf_op jit(solution)/shard_map/ppermute | solution.py:46
  40.0 9.3 %collective-permute-start.11 = (bf16[128,1024]{1,0:T(8,128)(2,1)S(1)}, bf16[128,1024]{1,0:T(8,128)(2,1)S(1)}, u32[]{:S(2)}, u32[]{:S(2)}) collective-permute-start(bf16[128,1024]{1,0:T(8,128)(2,1)S(1)} %shard_map.59), channel_id=1, source_target_pairs={{0,2},{2,0},{4,6},{6,4},{8,10},{10,8},{12,14},{14,12},{1,3},{3,1},... | collective-permute-start | bytes 786440 | tf_op jit(solution)/shard_map/ppermute | solution.py:46
  44.4 7.3 %collective-permute-start.17 = (bf16[128,1024]{1,0:T(8,128)(2,1)S(1)}, bf16[128,1024]{1,0:T(8,128)(2,1)S(1)}, u32[]{:S(2)}, u32[]{:S(2)}) collective-permute-start(bf16[128,1024]{1,0:T(8,128)(2,1)S(1)} %add_convert_fusion.3), channel_id=1, source_target_pairs={{0,4},{2,6},{4,0},{6,2},{8,12},{10,14},{12,8},{14,10},{1,5},{3,7},... | collective-permute-start | bytes 786440 | tf_op jit(solution)/shard_map/ppermute | solution.py:46
  48.0 7.9 %collective-permute-start.15 = (bf16[128,1024]{1,0:T(8,128)(2,1)S(1)}, bf16[128,1024]{1,0:T(8,128)(2,1)S(1)}, u32[]{:S(2)}, u32[]{:S(2)}) collective-permute-start(bf16[128,1024]{1,0:T(8,128)(2,1)S(1)} %get-tuple-element.44), channel_id=1, source_target_pairs={{0,2},{2,0},{4,6},{6,4},{8,10},{10,8},{12,14},{14,12},{1,3},{3,1},... | collective-permute-start | bytes 786440 | tf_op jit(solution)/shard_map/ppermute | solution.py:46
  49.3 9.4 %collective-permute-start.12 = (bf16[128,1024]{1,0:T(8,128)(2,1)S(1)}, bf16[128,1024]{1,0:T(8,128)(2,1)S(1)}, u32[]{:S(2)}, u32[]{:S(2)}) collective-permute-start(bf16[128,1024]{1,0:T(8,128)(2,1)S(1)} %shard_map.57), channel_id=1, source_target_pairs={{0,2},{2,0},{4,6},{6,4},{8,10},{10,8},{12,14},{14,12},{1,3},{3,1},... | collective-permute-start | bytes 786440 | tf_op jit(solution)/shard_map/ppermute | solution.py:46
  51.9 10.3 %collective-permute-start.19 = (bf16[128,1024]{1,0:T(8,128)(2,1)S(1)}, bf16[128,1024]{1,0:T(8,128)(2,1)S(1)}, u32[]{:S(2)}, u32[]{:S(2)}) collective-permute-start(bf16[128,1024]{1,0:T(8,128)(2,1)S(1)} %add_convert_fusion.2), channel_id=1, source_target_pairs={{0,8},{2,10},{4,12},{6,14},{8,0},{10,2},{12,4},{14,6},{1,9},{3,11}... | collective-permute-start | bytes 786440 | tf_op jit(solution)/shard_map/ppermute | solution.py:46
  56.0 8.3 %collective-permute-start.18 = (bf16[128,1024]{1,0:T(8,128)(2,1)S(1)}, bf16[128,1024]{1,0:T(8,128)(2,1)S(1)}, u32[]{:S(2)}, u32[]{:S(2)}) collective-permute-start(bf16[128,1024]{1,0:T(8,128)(2,1)S(1)} %add_convert_fusion.1), channel_id=1, source_target_pairs={{0,4},{2,6},{4,0},{6,2},{8,12},{10,14},{12,8},{14,10},{1,5},{3,7},... | collective-permute-start | bytes 786440 | tf_op jit(solution)/shard_map/ppermute | solution.py:46
